TPU v7x, 768 devices: a whole 4x8x12 slice. The times are simulated.
768 devices in a mesh: users: 192 (over z, y, core), items: 4 (over x).
Axes of the slice: x: 4, y: 8, z: 12, core: 2. Of those that a mesh axis runs over, the one named last changes fastest.
Arguments:
- block_ids: int32 [768, 4, 8], P('users', 'items'), may hold values from 0 to 191, all different within a row
- pair_live: int32 [768, 4, 8], P('users', 'items'), may hold values from 1 to 64, 320 in all within a row
- user_rows: int32 [768, 4, 8, 64], P('users', 'items'), may hold values from 0 to 127
- item_rows: int32 [768, 4, 8, 64], P('users', 'items'), may hold values from 0 to 127
- counts: int32 [768, 4, 8, 64], P('users', 'items'), may hold values from 1 to 8
- item_emb: float32 [4, 24576, 128], P('items', 'users'), may hold values from -1 to 1
- user_emb: float32 [98304, 128], P('users'), may hold values from -6 to 6
Outputs:
- new_users: float32 [98304, 128], P('users')
Inputs may be any that keep to these rules, and one draw needn't show every extreme that they name: `block_ids`: the 8 blocks of one user block and item shard are distinct; every block is named somewhere. `pair_live`: for each user block and item shard the counts sum to 320; the largest is 64.
All inputs are finite; a program needn't handle non-finite values.
Results may differ from a plain program's by a relative error of at most 0.0077.
Values may be sent and summed in bfloat16 or wider, within the bound.
No kernel may reach another device: no remote copies, remote signals or barrier semaphores. Data moves between devices by JAX's collectives and lax.ppermute only.
A program may use at most 32 MiB of HBM per device.

v0:
```python
import jax
import jax.numpy as jnp
from jax import lax
from jax.sharding import PartitionSpec as P

ITERS = 3


conf_rate = 0.5
ridge_weight = 0.5


def gram_matrix(matrix):
    return lax.dot_general(
        matrix, matrix, (((0,), (0,)), ((), ())), preferred_element_type=jnp.float32
    )


def local(block_ids, pair_live, user_rows, item_rows, counts, item_emb, user_emb):
    highest = lax.Precision.HIGHEST
    n_users = lax.axis_size("users")
    n_items = lax.axis_size("items")
    own_block = item_emb[0].astype(jnp.bfloat16)
    block_rows = own_block.shape[0]
    width = own_block.shape[1]
    total_items = block_rows * n_users * n_items
    user_blocks = block_ids.shape[0]
    pair_count = block_ids.shape[2]
    slot_count = user_rows.shape[3]
    wanted = block_ids.reshape(user_blocks * pair_count)
    empty_blocks = jnp.zeros((user_blocks * pair_count, block_rows, width), jnp.bfloat16)
    portion = lax.all_gather(own_block, "users", axis=0, tiled=True)
    row_count = portion.shape[0]
    offsets = wanted * block_rows
    inside = (offsets >= 0) & (offsets < row_count)
    places = jnp.clip(offsets, 0, row_count - block_rows)
    sliced = jax.vmap(lambda anchor: lax.dynamic_slice_in_dim(portion, anchor, block_rows, 0))(
        places
    )
    chosen = jnp.where(inside[:, None, None], sliced, empty_blocks)
    gramian = lax.psum(gram_matrix(own_block), ("users", "items"))
    base_matrix = gramian * (width / total_items) + ridge_weight * jnp.eye(width, dtype=jnp.float32)
    item_vecs = chosen.reshape(user_blocks, pair_count, block_rows, width).astype(jnp.float32)
    slot_index = jnp.arange(slot_count, dtype=jnp.int32)
    row_index = jnp.arange(block_rows, dtype=jnp.int32)
    live_mask = (slot_index[None, None, :] < pair_live[:, 0, :, None]).astype(jnp.float32)
    counts_float = counts[:, 0].astype(jnp.float32)
    confidence = conf_rate * counts_float * live_mask
    full_conf = live_mask * (1.0 + conf_rate * counts_float)
    onehot_user = (user_rows[:, 0, :, :, None] == row_index).astype(jnp.float32)
    onehot_item = (item_rows[:, 0, :, :, None] == row_index).astype(jnp.float32)
    weight_map = jnp.einsum(
        "upkb,upki->upbi", onehot_user * confidence[..., None], onehot_item, precision=highest
    )
    weight_full = jnp.einsum(
        "upkb,upki->upbi", onehot_user * full_conf[..., None], onehot_item, precision=highest
    )
    rhs_part = jnp.einsum("upbi,upie->ube", weight_full, item_vecs, precision=highest).reshape(
        user_blocks * block_rows, width
    )

    def local_product(vectors):
        grouped = vectors.reshape(user_blocks, block_rows, width)
        dot_table = jnp.einsum("ube,upie->upbi", grouped, item_vecs, precision=highest)
        summed = jnp.einsum("upbi,upie->ube", weight_map * dot_table, item_vecs, precision=highest)
        return summed.reshape(user_blocks * block_rows, width)

    def operator(vectors, summed):
        return jnp.dot(vectors, base_matrix, precision=highest) + summed

    solution = user_emb
    rhs, start_sum = lax.psum((rhs_part, local_product(solution)), "items")
    remain = rhs - operator(solution, start_sum)
    direction = remain
    norm_now = jnp.sum(remain * remain, axis=1, keepdims=True)
    for turn_index in range(ITERS):
        image = operator(direction, lax.psum(local_product(direction), "items"))
        step_len = norm_now / jnp.sum(direction * image, axis=1, keepdims=True)
        solution = solution + step_len * direction
        remain = remain - step_len * image
        norm_next = jnp.sum(remain * remain, axis=1, keepdims=True)
        direction = remain + norm_next / norm_now * direction
        norm_now = norm_next
    return solution


def solution(mesh):
    return jax.shard_map(
        local,
        mesh=mesh,
        in_specs=(
            P("users", "items", None),
            P("users", "items", None),
            P("users", "items", None, None),
            P("users", "items", None, None),
            P("users", "items", None, None),
            P("items", "users", None),
            P("users", None),
        ),
        out_specs=P("users", None),
        check_vma=False,
    )
```

profile of v0, /device:TPU:8, one launch (start us, length us, event | category | flops | bytes accessed | tf_op | source)
XLA Modules:
  0.0 741.0 jit_solution(5085606685566912620)
XLA Ops:
  7.4 1.5 convert_element_type.25
  8.9 1.6 fusion.28
  12.9 4.1 fusion.8
  17.1 4.1 fusion.10
  21.2 123.5 %all-gather.3.cloned.1.call-done = bf16[1,24576,128]{2,1,0:T(8,128)(2,1)} async-done(((bf16[1,128,128]{2,1,0:T(8,128)(2,1)}), bf16[1,24576,128]{2,1,0:T(8,128)(2,1)}) %all-gather.3.cloned.1.call-update) | async-done | bytes 6291472 | tf_op jit(solution)/shard_map/all_gather | solution.py:32
  144.7 65.2 %while.1 = (s32[]{:T(128)}, bf16[24576,128]{1,0:T(8,128)(2,1)}, s32[32,2]{0,1:T(2,128)S(1)}, bf16[32,128,128]{2,1,0:T(8,128)(2,1)S(1)}, s32[]{:T(128)}) while((s32[]{:T(128)}, bf16[24576,128]{1,0:T(8,128)(2,1)}, s32[32,2]{0,1:T(2,128)S(1)}, bf16[32,128,128]{2,1,0:T(8,128)(2,1)S(1)}, s32[]{:T(128)}) %tuple.37), condition=%wide.while_cond, body=%wide.while_body.sunk | while | flops 2 | bytes 65633 | solution.py:37
  145.3 1.4 bitcast_dynamic-update-slice_fusion.2
  147.3 1.4 bitcast_dynamic-update-slice_fusion.2
  149.4 1.4 bitcast_dynamic-update-slice_fusion.2
  151.4 1.4 bitcast_dynamic-update-slice_fusion.2
  153.4 1.4 bitcast_dynamic-update-slice_fusion.2
  155.5 1.4 bitcast_dynamic-update-slice_fusion.2
  157.5 1.4 bitcast_dynamic-update-slice_fusion.2
  159.6 1.4 bitcast_dynamic-update-slice_fusion.2
  161.6 1.4 bitcast_dynamic-update-slice_fusion.2
  163.6 1.4 bitcast_dynamic-update-slice_fusion.2
  165.7 1.4 bitcast_dynamic-update-slice_fusion.2
  167.7 1.4 bitcast_dynamic-update-slice_fusion.2
  169.7 1.4 bitcast_dynamic-update-slice_fusion.2
  171.8 1.4 bitcast_dynamic-update-slice_fusion.2
  173.8 1.4 bitcast_dynamic-update-slice_fusion.2
  175.9 1.4 bitcast_dynamic-update-slice_fusion.2
  177.9 1.4 bitcast_dynamic-update-slice_fusion.2
  179.9 1.4 bitcast_dynamic-update-slice_fusion.2
  182.0 1.4 bitcast_dynamic-update-slice_fusion.2
  184.0 1.4 bitcast_dynamic-update-slice_fusion.2
  186.1 1.4 bitcast_dynamic-update-slice_fusion.2
  188.1 1.4 bitcast_dynamic-update-slice_fusion.2
  190.1 1.4 bitcast_dynamic-update-slice_fusion.2
  192.2 1.4 bitcast_dynamic-update-slice_fusion.2
  194.2 1.4 bitcast_dynamic-update-slice_fusion.2
  196.2 1.4 bitcast_dynamic-update-slice_fusion.2
  198.3 1.4 bitcast_dynamic-update-slice_fusion.2
  200.3 1.4 bitcast_dynamic-update-slice_fusion.2
  202.4 1.4 bitcast_dynamic-update-slice_fusion.2
  204.4 1.4 bitcast_dynamic-update-slice_fusion.2
  206.4 1.4 bitcast_dynamic-update-slice_fusion.2
  208.5 1.4 bitcast_dynamic-update-slice_fusion.2
  209.9 1.1 fusion.26
  211.0 1.3 fusion.3
  212.6 1.9 fusion.27
  215.4 1.8 copy.8
  217.3 253.2 %all-reduce.8.cloned.1.call-done = f32[128,128]{1,0:T(8,128)} async-done(((f32[128,128]{1,0:T(8,128)}), f32[128,128]{1,0:T(8,128)}) %all-reduce.8.cloned.1.call-update) | async-done | bytes 65552 | tf_op jit(solution)/shard_map/psum | solution.py:41
  470.4 53.8 %all-reduce.16.cloned.1.call-done = (f32[512,128]{0,1:T(8,128)}, f32[512,128]{0,1:T(8,128)}) async-done(((f32[512,128]{0,1:T(8,128)}, f32[512,128]{0,1:T(8,128)}), (f32[512,128]{0,1:T(8,128)}, f32[512,128]{0,1:T(8,128)})) %all-reduce.16.cloned.1.call-update) | async-done | bytes 524304 | tf_op jit(solution)/shard_map/psum | solution.py:72
  524.2 1.6 fusion.6
  526.6 2.0 fusion.24
  528.6 2.0 fusion.2
  530.6 1.8 copy.29
  532.7 58.1 %all-reduce.10.cloned.1.call-done = f32[512,128]{0,1:T(8,128)} async-done(((f32[512,128]{0,1:T(8,128)}), f32[512,128]{0,1:T(8,128)}) %all-reduce.10.cloned.1.call-update) | async-done | bytes 262160 | tf_op jit(solution)/shard_map/psum | solution.py:77
  590.8 1.4 multiply_reduce_fusion.3
  593.7 1.7 reshape.163
  595.4 2.0 fusion.22
  597.5 2.0 fusion.1
  599.5 1.8 copy.30
  601.3 58.3 %all-reduce.12.cloned.1.call-done = f32[512,128]{0,1:T(8,128)} async-done(((f32[512,128]{0,1:T(8,128)}), f32[512,128]{0,1:T(8,128)}) %all-reduce.12.cloned.1.call-update) | async-done | bytes 262160 | tf_op jit(solution)/shard_map/psum | solution.py:77
  659.6 1.5 multiply_reduce_fusion.1
  662.2 1.8 multiply_add_fusion.1
  664.0 1.7 reshape.165
  665.7 2.0 fusion.20
  667.8 2.0 fusion
  669.8 1.8 copy.31
  672.6 57.2 %all-reduce.14.cloned.1.call-done = f32[512,128]{0,1:T(8,128)} async-done(((f32[512,128]{0,1:T(8,128)}), f32[512,128]{0,1:T(8,128)}) %all-reduce.14.cloned.1.call-update) | async-done | bytes 262160 | tf_op jit(solution)/shard_map/psum | solution.py:77
  729.9 1.5 fusion.7
  731.4 1.1 multiply_add_fusion
  (108 shorter events, 28.0 us)
Async XLA Ops:
  7.4 9.7 %copy-start.5 = (s32[4,1,8,64]{3,2,1,0:T(8,128)S(1)}, s32[4,1,8,64]{3,2,1,0:T(8,128)}, u32[]{:S(2)}) copy-start(s32[4,1,8,64]{3,2,1,0:T(8,128)} %param.9) | copy-start | bytes 24580
  7.4 9.7 %copy-start.4 = (s32[4,1,8,64]{3,2,1,0:T(8,128)S(1)}, s32[4,1,8,64]{3,2,1,0:T(8,128)}, u32[]{:S(2)}) copy-start(s32[4,1,8,64]{3,2,1,0:T(8,128)} %param.10) | copy-start | bytes 24580
  7.4 137.3 %all-gather.3.cloned.1.call-start = ((), (), s32[]{:S(2)}) async-start(), calls=%async_computation.4 | async-start | bytes 6324224 | tf_op jit(solution)/shard_map/all_gather | solution.py:32
  8.9 461.6 %all-reduce.8.cloned.1.call-start = ((), (), s32[]{:S(2)}) async-start(), calls=%async_computation | async-start | bytes 131072 | tf_op jit(solution)/shard_map/psum | solution.py:41
  10.6 513.6 %all-reduce.16.cloned.1.call-start = ((), (), s32[]{:S(2)}) async-start(), calls=%async_computation.5 | async-start | bytes 1048576 | tf_op jit(solution)/shard_map/psum | solution.py:72
  12.9 197.0 %copy-start.2 = (f32[512,128]{1,0:T(8,128)S(1)}, f32[512,128]{1,0:T(8,128)}, u32[]{:S(2)}) copy-start(f32[512,128]{1,0:T(8,128)} %param.13) | copy-start | bytes 786436
  211.0 1.6 copy-start
  217.2 373.6 %all-reduce.10.cloned.1.call-start = ((), (), s32[]{:S(2)}) async-start(), calls=%async_computation.1 | async-start | bytes 524288 | tf_op jit(solution)/shard_map/psum | solution.py:77
  528.6 62.2 %copy-start.3 = (f32[128,128]{1,0:T(8,128)S(1)}, f32[128,128]{1,0:T(8,128)}, u32[]{:S(2)}) copy-start(f32[128,128]{1,0:T(8,128)} %all-reduce.8.cloned.1.call-done) | copy-start | bytes 196612
  532.4 127.1 %all-reduce.12.cloned.1.call-start = ((), (), s32[]{:S(2)}) async-start(), calls=%async_computation.2 | async-start | bytes 524288 | tf_op jit(solution)/shard_map/psum | solution.py:77
  592.3 0.7 copy-start.1
  601.3 128.6 %all-reduce.14.cloned.1.call-start = ((), (), s32[]{:S(2)}) async-start(), calls=%async_computation.3 | async-start | bytes 524288 | tf_op jit(solution)/shard_map/psum | solution.py:77
Sparse Core Ops, SparseCore 0:
  12.6 132.0 all-gather.2
Sparse Core Ops, SparseCore 1:
  14.7 455.6 all-reduce.7
  472.9 51.3 all-reduce.15
  532.5 58.2 all-reduce.9
  601.4 58.2 all-reduce.11
  671.6 58.2 all-reduce.13
where the time goes:
time: 744 us; the launch traced here: 741 us
  waiting for transfers between devices  604 us (81%)
  local copies, waits for them, and re-layouts  79.9 us (11%)
  matrix products  32.3 us (4%)
  between operations  15.2 us (2%)
  other arithmetic  8.51 us (1%)
    psum x1, waiting for transfers between devices, local(): gramian = lax.psum(gram_matrix(own_block), ('users', 'items'))  253 us
    psum x3, waiting for transfers between devices, local(): image = operator(direction, lax.psum(local_product(direction), 'items'))  174 us
    all_gather x1, waiting for transfers between devices, local(): portion = lax.all_gather(own_block, 'users', axis=0, tiled=True)  123 us
    gather x96, local copies, waits for them, and re-layouts  64.7 us
    psum x1, waiting for transfers between devices, local(): rhs, start_sum = lax.psum((rhs_part, local_product(solution)), 'items')  53.8 us
  transfers between devices with their start and end apart: 6, of which 6 were waited for; matrix products, arithmetic and copies ran while one was open for 11% of the time, Pallas kernels for 0%

commit v1 on v0

v1 whole, which is shorter than its diff:
```python
import functools

import jax
import jax.numpy as jnp
from jax import lax
from jax.experimental import pallas as pl
from jax.experimental.pallas import tpu as pltpu
from jax.sharding import Mesh, PartitionSpec as P

Z, Y, C, X = 12, 8, 2, 4
E = 128
BLK = 128
PAIRS = 8
NNZ = 64
LIVE = 320
ITERS = 3
GROUPS = 4
GRAM = E // (C * X)

conf_rate = 0.5
ridge_weight = 0.5

bf16 = jnp.bfloat16
f32 = jnp.float32


def dot(a, b):
    return lax.dot_general(a, b, (((1,), (0,)), ((), ())), preferred_element_type=f32)


def split(a):
    hi = a.astype(bf16)
    return hi, (a - hi.astype(f32)).astype(bf16)


def offsets(live_ref, base):
    out = [0]
    for p in range(PAIRS - 1):
        out.append(out[-1] + live_ref[base + p])
    return out


def weight_kernel(live_ref, user_ref, count_ref, out_ref, rows_ref):
    lane = lax.broadcasted_iota(jnp.int32, (NNZ, BLK), 1)
    slot = lax.broadcasted_iota(jnp.int32, (NNZ, BLK), 0)
    for s in range(X):
        offs = offsets(live_ref, s * PAIRS)
        for p in range(PAIRS):
            q = s * PAIRS + p
            hit = (user_ref[:, q : q + 1] == lane) & (slot < live_ref[q])
            rows = jnp.where(hit, count_ref[:, q : q + 1].astype(f32), 0.0)
            rows_ref[s, pl.ds(offs[p], NNZ), :] = rows
        out_ref[s * LIVE : (s + 1) * LIVE, :] = rows_ref[s, :LIVE, :].astype(bf16)


def select_kernel(
    block_ref, seen_ref, live_ref, item_ref, gram_ref, half_ref, out_ref, held, rows_ref, sems
):
    copies = []
    for q in range(C * GROUPS * PAIRS):
        start = pl.multiple_of(block_ref[q] * BLK, BLK)
        copy = pltpu.make_async_copy(half_ref.at[pl.ds(start, BLK), :], held.at[q], sems.at[q])
        copy.start()
        copies.append(copy)
    gram_hi, gram_lo = split(gram_ref[...])
    lane = lax.broadcasted_iota(jnp.int32, (NNZ, BLK), 1)
    slot = lax.broadcasted_iota(jnp.int32, (NNZ, BLK), 0)
    for d in range(C * GROUPS):
        offs = offsets(live_ref, d * PAIRS)
        for p in range(PAIRS):
            q = d * PAIRS + p
            hit = (item_ref[:, q : q + 1] == lane) & (slot < seen_ref[q])
            onehot = jnp.where(hit, 1.0, 0.0).astype(bf16)
            copies[q].wait()
            rows_ref[d, pl.ds(offs[p], NNZ), :] = dot(onehot, held[q])
        out_ref[d, :LIVE, :] = rows_ref[d, :LIVE, :].astype(bf16)
        out_ref[d, LIVE : LIVE + GRAM, :] = gram_hi
        out_ref[d, LIVE + GRAM :, :] = gram_lo


def solve_kernel(recv_ref, weight_ref, start_ref, out_ref):
    items = (recv_ref[:X, :LIVE, :] + recv_ref[X:, :LIVE, :]).reshape(X * LIVE, E)
    items_t = items.T
    weight = weight_ref[...]
    conf = weight.astype(f32) * conf_rate
    full = jnp.where(weight > 0, 1.0 + conf, 0.0).astype(bf16)
    gram = recv_ref[:, LIVE : LIVE + GRAM, :].astype(f32) + recv_ref[:, LIVE + GRAM :, :].astype(f32)
    gram = gram.reshape(E, E)
    eye = lax.broadcasted_iota(jnp.int32, (E, E), 0) == lax.broadcasted_iota(jnp.int32, (E, E), 1)
    base_hi, base_lo = split(
        gram * (E / (X * Z * Y * C * BLK)) + jnp.where(eye, ridge_weight, 0.0)
    )

    def operator(vectors):
        hi, lo = split(vectors)
        both = jnp.concatenate([hi, lo], axis=1)
        table = dot(items, both)
        table = conf * (table[:, :BLK] + table[:, BLK:])
        table_hi, table_lo = split(table)
        summed = dot(items_t, jnp.concatenate([table_hi, table_lo], axis=1))
        dense = dot(base_hi, both)
        return (
            (summed[:, :BLK] + summed[:, BLK:])
            + (dense[:, :BLK] + dense[:, BLK:])
            + dot(base_lo, hi)
        )

    x = start_ref[...].T
    remain = dot(items_t, full) - operator(x)
    direction = remain
    norm_now = jnp.sum(remain * remain, axis=0, keepdims=True)
    for turn in range(ITERS):
        image = operator(direction)
        step = norm_now / jnp.sum(direction * image, axis=0, keepdims=True)
        x = x + step * direction
        if turn < ITERS - 1:
            remain = remain - step * image
            norm_next = jnp.sum(remain * remain, axis=0, keepdims=True)
            direction = remain + norm_next / norm_now * direction
            norm_now = norm_next
    out_ref[...] = x.T


def vmem():
    return pl.BlockSpec(memory_space=pltpu.VMEM)


def smem():
    return pl.BlockSpec(memory_space=pltpu.SMEM)


def params():
    return pltpu.CompilerParams(vmem_limit_bytes=24 * 1024 * 1024)


def local(block_ids, pair_live, user_rows, item_rows, counts, item_emb, user_emb):
    core = lax.axis_index("core")
    part = lax.axis_index("x")
    own_block = item_emb[0].astype(bf16)
    with jax.named_scope("gather_z"):
        column = lax.all_gather(own_block, "z", axis=0, tiled=True)
    with jax.named_scope("gather_y"):
        half = lax.all_gather(column, "y", axis=0, tiled=True)

    with jax.named_scope("gramian"):
        gram = lax.dot_general(
            column, column, (((0,), (0,)), ((), ())), preferred_element_type=f32
        )
        gram = lax.all_to_all(gram.reshape(C * X, GRAM, E), ("core", "x"), 0, 0, tiled=True)
        gram = jnp.broadcast_to(jnp.sum(gram, axis=0)[None], (Y, GRAM, E))
        gram = jnp.sum(lax.all_to_all(gram, "y", 0, 0, tiled=True), axis=0)

    with jax.named_scope("index_exchange"):
        item_pack = jnp.concatenate(
            [
                item_rows.reshape(GROUPS, PAIRS * NNZ),
                jnp.pad(block_ids.reshape(GROUPS, PAIRS), ((0, 0), (0, NNZ - PAIRS))),
                jnp.pad(pair_live.reshape(GROUPS, PAIRS), ((0, 0), (0, NNZ - PAIRS))),
            ],
            axis=1,
        )
        item_pack = lax.all_gather(item_pack, "core", axis=0, tiled=False)
        item_pack = item_pack.reshape(C * GROUPS, (PAIRS + 2) * NNZ)
        user_pack = jnp.concatenate(
            [
                user_rows.reshape(GROUPS, PAIRS * NNZ),
                counts.reshape(GROUPS, PAIRS * NNZ),
                jnp.pad(pair_live.reshape(GROUPS, PAIRS), ((0, 0), (0, BLK - PAIRS))),
            ],
            axis=1,
        )
        user_pack = lax.all_to_all(user_pack, "x", 0, 0, tiled=True)

    span = PAIRS * NNZ
    ids = item_pack[:, span : span + PAIRS].reshape(-1)
    live = item_pack[:, span + NNZ : span + NNZ + PAIRS].reshape(-1)
    z_of, y_of, c_of = ids // (Y * C), ids // C % Y, ids % C
    spots = jnp.clip(y_of * Z + z_of, 0, Z * Y - 1)
    seen = jnp.where(c_of == core, live, 0)
    slots = item_pack[:, :span].reshape(C * GROUPS * PAIRS, NNZ).T

    with jax.named_scope("weights"):
        weight = pl.pallas_call(
            weight_kernel,
            out_shape=jax.ShapeDtypeStruct((X * LIVE, BLK), bf16),
            in_specs=[smem(), vmem(), vmem()],
            out_specs=vmem(),
            scratch_shapes=[pltpu.VMEM((X, LIVE + NNZ, BLK), f32)],
            compiler_params=params(),
            cost_estimate=pl.CostEstimate(flops=2_000_000, bytes_accessed=400_000, transcendentals=0),
        )(
            user_pack[:, 2 * span : 2 * span + PAIRS].reshape(-1),
            user_pack[:, :span].reshape(X * PAIRS, NNZ).T,
            user_pack[:, span : 2 * span].reshape(X * PAIRS, NNZ).T,
        )
    with jax.named_scope("select"):
        chosen = pl.pallas_call(
            select_kernel,
            out_shape=jax.ShapeDtypeStruct((C * GROUPS, LIVE + 2 * GRAM, E), bf16),
            in_specs=[smem()] * 3 + [vmem()] * 2 + [pl.BlockSpec(memory_space=pltpu.HBM)],
            out_specs=vmem(),
            scratch_shapes=[
                pltpu.VMEM((C * GROUPS * PAIRS, BLK, E), bf16),
                pltpu.VMEM((C * GROUPS, LIVE + NNZ, E), f32),
                pltpu.SemaphoreType.DMA((C * GROUPS * PAIRS,)),
            ],
            compiler_params=params(),
            cost_estimate=pl.CostEstimate(
                flops=140_000_000, bytes_accessed=3_000_000, transcendentals=0
            ),
        )(spots, seen, live, slots, gram, half)
    with jax.named_scope("exchange"):
        received = lax.all_to_all(chosen, ("core", "x"), 0, 0, tiled=True)
    with jax.named_scope("solve"):
        start = lax.dynamic_slice_in_dim(user_emb, part * BLK, BLK, 0)
        solved = pl.pallas_call(
            solve_kernel,
            out_shape=jax.ShapeDtypeStruct((BLK, E), f32),
            in_specs=[vmem()] * 3,
            out_specs=vmem(),
            compiler_params=params(),
            cost_estimate=pl.CostEstimate(
                flops=800_000_000, bytes_accessed=1_200_000, transcendentals=0
            ),
        )(received, weight, start)
    with jax.named_scope("gather_x"):
        return lax.all_gather(solved, "x", axis=0, tiled=True)


def solution(mesh):
    grid = Mesh(mesh.devices.reshape(Z, Y, C, X), ("z", "y", "core", "x"))
    users = ("z", "y", "core")
    return jax.shard_map(
        local,
        mesh=grid,
        in_specs=(
            P(users, "x", None),
            P(users, "x", None),
            P(users, "x", None, None),
            P(users, "x", None, None),
            P(users, "x", None, None),
            P("x", users, None),
            P(users, None),
        ),
        out_specs=P(users, None),
        check_vma=False,
    )
```

time: 744 us -> 146 us (0.20)
  waiting for transfers between devices: 604 us -> 30.3 us
  local copies, waits for them, and re-layouts: 79.9 us -> 7.06 us
  blocking collectives: 0 us -> 50.5 us
  matrix products: 32.3 us -> 2.05 us
  starting transfers between devices: 0.4 us -> 20.6 us
  Pallas kernels: 0 us -> 18.4 us
    psum x5 -> x0, waiting for transfers between devices: 481 us -> none  [the longest x1 253 us: local(): gramian = lax.psum(gram_matrix(own_block), ('users', 'items'))]
    all_gather x1, waiting for transfers between devices: 123 us -> 13.8 us  [local(): half = lax.all_gather(column, 'y', axis=0, tiled=True)]
    gather x96 -> x0, local copies, waits for them, and re-layouts: 64.7 us -> none
    all_gather x0 -> x3, blocking collectives: none -> 50.5 us  [the longest x1 36.3 us: local(): column = lax.all_gather(own_block, 'z', axis=0, tiled=True)]
    dot_general x16 -> x1, matrix products: 32.3 us -> 2.05 us  [local(): lax.dot_general(column, column, (((0,), (0,)), ((), ())), preferred_eleme...]
    all_to_all x0 -> x4, starting transfers between devices: none -> 20.6 us  [the longest x1 7.54 us: local(): gram = jnp.sum(lax.all_to_all(gram, 'y', 0, 0, tiled=True), axis=0)]
    pallas_call x0 -> x3, Pallas kernels: none -> 18.4 us  [the longest x1 14 us: local(): pl.pallas_call(select_kernel, out_shape=jax.ShapeDtypeStruct((C * GROUPS,...]
    all_to_all x0 -> x4, waiting for transfers between devices: none -> 16.5 us  [the longest x1 10.1 us: local(): received = lax.all_to_all(chosen, ('core', 'x'), 0, 0, tiled=True)]
  transfers between devices with their start and end apart: 6 -> 5, of which waited for: 6 -> 3; matrix products, arithmetic and copies ran while one was open for 11% -> 5% of each run, Pallas kernels for 0% -> 10%
where the time goes in v1:
time: 146 us; the launch traced here: 145 us
  blocking collectives  50.5 us (35%)
  waiting for transfers between devices  30.3 us (21%)
  starting transfers between devices  20.6 us (14%)
  Pallas kernels  18.4 us (13%)
  between operations  13.5 us (9%)
  local copies, waits for them, and re-layouts  7.06 us (5%)
  other arithmetic  2.39 us (2%)
  matrix products  2.05 us (1%)
    all_gather x1, blocking collectives, local(): column = lax.all_gather(own_block, 'z', axis=0, tiled=True)  36.3 us
    pallas_call x1, Pallas kernels, local(): pl.pallas_call(select_kernel, out_shape=jax.ShapeDtypeStruct((C * GROUPS,...  14 us
    all_gather x1, waiting for transfers between devices, local(): half = lax.all_gather(column, 'y', axis=0, tiled=True)  13.8 us
    all_gather x1, blocking collectives, local(): return lax.all_gather(solved, 'x', axis=0, tiled=True)  12.3 us
    all_to_all x1, waiting for transfers between devices, local(): received = lax.all_to_all(chosen, ('core', 'x'), 0, 0, tiled=True)  10.1 us
    all_to_all x1, starting transfers between devices, local(): gram = jnp.sum(lax.all_to_all(gram, 'y', 0, 0, tiled=True), axis=0)  7.54 us
    all_to_all x1, waiting for transfers between devices, local(): gram = jnp.sum(lax.all_to_all(gram, 'y', 0, 0, tiled=True), axis=0)  6.37 us
    all_to_all x1, starting transfers between devices, local(): user_pack = lax.all_to_all(user_pack, 'x', 0, 0, tiled=True)  4.51 us
  transfers between devices with their start and end apart: 5, of which 3 were waited for; matrix products, arithmetic and copies ran while one was open for 5% of the time, Pallas kernels for 10%

profile of v1, /device:TPU:8, one launch (start us, length us, event | category | flops | bytes accessed | tf_op | source)
XLA Modules:
  0.0 144.9 jit_solution(8040621513857117277)
XLA Ops:
  6.5 0.0 copy-start
  6.5 0.0 all-gather.6.cloned.1.call-start
  6.5 0.9 convert_element_type.6
  7.4 36.3 %all-gather.1 = bf16[1,1536,128]{2,1,0:T(8,128)(2,1)} all-gather(bf16[1,128,128]{2,1,0:T(8,128)(2,1)S(1)} %convert_element_type.6), channel_id=3, replica_groups=mesh['z'=12,'y'=8,'core'=2,'x'=4] {'z'}, dimensions={1}, use_global_device_ids=true | all-gather | bytes 425984 | tf_op jit(solution)/shard_map/gather_z/all_gather | solution.py:141
  43.7 0.0 all-gather.6.cloned.1.call-update
  43.7 2.0 %fusion = f32[128,128]{1,0:T(8,128)} fusion(bf16[1,1536,128]{2,1,0:T(8,128)(2,1)} %all-gather.1), kind=kOutput, calls=%fused_computation | convolution fusion | flops 50331648 | bytes 458752 | tf_op jit(solution)/shard_map/gramian/dot_general | solution.py:146
  45.8 4.3 %all-to-all-start = ((f32[8,16,128]{2,1,0:T(8,128)}), f32[8,16,128]{2,1,0:T(8,128)S(1)}, u32[]{:S(2)}, u32[]{:S(2)}) async-start(f32[8,16,128]{2,1,0:T(8,128)} %bitcast.5), calls=%async_computation | async-start | bytes 131072 | tf_op jit(solution)/shard_map/gramian/all_to_all | solution.py:149
  50.1 0.8 reshape.44
  50.9 0.8 fusion.2
  51.6 2.0 %all-gather.3 = s32[2,4,640]{2,1,0:T(4,128)S(1)} all-gather(s32[1,4,640]{2,1,0:T(4,128)S(1)} %fusion.2), channel_id=2, replica_groups=mesh['z'=12,'y'=8,'core'=2,'x'=4] {'core'}, dimensions={0}, use_global_device_ids=true | all-gather | bytes 30720 | tf_op jit(solution)/shard_map/index_exchange/all_gather | solution.py:162
  53.6 0.1 fusion.7
  53.7 0.1 reshape.49.live_ref
  53.8 0.1 reshape.48
  53.9 0.8 reshape.52
  54.7 0.8 reshape.53
  55.5 0.0 all-to-all-done
  55.5 0.6 broadcast_in_dim.3
  56.1 7.5 %all-to-all-start.1 = ((f32[8,16,128]{2,1,0:T(8,128)}), f32[8,16,128]{2,1,0:T(8,128)S(1)}, u32[]{:S(2)}, u32[]{:S(2)}) async-start(f32[8,16,128]{2,1,0:T(8,128)} %broadcast_in_dim.3), calls=%async_computation.1 | async-start | bytes 131072 | tf_op jit(solution)/shard_map/gramian/all_to_all | solution.py:151
  63.7 0.7 pad_add_fusion
  64.4 0.6 all_to_all.20
  65.0 6.4 %all-to-all-done.1 = f32[8,16,128]{2,1,0:T(8,128)S(1)} async-done(((f32[8,16,128]{2,1,0:T(8,128)}), f32[8,16,128]{2,1,0:T(8,128)S(1)}, u32[]{:S(2)}, u32[]{:S(2)}) %all-to-all-start.1) | async-done | bytes 65568 | tf_op jit(solution)/shard_map/gramian/all_to_all | solution.py:151
  71.3 4.5 %all-to-all-start.3 = ((s32[4,1,1152]{2,1,0:T(1,128)}), s32[4,1,1152]{2,1,0:T(1,128)S(1)}, u32[]{:S(2)}, u32[]{:S(2)}) async-start(s32[4,1,1152]{2,1,0:T(1,128)} %all_to_all.20), calls=%async_computation.3 | async-start | bytes 36864 | tf_op jit(solution)/shard_map/index_exchange/all_to_all | solution.py:172
  75.9 0.1 reshape.50
  76.0 0.1 copy.14
  76.1 13.8 %all-gather.6.cloned.1.call-done = bf16[1,12288,128]{2,1,0:T(8,128)(2,1)} async-done(((bf16[1,1536,128]{2,1,0:T(8,128)(2,1)}), bf16[1,12288,128]{2,1,0:T(8,128)(2,1)}) %all-gather.6.cloned.1.call-update) | async-done | bytes 3145744 | tf_op jit(solution)/shard_map/gather_y/all_gather | solution.py:143
  89.8 0.0 copy-start.1
  89.8 1.9 %copy-done.1 = bf16[1,12288,128]{2,1,0:T(8,128)(2,1)S(1)} copy-done((bf16[1,12288,128]{2,1,0:T(8,128)(2,1)S(1)}, bf16[1,12288,128]{2,1,0:T(8,128)(2,1)}, u32[]{:S(2)}) %copy-start.1) | copy-done | bytes 3145752
  91.7 14.0 %select.16 = bf16[8,352,128]{2,1,0:T(8,128)(2,1)} custom-call(s32[64]{0:T(128)S(1)} %get-tuple-element.10.block_ref, s32[64]{0:T(128)S(1)} %get-tuple-element.9.seen_ref, s32[64]{0:T(128)S(1)} %reshape.49.live_ref, s32[64,64]{1,0:T(8,128)S(1)} %bitcast.22, f32[16,128]{1,0:T(8,128)S(1)} %reduce_sum.19.gram_ref, bf16[12288,128]{1,0:T(8,128)(2,1)S(1)} %bitcast.21), custom_call_target="tpu_custom_call" | custom-call | flops 140000000 | bytes 3000000 | tf_op jit(solution)/shard_map/select/pallas_call | solution.py:197
  105.7 0.0 all-to-all-done.3
  105.7 4.3 %all-to-all-start.2 = ((bf16[8,352,128]{2,1,0:T(8,128)(2,1)}), bf16[8,352,128]{2,1,0:T(8,128)(2,1)S(1)}, u32[]{:S(2)}, u32[]{:S(2)}) async-start(bf16[8,352,128]{2,1,0:T(8,128)(2,1)} %select.16), calls=%async_computation.2 | async-start | bytes 1441792 | tf_op jit(solution)/shard_map/exchange/all_to_all | solution.py:213
  110.0 0.0 copy-done
  110.1 0.1 reshape.55
  110.1 0.1 copy.15
  110.2 0.1 reshape.56
  110.3 0.1 copy.16
  110.4 0.1 reshape.54.live_ref
  110.5 1.2 weights.1.weight_ref
  111.7 10.1 %all-to-all-done.2.recv_ref = bf16[8,352,128]{2,1,0:T(8,128)(2,1)S(1)} async-done(((bf16[8,352,128]{2,1,0:T(8,128)(2,1)}), bf16[8,352,128]{2,1,0:T(8,128)(2,1)S(1)}, u32[]{:S(2)}, u32[]{:S(2)}) %all-to-all-start.2) | async-done | bytes 720928 | tf_op jit(solution)/shard_map/exchange/all_to_all | solution.py:213
  121.8 3.2 %solve.1 = f32[128,128]{1,0:T(8,128)S(1)} custom-call(bf16[8,352,128]{2,1,0:T(8,128)(2,1)S(1)} %all-to-all-done.2.recv_ref, bf16[1280,128]{1,0:T(8,128)(2,1)S(1)} %weights.1.weight_ref, f32[128,128]{1,0:T(8,128)S(1)} %constant_dynamic-slice_fusion.start_ref), custom_call_target="tpu_custom_call" | custom-call | flops 800000000 | bytes 1200000 | tf_op jit(solution)/shard_map/solve/pallas_call | solution.py:216
  125.0 12.3 %all_gather.19 = f32[512,128]{1,0:T(8,128)S(1)} all-gather(f32[128,128]{1,0:T(8,128)S(1)} %solve.1), channel_id=1, replica_groups=mesh['z'=12,'y'=8,'core'=2,'x'=4] {'x'}, dimensions={0}, use_global_device_ids=true | all-gather | bytes 327680 | tf_op jit(solution)/shard_map/gather_x/all_gather | solution.py:227
  137.3 0.7 copy.21
  (9 shorter events, 0.1 us)
Async XLA Ops:
  6.5 103.5 %copy-start = (f32[512,128]{1,0:T(8,128)S(1)}, f32[512,128]{1,0:T(8,128)}, u32[]{:S(2)}) copy-start(f32[512,128]{1,0:T(8,128)} %param.13) | copy-start | bytes 786436
  6.5 83.3 %all-gather.6.cloned.1.call-start = ((), (), s32[]{:S(2)}) async-start(), calls=%async_computation.4 | async-start | bytes 3538944 | tf_op jit(solution)/shard_map/gather_y/all_gather | solution.py:143
  45.8 9.7 %all-to-all-start = ((f32[8,16,128]{2,1,0:T(8,128)}), f32[8,16,128]{2,1,0:T(8,128)S(1)}, u32[]{:S(2)}, u32[]{:S(2)}) async-start(f32[8,16,128]{2,1,0:T(8,128)} %bitcast.5), calls=%async_computation | async-start | bytes 131072 | tf_op jit(solution)/shard_map/gramian/all_to_all | solution.py:149
  56.1 15.2 %all-to-all-start.1 = ((f32[8,16,128]{2,1,0:T(8,128)}), f32[8,16,128]{2,1,0:T(8,128)S(1)}, u32[]{:S(2)}, u32[]{:S(2)}) async-start(f32[8,16,128]{2,1,0:T(8,128)} %broadcast_in_dim.3), calls=%async_computation.1 | async-start | bytes 131072 | tf_op jit(solution)/shard_map/gramian/all_to_all | solution.py:151
  71.3 34.4 %all-to-all-start.3 = ((s32[4,1,1152]{2,1,0:T(1,128)}), s32[4,1,1152]{2,1,0:T(1,128)S(1)}, u32[]{:S(2)}, u32[]{:S(2)}) async-start(s32[4,1,1152]{2,1,0:T(1,128)} %all_to_all.20), calls=%async_computation.3 | async-start | bytes 36864 | tf_op jit(solution)/shard_map/index_exchange/all_to_all | solution.py:172
  89.8 1.9 %copy-start.1 = (bf16[1,12288,128]{2,1,0:T(8,128)(2,1)S(1)}, bf16[1,12288,128]{2,1,0:T(8,128)(2,1)}, u32[]{:S(2)}) copy-start(bf16[1,12288,128]{2,1,0:T(8,128)(2,1)} %all-gather.6.cloned.1.call-done) | copy-start | bytes 9437188
  105.7 16.1 %all-to-all-start.2 = ((bf16[8,352,128]{2,1,0:T(8,128)(2,1)}), bf16[8,352,128]{2,1,0:T(8,128)(2,1)S(1)}, u32[]{:S(2)}, u32[]{:S(2)}) async-start(bf16[8,352,128]{2,1,0:T(8,128)(2,1)} %select.16), calls=%async_computation.2 | async-start | bytes 1441792 | tf_op jit(solution)/shard_map/exchange/all_to_all | solution.py:213
Sparse Core Ops, SparseCore 0:
  43.8 45.9 all-gather.5

commit v2 on v1

--- a/solution.py
+++ b/solution.py
@@ -53,27 +53,31 @@
         out_ref[s * LIVE : (s + 1) * LIVE, :] = rows_ref[s, :LIVE, :].astype(bf16)
 
 
-def select_kernel(
-    block_ref, seen_ref, live_ref, item_ref, gram_ref, half_ref, out_ref, held, rows_ref, sems
-):
-    copies = []
-    for q in range(C * GROUPS * PAIRS):
-        start = pl.multiple_of(block_ref[q] * BLK, BLK)
-        copy = pltpu.make_async_copy(half_ref.at[pl.ds(start, BLK), :], held.at[q], sems.at[q])
-        copy.start()
-        copies.append(copy)
-    gram_hi, gram_lo = split(gram_ref[...])
-    lane = lax.broadcasted_iota(jnp.int32, (NNZ, BLK), 1)
-    slot = lax.broadcasted_iota(jnp.int32, (NNZ, BLK), 0)
+def place_kernel(seen_ref, live_ref, item_ref, out_ref, rows_ref):
+    lane = lax.broadcasted_iota(jnp.int32, (LIVE, BLK), 1)
+    slot = lax.broadcasted_iota(jnp.int32, (NNZ, 1), 0)
+    merged = jnp.full((LIVE, BLK), -1, jnp.int32)
     for d in range(C * GROUPS):
         offs = offsets(live_ref, d * PAIRS)
         for p in range(PAIRS):
             q = d * PAIRS + p
-            hit = (item_ref[:, q : q + 1] == lane) & (slot < seen_ref[q])
-            onehot = jnp.where(hit, 1.0, 0.0).astype(bf16)
-            copies[q].wait()
-            rows_ref[d, pl.ds(offs[p], NNZ), :] = dot(onehot, held[q])
-        out_ref[d, :LIVE, :] = rows_ref[d, :LIVE, :].astype(bf16)
+            spot = jnp.where(slot < seen_ref[q], item_ref[:, q : q + 1] + p * BLK, -1)
+            rows_ref[d, pl.ds(offs[p], NNZ), :] = jnp.broadcast_to(spot, (NNZ, BLK))
+        merged = jnp.where(lane == d, rows_ref[d, :LIVE, :], merged)
+    out_ref[...] = merged
+
+
+def select_kernel(block_ref, place_ref, gram_ref, half_ref, out_ref):
+    gram_hi, gram_lo = split(gram_ref[...])
+    lane = lax.broadcasted_iota(jnp.int32, (LIVE, PAIRS * BLK), 1)
+    for d in range(C * GROUPS):
+        blocks = []
+        for p in range(PAIRS):
+            start = pl.multiple_of(block_ref[d * PAIRS + p] * BLK, BLK)
+            blocks.append(half_ref[pl.ds(start, BLK), :])
+        onehot = jnp.where(place_ref[:, d : d + 1] == lane, 1.0, 0.0).astype(bf16)
+        rows = dot(onehot, jnp.concatenate(blocks, axis=0))
+        out_ref[d, :LIVE, :] = rows.astype(bf16)
         out_ref[d, LIVE : LIVE + GRAM, :] = gram_hi
         out_ref[d, LIVE + GRAM :, :] = gram_lo
 
@@ -193,22 +197,29 @@
             user_pack[:, :span].reshape(X * PAIRS, NNZ).T,
             user_pack[:, span : 2 * span].reshape(X * PAIRS, NNZ).T,
         )
+    with jax.named_scope("place"):
+        place = pl.pallas_call(
+            place_kernel,
+            out_shape=jax.ShapeDtypeStruct((LIVE, BLK), jnp.int32),
+            in_specs=[smem(), smem(), vmem()],
+            out_specs=vmem(),
+            scratch_shapes=[pltpu.VMEM((C * GROUPS, LIVE + NNZ, BLK), jnp.int32)],
+            compiler_params=params(),
+            cost_estimate=pl.CostEstimate(
+                flops=2_000_000, bytes_accessed=300_000, transcendentals=0
+            ),
+        )(seen, live, slots)
     with jax.named_scope("select"):
         chosen = pl.pallas_call(
             select_kernel,
             out_shape=jax.ShapeDtypeStruct((C * GROUPS, LIVE + 2 * GRAM, E), bf16),
-            in_specs=[smem()] * 3 + [vmem()] * 2 + [pl.BlockSpec(memory_space=pltpu.HBM)],
-            out_specs=vmem(),
-            scratch_shapes=[
-                pltpu.VMEM((C * GROUPS * PAIRS, BLK, E), bf16),
-                pltpu.VMEM((C * GROUPS, LIVE + NNZ, E), f32),
-                pltpu.SemaphoreType.DMA((C * GROUPS * PAIRS,)),
-            ],
+            in_specs=[smem()] + [vmem()] * 3,
+            out_specs=vmem(),
             compiler_params=params(),
             cost_estimate=pl.CostEstimate(
-                flops=140_000_000, bytes_accessed=3_000_000, transcendentals=0
+                flops=700_000_000, bytes_accessed=4_000_000, transcendentals=0
             ),
-        )(spots, seen, live, slots, gram, half)
+        )(spots, place, gram, half)
     with jax.named_scope("exchange"):
         received = lax.all_to_all(chosen, ("core", "x"), 0, 0, tiled=True)
     with jax.named_scope("solve"):

time: 146 us -> 135 us (0.925)
  Pallas kernels: 18.4 us -> 8.68 us
    pallas_call x1, Pallas kernels: 14 us -> 3 us  [local(): pl.pallas_call(select_kernel, out_shape=jax.ShapeDtypeStruct((C * GROUPS,...]
  transfers between devices with their start and end apart: 5 -> 5, of which waited for: 3 -> 3; matrix products, arithmetic and copies ran while one was open for 5% -> 6% of each run, Pallas kernels for 10% -> 4%
where the time goes in v2:
time: 135 us; the launch traced here: 134 us
  blocking collectives  50.5 us (37%)
  waiting for transfers between devices  28.9 us (21%)
  starting transfers between devices  20.8 us (15%)
  between operations  13.5 us (10%)
  Pallas kernels  8.68 us (6%)
  local copies, waits for them, and re-layouts  7.07 us (5%)
  other arithmetic  2.39 us (2%)
  matrix products  2.05 us (2%)
    all_gather x1, blocking collectives, local(): column = lax.all_gather(own_block, 'z', axis=0, tiled=True)  36.3 us
    all_gather x1, waiting for transfers between devices, local(): half = lax.all_gather(column, 'y', axis=0, tiled=True)  12.4 us
    all_gather x1, blocking collectives, local(): return lax.all_gather(solved, 'x', axis=0, tiled=True)  12.3 us
    all_to_all x1, waiting for transfers between devices, local(): received = lax.all_to_all(chosen, ('core', 'x'), 0, 0, tiled=True)  10.1 us
    all_to_all x1, starting transfers between devices, local(): gram = jnp.sum(lax.all_to_all(gram, 'y', 0, 0, tiled=True), axis=0)  7.55 us
    all_to_all x1, waiting for transfers between devices, local(): gram = jnp.sum(lax.all_to_all(gram, 'y', 0, 0, tiled=True), axis=0)  6.29 us
    all_to_all x1, starting transfers between devices, local(): user_pack = lax.all_to_all(user_pack, 'x', 0, 0, tiled=True)  4.65 us
    all_to_all x1, starting transfers between devices, local(): lax.all_to_all(gram.reshape(C * X, GRAM, E), ('core', 'x'), 0, 0, tiled=T...  4.3 us
  transfers between devices with their start and end apart: 5, of which 3 were waited for; matrix products, arithmetic and copies ran while one was open for 6% of the time, Pallas kernels for 4%

profile of v2, /device:TPU:8, one launch (start us, length us, event | category | flops | bytes accessed | tf_op | source)
XLA Modules:
  0.0 133.8 jit_solution(11662394349070465734)
XLA Ops:
  6.5 0.0 copy-start
  6.5 0.0 all-gather.6.cloned.1.call-start
  6.5 0.9 convert_element_type.6
  7.4 36.3 %all-gather.1 = bf16[1,1536,128]{2,1,0:T(8,128)(2,1)} all-gather(bf16[1,128,128]{2,1,0:T(8,128)(2,1)S(1)} %convert_element_type.6), channel_id=3, replica_groups=mesh['z'=12,'y'=8,'core'=2,'x'=4] {'z'}, dimensions={1}, use_global_device_ids=true | all-gather | bytes 425984 | tf_op jit(solution)/shard_map/gather_z/all_gather | solution.py:145
  43.7 0.0 all-gather.6.cloned.1.call-update
  43.7 2.0 %fusion = f32[128,128]{1,0:T(8,128)} fusion(bf16[1,1536,128]{2,1,0:T(8,128)(2,1)} %all-gather.1), kind=kOutput, calls=%fused_computation | convolution fusion | flops 50331648 | bytes 458752 | tf_op jit(solution)/shard_map/gramian/dot_general | solution.py:150
  45.8 4.3 %all-to-all-start = ((f32[8,16,128]{2,1,0:T(8,128)}), f32[8,16,128]{2,1,0:T(8,128)S(1)}, u32[]{:S(2)}, u32[]{:S(2)}) async-start(f32[8,16,128]{2,1,0:T(8,128)} %bitcast.5), calls=%async_computation | async-start | bytes 131072 | tf_op jit(solution)/shard_map/gramian/all_to_all | solution.py:153
  50.1 0.8 reshape.44
  50.9 0.8 fusion.2
  51.6 2.0 %all-gather.3 = s32[2,4,640]{2,1,0:T(4,128)S(1)} all-gather(s32[1,4,640]{2,1,0:T(4,128)S(1)} %fusion.2), channel_id=2, replica_groups=mesh['z'=12,'y'=8,'core'=2,'x'=4] {'core'}, dimensions={0}, use_global_device_ids=true | all-gather | bytes 30720 | tf_op jit(solution)/shard_map/index_exchange/all_gather | solution.py:166
  53.6 0.8 reshape.52
  54.4 0.8 reshape.53
  55.2 0.7 pad_add_fusion
  55.9 0.1 fusion.7
  56.0 0.1 reshape.49.live_ref
  56.1 0.1 reshape.48
  56.2 0.1 reshape.50
  56.2 0.1 copy.14
  56.3 0.6 all_to_all.20
  56.9 0.0 all-to-all-done
  57.0 0.6 broadcast_in_dim.3
  57.6 7.5 %all-to-all-start.1 = ((f32[8,16,128]{2,1,0:T(8,128)}), f32[8,16,128]{2,1,0:T(8,128)S(1)}, u32[]{:S(2)}, u32[]{:S(2)}) async-start(f32[8,16,128]{2,1,0:T(8,128)} %broadcast_in_dim.3), calls=%async_computation.1 | async-start | bytes 131072 | tf_op jit(solution)/shard_map/gramian/all_to_all | solution.py:155
  65.2 1.3 place.1.place_ref
  66.4 6.3 %all-to-all-done.1 = f32[8,16,128]{2,1,0:T(8,128)S(1)} async-done(((f32[8,16,128]{2,1,0:T(8,128)}), f32[8,16,128]{2,1,0:T(8,128)S(1)}, u32[]{:S(2)}, u32[]{:S(2)}) %all-to-all-start.1) | async-done | bytes 65568 | tf_op jit(solution)/shard_map/gramian/all_to_all | solution.py:155
  72.7 4.6 %all-to-all-start.3 = ((s32[4,1,1152]{2,1,0:T(1,128)}), s32[4,1,1152]{2,1,0:T(1,128)S(1)}, u32[]{:S(2)}, u32[]{:S(2)}) async-start(s32[4,1,1152]{2,1,0:T(1,128)} %all_to_all.20), calls=%async_computation.3 | async-start | bytes 36864 | tf_op jit(solution)/shard_map/index_exchange/all_to_all | solution.py:176
  77.4 12.4 %all-gather.6.cloned.1.call-done = bf16[1,12288,128]{2,1,0:T(8,128)(2,1)} async-done(((bf16[1,1536,128]{2,1,0:T(8,128)(2,1)}), bf16[1,12288,128]{2,1,0:T(8,128)(2,1)}) %all-gather.6.cloned.1.call-update) | async-done | bytes 3145744 | tf_op jit(solution)/shard_map/gather_y/all_gather | solution.py:147
  89.8 0.0 copy-start.1
  89.8 1.9 %copy-done.1 = bf16[1,12288,128]{2,1,0:T(8,128)(2,1)S(1)} copy-done((bf16[1,12288,128]{2,1,0:T(8,128)(2,1)S(1)}, bf16[1,12288,128]{2,1,0:T(8,128)(2,1)}, u32[]{:S(2)}) %copy-start.1) | copy-done | bytes 3145752
  91.7 3.0 %select.16 = bf16[8,352,128]{2,1,0:T(8,128)(2,1)} custom-call(s32[64]{0:T(128)S(1)} %get-tuple-element.10.block_ref, s32[320,128]{1,0:T(8,128)S(1)} %place.1.place_ref, f32[16,128]{1,0:T(8,128)S(1)} %reduce_sum.19.gram_ref, bf16[12288,128]{1,0:T(8,128)(2,1)S(1)} %bitcast.21), custom_call_target="tpu_custom_call" | custom-call | flops 700000000 | bytes 4000000 | tf_op jit(solution)/shard_map/select/pallas_call | solution.py:213
  94.7 0.0 all-to-all-done.3
  94.7 4.3 %all-to-all-start.2 = ((bf16[8,352,128]{2,1,0:T(8,128)(2,1)}), bf16[8,352,128]{2,1,0:T(8,128)(2,1)S(1)}, u32[]{:S(2)}, u32[]{:S(2)}) async-start(bf16[8,352,128]{2,1,0:T(8,128)(2,1)} %select.16), calls=%async_computation.2 | async-start | bytes 1441792 | tf_op jit(solution)/shard_map/exchange/all_to_all | solution.py:224
  99.0 0.0 copy-done
  99.0 0.1 reshape.55
  99.1 0.1 copy.15
  99.2 0.1 reshape.56
  99.3 0.1 copy.16
  99.4 0.1 reshape.54.live_ref
  99.5 1.2 weights.1.weight_ref
  100.7 10.1 %all-to-all-done.2.recv_ref = bf16[8,352,128]{2,1,0:T(8,128)(2,1)S(1)} async-done(((bf16[8,352,128]{2,1,0:T(8,128)(2,1)}), bf16[8,352,128]{2,1,0:T(8,128)(2,1)S(1)}, u32[]{:S(2)}, u32[]{:S(2)}) %all-to-all-start.2) | async-done | bytes 720928 | tf_op jit(solution)/shard_map/exchange/all_to_all | solution.py:224
  110.8 3.2 %solve.1 = f32[128,128]{1,0:T(8,128)S(1)} custom-call(bf16[8,352,128]{2,1,0:T(8,128)(2,1)S(1)} %all-to-all-done.2.recv_ref, bf16[1280,128]{1,0:T(8,128)(2,1)S(1)} %weights.1.weight_ref, f32[128,128]{1,0:T(8,128)S(1)} %constant_dynamic-slice_fusion.start_ref), custom_call_target="tpu_custom_call" | custom-call | flops 800000000 | bytes 1200000 | tf_op jit(solution)/shard_map/solve/pallas_call | solution.py:227
  114.0 12.3 %all_gather.19 = f32[512,128]{1,0:T(8,128)S(1)} all-gather(f32[128,128]{1,0:T(8,128)S(1)} %solve.1), channel_id=1, replica_groups=mesh['z'=12,'y'=8,'core'=2,'x'=4] {'x'}, dimensions={0}, use_global_device_ids=true | all-gather | bytes 327680 | tf_op jit(solution)/shard_map/gather_x/all_gather | solution.py:238
  126.3 0.7 copy.21
  (9 shorter events, 0.1 us)
Async XLA Ops:
  6.5 92.5 %copy-start = (f32[512,128]{1,0:T(8,128)S(1)}, f32[512,128]{1,0:T(8,128)}, u32[]{:S(2)}) copy-start(f32[512,128]{1,0:T(8,128)} %param.13) | copy-start | bytes 786436
  6.5 83.3 %all-gather.6.cloned.1.call-start = ((), (), s32[]{:S(2)}) async-start(), calls=%async_computation.4 | async-start | bytes 3538944 | tf_op jit(solution)/shard_map/gather_y/all_gather | solution.py:147
  45.8 11.2 %all-to-all-start = ((f32[8,16,128]{2,1,0:T(8,128)}), f32[8,16,128]{2,1,0:T(8,128)S(1)}, u32[]{:S(2)}, u32[]{:S(2)}) async-start(f32[8,16,128]{2,1,0:T(8,128)} %bitcast.5), calls=%async_computation | async-start | bytes 131072 | tf_op jit(solution)/shard_map/gramian/all_to_all | solution.py:153
  57.6 15.1 %all-to-all-start.1 = ((f32[8,16,128]{2,1,0:T(8,128)}), f32[8,16,128]{2,1,0:T(8,128)S(1)}, u32[]{:S(2)}, u32[]{:S(2)}) async-start(f32[8,16,128]{2,1,0:T(8,128)} %broadcast_in_dim.3), calls=%async_computation.1 | async-start | bytes 131072 | tf_op jit(solution)/shard_map/gramian/all_to_all | solution.py:155
  72.7 22.0 %all-to-all-start.3 = ((s32[4,1,1152]{2,1,0:T(1,128)}), s32[4,1,1152]{2,1,0:T(1,128)S(1)}, u32[]{:S(2)}, u32[]{:S(2)}) async-start(s32[4,1,1152]{2,1,0:T(1,128)} %all_to_all.20), calls=%async_computation.3 | async-start | bytes 36864 | tf_op jit(solution)/shard_map/index_exchange/all_to_all | solution.py:176
  89.8 1.9 %copy-start.1 = (bf16[1,12288,128]{2,1,0:T(8,128)(2,1)S(1)}, bf16[1,12288,128]{2,1,0:T(8,128)(2,1)}, u32[]{:S(2)}) copy-start(bf16[1,12288,128]{2,1,0:T(8,128)(2,1)} %all-gather.6.cloned.1.call-done) | copy-start | bytes 9437188
  94.7 16.1 %all-to-all-start.2 = ((bf16[8,352,128]{2,1,0:T(8,128)(2,1)}), bf16[8,352,128]{2,1,0:T(8,128)(2,1)S(1)}, u32[]{:S(2)}, u32[]{:S(2)}) async-start(bf16[8,352,128]{2,1,0:T(8,128)(2,1)} %select.16), calls=%async_computation.2 | async-start | bytes 1441792 | tf_op jit(solution)/shard_map/exchange/all_to_all | solution.py:224
Sparse Core Ops, SparseCore 0:
  43.8 45.9 all-gather.5

commit v3 on v2

--- a/solution.py
+++ b/solution.py
@@ -137,6 +137,23 @@
     return pltpu.CompilerParams(vmem_limit_bytes=24 * 1024 * 1024)
 
 
+def spread(value, axis, size):
+    return lax.all_to_all(jnp.broadcast_to(value[None], (size,) + value.shape), axis, 0, 0, tiled=True)
+
+
+def from_next(value):
+    return lax.ppermute(value, "y", [(i, (i - 1) % Y) for i in range(Y)])
+
+
+def from_last(value):
+    return lax.ppermute(value, "y", [(i, (i + 1) % Y) for i in range(Y)])
+
+
+def lines(values, width):
+    rows = values.reshape(-1, width).astype(f32)
+    return jnp.pad(rows, ((0, 0), (0, BLK - width)))
+
+
 def local(block_ids, pair_live, user_rows, item_rows, counts, item_emb, user_emb):
     core = lax.axis_index("core")
     part = lax.axis_index("x")
@@ -144,44 +161,62 @@
     with jax.named_scope("gather_z"):
         column = lax.all_gather(own_block, "z", axis=0, tiled=True)
     with jax.named_scope("gather_y"):
-        half = lax.all_gather(column, "y", axis=0, tiled=True)
+        ups, downs = [column], [column]
+        for _ in range(Y // 2 - 1):
+            ups.append(from_next(ups[-1]))
+            downs.append(from_last(downs[-1]))
+        ups.append(from_next(ups[-1]))
+        half = jnp.concatenate(ups + downs[:0:-1], axis=0)
 
     with jax.named_scope("gramian"):
         gram = lax.dot_general(
             column, column, (((0,), (0,)), ((), ())), preferred_element_type=f32
-        )
-        gram = lax.all_to_all(gram.reshape(C * X, GRAM, E), ("core", "x"), 0, 0, tiled=True)
-        gram = jnp.broadcast_to(jnp.sum(gram, axis=0)[None], (Y, GRAM, E))
-        gram = jnp.sum(lax.all_to_all(gram, "y", 0, 0, tiled=True), axis=0)
-
+        ).reshape(C * X, GRAM, E)
     with jax.named_scope("index_exchange"):
+        user_pack = jnp.concatenate(
+            [
+                lines(user_rows, BLK).reshape(GROUPS, -1, BLK),
+                lines(counts, BLK).reshape(GROUPS, -1, BLK),
+                lines(pair_live, PAIRS).reshape(GROUPS, -1, BLK),
+            ],
+            axis=1,
+        )
         item_pack = jnp.concatenate(
             [
-                item_rows.reshape(GROUPS, PAIRS * NNZ),
-                jnp.pad(block_ids.reshape(GROUPS, PAIRS), ((0, 0), (0, NNZ - PAIRS))),
-                jnp.pad(pair_live.reshape(GROUPS, PAIRS), ((0, 0), (0, NNZ - PAIRS))),
+                lines(item_rows, BLK),
+                lines(block_ids, GROUPS * PAIRS),
+                lines(pair_live, GROUPS * PAIRS),
+            ],
+            axis=0,
+        )
+        pack = jnp.concatenate(
+            [
+                gram,
+                jnp.tile(user_pack, (C, 1, 1)),
+                jnp.broadcast_to(item_pack[None], (C * X,) + item_pack.shape),
             ],
             axis=1,
         )
-        item_pack = lax.all_gather(item_pack, "core", axis=0, tiled=False)
-        item_pack = item_pack.reshape(C * GROUPS, (PAIRS + 2) * NNZ)
-        user_pack = jnp.concatenate(
-            [
-                user_rows.reshape(GROUPS, PAIRS * NNZ),
-                counts.reshape(GROUPS, PAIRS * NNZ),
-                jnp.pad(pair_live.reshape(GROUPS, PAIRS), ((0, 0), (0, BLK - PAIRS))),
-            ],
-            axis=1,
-        )
-        user_pack = lax.all_to_all(user_pack, "x", 0, 0, tiled=True)
-
-    span = PAIRS * NNZ
-    ids = item_pack[:, span : span + PAIRS].reshape(-1)
-    live = item_pack[:, span + NNZ : span + NNZ + PAIRS].reshape(-1)
+        n_user, n_item = user_pack.shape[1], item_pack.shape[0]
+        pack = jnp.pad(pack, ((0, 0), (0, -pack.shape[1] % 8), (0, 0)))
+        pack = lax.all_to_all(pack, ("core", "x"), 0, 0, tiled=True)
+        gram = jnp.sum(pack[:, :GRAM], axis=0)
+        pack = pack.reshape(C, X, -1, BLK)
+        user_pack = lax.dynamic_index_in_dim(pack, core, 0, keepdims=False)
+        user_pack = user_pack[:, GRAM : GRAM + n_user].astype(jnp.int32)
+        item_pack = lax.dynamic_index_in_dim(pack, part, 1, keepdims=False)
+        item_pack = item_pack[:, GRAM + n_user : GRAM + n_user + n_item].astype(jnp.int32)
+    with jax.named_scope("gramian"):
+        gram = jnp.sum(spread(gram, "y", Y), axis=0)
+
+    span = PAIRS * NNZ // BLK
+    ids = item_pack[:, -2, : GROUPS * PAIRS].reshape(-1)
+    live = item_pack[:, -1, : GROUPS * PAIRS].reshape(-1)
     z_of, y_of, c_of = ids // (Y * C), ids // C % Y, ids % C
-    spots = jnp.clip(y_of * Z + z_of, 0, Z * Y - 1)
+    turn = (y_of - lax.axis_index("y")) % Y
+    spots = jnp.clip(turn * Z + z_of, 0, Z * Y - 1)
     seen = jnp.where(c_of == core, live, 0)
-    slots = item_pack[:, :span].reshape(C * GROUPS * PAIRS, NNZ).T
+    slots = item_pack[:, :-2].reshape(C * GROUPS * PAIRS, NNZ).T
 
     with jax.named_scope("weights"):
         weight = pl.pallas_call(
@@ -193,7 +228,7 @@
             compiler_params=params(),
             cost_estimate=pl.CostEstimate(flops=2_000_000, bytes_accessed=400_000, transcendentals=0),
         )(
-            user_pack[:, 2 * span : 2 * span + PAIRS].reshape(-1),
+            user_pack[:, 2 * span, :PAIRS].reshape(-1),
             user_pack[:, :span].reshape(X * PAIRS, NNZ).T,
             user_pack[:, span : 2 * span].reshape(X * PAIRS, NNZ).T,
         )
@@ -235,7 +270,7 @@
             ),
         )(received, weight, start)
     with jax.named_scope("gather_x"):
-        return lax.all_gather(solved, "x", axis=0, tiled=True)
+        return spread(solved, "x", X).reshape(X * BLK, E)
 
 
 def solution(mesh):

time: 135 us -> 140 us (1.037)
  the two profiles are of different devices: /device:TPU:8 before, /device:TPU:24 now
where the time goes in v3:
time: 140 us; the launch traced here: 138 us
  blocking collectives  45.9 us (33%)
  starting transfers between devices  38.6 us (28%)
  waiting for transfers between devices  25.2 us (18%)
  local copies, waits for them, and re-layouts  12.2 us (9%)
  Pallas kernels  7.81 us (6%)
  other arithmetic  6.94 us (5%)
  matrix products  1.45 us (1%)
    all_gather x1, blocking collectives, local(): column = lax.all_gather(own_block, 'z', axis=0, tiled=True)  36.3 us
    ppermute x3, starting transfers between devices, from_last(): return lax.ppermute(value, 'y', [(i, (i + 1) % Y) for i in range(Y)])  14.9 us
    all_to_all x1, blocking collectives, spread(): lax.all_to_all(jnp.broadcast_to(value[None], (size,) + value.shape), axis...  9.64 us
    all_to_all x1, waiting for transfers between devices, local(): received = lax.all_to_all(chosen, ('core', 'x'), 0, 0, tiled=True)  9.18 us
    ppermute x4, waiting for transfers between devices, from_next(): return lax.ppermute(value, 'y', [(i, (i - 1) % Y) for i in range(Y)])  8.45 us
    ppermute x4, starting transfers between devices, from_next(): return lax.ppermute(value, 'y', [(i, (i - 1) % Y) for i in range(Y)])  8.1 us
    all_to_all x1, starting transfers between devices, spread(): lax.all_to_all(jnp.broadcast_to(value[None], (size,) + value.shape), axis...  7.76 us
    unnamed x16, local copies, waits for them, and re-layouts  7.59 us
  transfers between devices with their start and end apart: 10, of which 4 were waited for; matrix products, arithmetic and copies ran while one was open for 11% of the time, Pallas kernels for 2%

profile of v3, /device:TPU:24, one launch (start us, length us, event | category | flops | bytes accessed | tf_op | source)
XLA Modules:
  0.0 138.4 jit_solution(17540691253496430172)
XLA Ops:
  0.0 0.9 convert_element_type.71
  0.9 36.3 %all-gather = bf16[1,1536,128]{2,1,0:T(8,128)(2,1)} all-gather(bf16[1,128,128]{2,1,0:T(8,128)(2,1)S(1)} %convert_element_type.71), channel_id=2, replica_groups=mesh['z'=12,'y'=8,'core'=2,'x'=4] {'z'}, dimensions={1}, use_global_device_ids=true | all-gather | bytes 425984 | tf_op jit(solution)/shard_map/gather_z/all_gather | solution.py:162
  37.2 2.3 %collective-permute-start = (bf16[1536,128]{1,0:T(8,128)(2,1)}, bf16[1536,128]{1,0:T(8,128)(2,1)}, u32[]{:S(2)}, u32[]{:S(2)}) collective-permute-start(bf16[1536,128]{1,0:T(8,128)(2,1)} %bitcast), channel_id=1, source_target_pairs={{0,56},{8,0},{16,8},{24,16},{32,24},{40,32},{48,40},{56,48},{1,57}... | collective-permute-start | bytes 1179656 | tf_op jit(solution)/shard_map/gather_y/ppermute | solution.py:145
  39.5 4.7 %collective-permute-start.4 = (bf16[1536,128]{1,0:T(8,128)(2,1)}, bf16[1536,128]{1,0:T(8,128)(2,1)}, u32[]{:S(2)}, u32[]{:S(2)}) collective-permute-start(bf16[1536,128]{1,0:T(8,128)(2,1)} %bitcast), channel_id=1, source_target_pairs={{0,8},{8,16},{16,24},{24,32},{32,40},{40,48},{48,56},{56,0},{1,9},... | collective-permute-start | bytes 1179656 | tf_op jit(solution)/shard_map/gather_y/ppermute | solution.py:149
  44.2 1.5 %fusion.7 = f32[128,128]{1,0:T(8,128)S(1)} fusion(bf16[1,1536,128]{2,1,0:T(8,128)(2,1)} %all-gather), kind=kOutput, calls=%fused_computation.49 | convolution fusion | flops 50331648 | bytes 458752 | tf_op jit(solution)/shard_map/gramian/dot_general | solution.py:172
  45.7 0.7 convert_element_type.77
  46.4 0.7 convert_reduce_fusion
  47.1 0.1 convert_element_type.82
  47.2 0.1 convert_element_type.83
  47.3 0.7 convert_element_type.79
  48.0 0.1 convert_element_type.80
  48.1 0.7 convert_element_type.73
  48.8 0.1 convert_element_type.74
  48.9 0.7 convert_element_type.75
  49.6 0.1 convert_element_type.76
  49.7 0.7 select_maximum_fusion
  50.4 4.3 %all-to-all-start = ((f32[8,48,128]{2,1,0:T(8,128)}), f32[8,48,128]{2,1,0:T(8,128)}, u32[]{:S(2)}, u32[]{:S(2)}) async-start(f32[8,48,128]{2,1,0:T(8,128)} %select_maximum_fusion), calls=%async_computation | async-start | bytes 393216 | tf_op jit(solution)/shard_map/index_exchange/all_to_all | solution.py:202
  54.7 1.0 constant_dynamic-update-slice_fusion.7
  55.8 5.3 %all-to-all-done = f32[8,48,128]{2,1,0:T(8,128)} async-done(((f32[8,48,128]{2,1,0:T(8,128)}), f32[8,48,128]{2,1,0:T(8,128)}, u32[]{:S(2)}, u32[]{:S(2)}) %all-to-all-start) | async-done | bytes 196640 | tf_op jit(solution)/shard_map/index_exchange/all_to_all | solution.py:202
  61.1 0.8 dynamic-slice_bitcast_fusion.1
  61.9 0.0 collective-permute-done
  61.9 1.9 %collective-permute-start.1 = (bf16[1536,128]{1,0:T(8,128)(2,1)}, bf16[1536,128]{1,0:T(8,128)(2,1)}, u32[]{:S(2)}, u32[]{:S(2)}) collective-permute-start(bf16[1536,128]{1,0:T(8,128)(2,1)} %collective-permute-done), channel_id=1, source_target_pairs={{0,56},{8,0},{16,8},{24,16},{32,24},{40,32},{48,40},{56,48},{1,57}... | collective-permute-start | bytes 1179656 | tf_op jit(solution)/shard_map/gather_y/ppermute | solution.py:145
  63.9 0.1 reshape_squeeze.7.live_ref
  64.0 0.1 reshape_squeeze.6
  64.0 0.1 reshape.72
  64.1 0.1 copy.15
  64.2 0.9 slice_reduce_fusion
  65.1 0.6 broadcast_in_dim.8
  65.7 7.8 %all-to-all-start.1 = ((f32[8,16,128]{2,1,0:T(8,128)}), f32[8,16,128]{2,1,0:T(8,128)}, u32[]{:S(2)}, u32[]{:S(2)}) async-start(f32[8,16,128]{2,1,0:T(8,128)} %broadcast_in_dim.8), calls=%async_computation.1 | async-start | bytes 131072 | tf_op jit(solution)/shard_map/gramian/all_to_all | solution.py:141
  73.4 0.0 collective-permute-done.4
  73.5 4.6 %collective-permute-start.5 = (bf16[1536,128]{1,0:T(8,128)(2,1)}, bf16[1536,128]{1,0:T(8,128)(2,1)}, u32[]{:S(2)}, u32[]{:S(2)}) collective-permute-start(bf16[1536,128]{1,0:T(8,128)(2,1)} %collective-permute-done.4), channel_id=1, source_target_pairs={{0,8},{8,16},{16,24},{24,32},{32,40},{40,48},{48,56},{56,0},{1,9},... | collective-permute-start | bytes 1179656 | tf_op jit(solution)/shard_map/gather_y/ppermute | solution.py:149
  78.0 0.0 collective-permute-done.1
  78.0 1.9 %collective-permute-start.2 = (bf16[1536,128]{1,0:T(8,128)(2,1)}, bf16[1536,128]{1,0:T(8,128)(2,1)}, u32[]{:S(2)}, u32[]{:S(2)}) collective-permute-start(bf16[1536,128]{1,0:T(8,128)(2,1)} %collective-permute-done.1), channel_id=1, source_target_pairs={{0,56},{8,0},{16,8},{24,16},{32,24},{40,32},{48,40},{56,48},{1,57}... | collective-permute-start | bytes 1179656 | tf_op jit(solution)/shard_map/gather_y/ppermute | solution.py:145
  80.0 1.3 place.1.place_ref
  81.3 0.0 copy-start.2
  81.3 0.7 copy-done.2
  82.0 0.0 all-to-all-done.1
  82.0 0.9 reduce_sum.19.gram_ref
  82.8 1.1 constant_dynamic-update-slice_fusion.6
  83.9 2.3 %collective-permute-done.5 = bf16[1536,128]{1,0:T(8,128)(2,1)} collective-permute-done((bf16[1536,128]{1,0:T(8,128)(2,1)}, bf16[1536,128]{1,0:T(8,128)(2,1)}, u32[]{:S(2)}, u32[]{:S(2)}) %collective-permute-start.5) | collective-permute-done | bytes 393248 | tf_op jit(solution)/shard_map/gather_y/ppermute | solution.py:149
  86.2 5.6 %collective-permute-start.6 = (bf16[1536,128]{1,0:T(8,128)(2,1)}, bf16[1536,128]{1,0:T(8,128)(2,1)S(1)}, u32[]{:S(2)}, u32[]{:S(2)}) collective-permute-start(bf16[1536,128]{1,0:T(8,128)(2,1)} %collective-permute-done.5), channel_id=1, source_target_pairs={{0,8},{8,16},{16,24},{24,32},{32,40},{40,48},{48,56},{56,0},{1,9},... | collective-permute-start | bytes 1179656 | tf_op jit(solution)/shard_map/gather_y/ppermute | solution.py:149
  91.8 1.9 %collective-permute-start.3 = (bf16[1536,128]{1,0:T(8,128)(2,1)}, bf16[1536,128]{1,0:T(8,128)(2,1)S(1)}, u32[]{:S(2)}, u32[]{:S(2)}) collective-permute-start(bf16[1536,128]{1,0:T(8,128)(2,1)} %collective-permute-done.2), channel_id=1, source_target_pairs={{0,56},{8,0},{16,8},{24,16},{32,24},{40,32},{48,40},{56,48},{1,57}... | collective-permute-start | bytes 1179656 | tf_op jit(solution)/shard_map/gather_y/ppermute | solution.py:145
  93.7 1.0 constant_dynamic-update-slice_fusion.5
  94.8 1.0 constant_dynamic-update-slice_fusion.4
  95.8 8.4 %collective-permute-done.3 = bf16[1536,128]{1,0:T(8,128)(2,1)S(1)} collective-permute-done((bf16[1536,128]{1,0:T(8,128)(2,1)}, bf16[1536,128]{1,0:T(8,128)(2,1)S(1)}, u32[]{:S(2)}, u32[]{:S(2)}) %collective-permute-start.3) | collective-permute-done | bytes 393248 | tf_op jit(solution)/shard_map/gather_y/ppermute | solution.py:145
  104.3 0.1 constant_dynamic-update-slice_fusion.3
  104.3 0.0 collective-permute-done.6
  104.3 0.1 constant_dynamic-update-slice_fusion.2
  104.4 1.0 constant_dynamic-update-slice_fusion.1
  105.5 1.0 constant_dynamic-update-slice_fusion.half_ref
  106.5 2.1 %select.33 = bf16[8,352,128]{2,1,0:T(8,128)(2,1)S(1)} custom-call(s32[64]{0:T(128)S(1)} %get-tuple-element.10.block_ref, s32[320,128]{1,0:T(8,128)S(1)} %copy-done.3, f32[16,128]{1,0:T(8,128)S(1)} %reduce_sum.19.gram_ref, bf16[12288,128]{1,0:T(8,128)(2,1)S(1)} %constant_dynamic-update-slice_fusion.half_ref), custom_call_target="tpu_custom_call" | custom-call | flops 700000000 | bytes 4000000 | tf_op jit(solution)/shard_map/select/pallas_call | solution.py:248
  108.7 0.9 copy-done.1
  109.5 3.5 %all-to-all-start.2 = ((bf16[8,352,128]{2,1,0:T(8,128)(2,1)}), bf16[8,352,128]{2,1,0:T(8,128)(2,1)S(1)}, u32[]{:S(2)}, u32[]{:S(2)}) async-start(bf16[8,352,128]{2,1,0:T(8,128)(2,1)} %copy-done.1), calls=%async_computation.2 | async-start | bytes 1441792 | tf_op jit(solution)/shard_map/exchange/all_to_all | solution.py:259
  113.1 0.9 dynamic-slice_bitcast_fusion
  114.0 0.1 reshape.73
  114.1 0.1 copy.16
  114.2 0.1 reshape.74
  114.2 0.1 copy.17
  114.3 0.1 squeeze.14.live_ref
  114.4 1.2 weights.1.weight_ref
  115.6 9.2 %all-to-all-done.2.recv_ref = bf16[8,352,128]{2,1,0:T(8,128)(2,1)S(1)} async-done(((bf16[8,352,128]{2,1,0:T(8,128)(2,1)}), bf16[8,352,128]{2,1,0:T(8,128)(2,1)S(1)}, u32[]{:S(2)}, u32[]{:S(2)}) %all-to-all-start.2) | async-done | bytes 720928 | tf_op jit(solution)/shard_map/exchange/all_to_all | solution.py:259
  124.8 3.2 %solve.1 = f32[128,128]{1,0:T(8,128)S(1)} custom-call(bf16[8,352,128]{2,1,0:T(8,128)(2,1)S(1)} %all-to-all-done.2.recv_ref, bf16[1280,128]{1,0:T(8,128)(2,1)S(1)} %weights.1.weight_ref, f32[128,128]{1,0:T(8,128)S(1)} %constant_dynamic-slice_fusion.start_ref), custom_call_target="tpu_custom_call" | custom-call | flops 800000000 | bytes 1200000 | tf_op jit(solution)/shard_map/solve/pallas_call | solution.py:262
  128.1 9.6 %all_to_all.20 = f32[4,128,128]{2,1,0:T(8,128)S(1)} all-to-all(f32[4,128,128]{2,1,0:T(8,128)S(1)} %broadcast_in_dim.10), channel_id=1, replica_groups=mesh['z'=12,'y'=8,'core'=2,'x'=4] {'x'}, dimensions={0} | all-to-all | bytes 524288 | tf_op jit(solution)/shard_map/gather_x/all_to_all | solution.py:141
  137.7 0.7 copy.26
  (20 shorter events, 0.2 us)
Async XLA Ops:
  0.0 55.8 %copy-start = (f32[512,128]{1,0:T(8,128)S(1)}, f32[512,128]{1,0:T(8,128)}, u32[]{:S(2)}) copy-start(f32[512,128]{1,0:T(8,128)} %param.13) | copy-start | bytes 786436
  37.2 24.8 %collective-permute-start = (bf16[1536,128]{1,0:T(8,128)(2,1)}, bf16[1536,128]{1,0:T(8,128)(2,1)}, u32[]{:S(2)}, u32[]{:S(2)}) collective-permute-start(bf16[1536,128]{1,0:T(8,128)(2,1)} %bitcast), channel_id=1, source_target_pairs={{0,56},{8,0},{16,8},{24,16},{32,24},{40,32},{48,40},{56,48},{1,57}... | collective-permute-start | bytes 1179656 | tf_op jit(solution)/shard_map/gather_y/ppermute | solution.py:145
  39.5 33.9 %collective-permute-start.4 = (bf16[1536,128]{1,0:T(8,128)(2,1)}, bf16[1536,128]{1,0:T(8,128)(2,1)}, u32[]{:S(2)}, u32[]{:S(2)}) collective-permute-start(bf16[1536,128]{1,0:T(8,128)(2,1)} %bitcast), channel_id=1, source_target_pairs={{0,8},{8,16},{16,24},{24,32},{32,40},{40,48},{48,56},{56,0},{1,9},... | collective-permute-start | bytes 1179656 | tf_op jit(solution)/shard_map/gather_y/ppermute | solution.py:149
  50.4 10.7 %all-to-all-start = ((f32[8,48,128]{2,1,0:T(8,128)}), f32[8,48,128]{2,1,0:T(8,128)}, u32[]{:S(2)}, u32[]{:S(2)}) async-start(f32[8,48,128]{2,1,0:T(8,128)} %select_maximum_fusion), calls=%async_computation | async-start | bytes 393216 | tf_op jit(solution)/shard_map/index_exchange/all_to_all | solution.py:202
  61.9 16.1 %collective-permute-start.1 = (bf16[1536,128]{1,0:T(8,128)(2,1)}, bf16[1536,128]{1,0:T(8,128)(2,1)}, u32[]{:S(2)}, u32[]{:S(2)}) collective-permute-start(bf16[1536,128]{1,0:T(8,128)(2,1)} %collective-permute-done), channel_id=1, source_target_pairs={{0,56},{8,0},{16,8},{24,16},{32,24},{40,32},{48,40},{56,48},{1,57}... | collective-permute-start | bytes 1179656 | tf_op jit(solution)/shard_map/gather_y/ppermute | solution.py:145
  65.7 16.3 %all-to-all-start.1 = ((f32[8,16,128]{2,1,0:T(8,128)}), f32[8,16,128]{2,1,0:T(8,128)}, u32[]{:S(2)}, u32[]{:S(2)}) async-start(f32[8,16,128]{2,1,0:T(8,128)} %broadcast_in_dim.8), calls=%async_computation.1 | async-start | bytes 131072 | tf_op jit(solution)/shard_map/gramian/all_to_all | solution.py:141
  73.5 12.7 %collective-permute-start.5 = (bf16[1536,128]{1,0:T(8,128)(2,1)}, bf16[1536,128]{1,0:T(8,128)(2,1)}, u32[]{:S(2)}, u32[]{:S(2)}) collective-permute-start(bf16[1536,128]{1,0:T(8,128)(2,1)} %collective-permute-done.4), channel_id=1, source_target_pairs={{0,8},{8,16},{16,24},{24,32},{32,40},{40,48},{48,56},{56,0},{1,9},... | collective-permute-start | bytes 1179656 | tf_op jit(solution)/shard_map/gather_y/ppermute | solution.py:149
  78.0 13.8 %collective-permute-start.2 = (bf16[1536,128]{1,0:T(8,128)(2,1)}, bf16[1536,128]{1,0:T(8,128)(2,1)}, u32[]{:S(2)}, u32[]{:S(2)}) collective-permute-start(bf16[1536,128]{1,0:T(8,128)(2,1)} %collective-permute-done.1), channel_id=1, source_target_pairs={{0,56},{8,0},{16,8},{24,16},{32,24},{40,32},{48,40},{56,48},{1,57}... | collective-permute-start | bytes 1179656 | tf_op jit(solution)/shard_map/gather_y/ppermute | solution.py:145
  81.3 0.7 copy-start.2
  82.8 23.7 %copy-start.3 = (s32[320,128]{1,0:T(8,128)S(1)}, s32[320,128]{1,0:T(8,128)}, u32[]{:S(2)}) copy-start(s32[320,128]{1,0:T(8,128)} %copy-done.2) | copy-start | bytes 491524
  86.2 18.1 %collective-permute-start.6 = (bf16[1536,128]{1,0:T(8,128)(2,1)}, bf16[1536,128]{1,0:T(8,128)(2,1)S(1)}, u32[]{:S(2)}, u32[]{:S(2)}) collective-permute-start(bf16[1536,128]{1,0:T(8,128)(2,1)} %collective-permute-done.5), channel_id=1, source_target_pairs={{0,8},{8,16},{16,24},{24,32},{32,40},{40,48},{48,56},{56,0},{1,9},... | collective-permute-start | bytes 1179656 | tf_op jit(solution)/shard_map/gather_y/ppermute | solution.py:149
  91.8 12.5 %collective-permute-start.3 = (bf16[1536,128]{1,0:T(8,128)(2,1)}, bf16[1536,128]{1,0:T(8,128)(2,1)S(1)}, u32[]{:S(2)}, u32[]{:S(2)}) collective-permute-start(bf16[1536,128]{1,0:T(8,128)(2,1)} %collective-permute-done.2), channel_id=1, source_target_pairs={{0,56},{8,0},{16,8},{24,16},{32,24},{40,32},{48,40},{56,48},{1,57}... | collective-permute-start | bytes 1179656 | tf_op jit(solution)/shard_map/gather_y/ppermute | solution.py:145
  108.6 0.9 copy-start.1
  109.5 15.3 %all-to-all-start.2 = ((bf16[8,352,128]{2,1,0:T(8,128)(2,1)}), bf16[8,352,128]{2,1,0:T(8,128)(2,1)S(1)}, u32[]{:S(2)}, u32[]{:S(2)}) async-start(bf16[8,352,128]{2,1,0:T(8,128)(2,1)} %copy-done.1), calls=%async_computation.2 | async-start | bytes 1441792 | tf_op jit(solution)/shard_map/exchange/all_to_all | solution.py:259

commit v4 on v3

v4 whole, which is shorter than its diff:
```python
import functools

import jax
import jax.numpy as jnp
from jax import lax
from jax.experimental import pallas as pl
from jax.experimental.pallas import tpu as pltpu
from jax.sharding import Mesh, PartitionSpec as P

Z, Y, C, X = 12, 8, 2, 4
E = 128
BLK = 128
PAIRS = 8
NNZ = 64
LIVE = 320
ITERS = 3
GROUPS = 4
GRAM = E // (C * X)

conf_rate = 0.5
ridge_weight = 0.5

bf16 = jnp.bfloat16
f32 = jnp.float32


def dot(a, b):
    return lax.dot_general(a, b, (((1,), (0,)), ((), ())), preferred_element_type=f32)


def split(a):
    hi = a.astype(bf16)
    return hi, (a - hi.astype(f32)).astype(bf16)


def offsets(live_ref, base):
    out = [0]
    for p in range(PAIRS - 1):
        out.append(out[-1] + live_ref[base + p])
    return out


USER_AT = GRAM
COUNT_AT = USER_AT + PAIRS
ITEM_AT = COUNT_AT + PAIRS
BLOCK_AT = ITEM_AT + GROUPS * PAIRS
LIVE_AT = BLOCK_AT + GROUPS
PACK = LIVE_AT + GROUPS


def pack_kernel(gram_ref, block_ref, live_ref, user_ref, item_ref, count_ref, out_ref):
    out_ref[...] = jnp.zeros(out_ref.shape, f32)
    items = item_ref[...].reshape(GROUPS * PAIRS, NNZ).astype(f32)
    for d in range(C * X):
        out_ref[d, :GRAM, :] = gram_ref[d * GRAM : (d + 1) * GRAM, :]
        out_ref[d, USER_AT : USER_AT + PAIRS, :NNZ] = user_ref[d % X].astype(f32)
        out_ref[d, COUNT_AT : COUNT_AT + PAIRS, :NNZ] = count_ref[d % X].astype(f32)
        out_ref[d, ITEM_AT : ITEM_AT + GROUPS * PAIRS, :NNZ] = items
        out_ref[d, BLOCK_AT : BLOCK_AT + GROUPS, :PAIRS] = block_ref[...].astype(f32)
        out_ref[d, LIVE_AT : LIVE_AT + GROUPS, :PAIRS] = live_ref[...].astype(f32)


def weight_kernel(core_ref, live_ref, pack_ref, out_ref, rows_ref):
    packs = [pack_ref[core_ref[0] * X + s] for s in range(X)]
    users = [pack[USER_AT : USER_AT + PAIRS] for pack in packs]
    counts = [pack[COUNT_AT : COUNT_AT + PAIRS] for pack in packs]
    table = jnp.concatenate(users + counts, axis=0).T[:NNZ]
    lane = lax.broadcasted_iota(jnp.int32, (NNZ, BLK), 1).astype(f32)
    slot = lax.broadcasted_iota(jnp.int32, (NNZ, BLK), 0)
    for s in range(X):
        offs = offsets(live_ref, s * PAIRS)
        for p in range(PAIRS):
            q = s * PAIRS + p
            hit = (table[:, q : q + 1] == lane) & (slot < live_ref[q])
            rows = jnp.where(hit, table[:, X * PAIRS + q : X * PAIRS + q + 1], 0.0)
            rows_ref[s, pl.ds(offs[p], NNZ), :] = rows
        out_ref[s * LIVE : (s + 1) * LIVE, :] = rows_ref[s, :LIVE, :].astype(bf16)


def place_kernel(part_ref, seen_ref, live_ref, pack_ref, out_ref, rows_ref):
    items = [
        pack_ref[c * X + part_ref[0], ITEM_AT : ITEM_AT + GROUPS * PAIRS, :] for c in range(C)
    ]
    table = jnp.concatenate(items, axis=0).T[:NNZ].astype(jnp.int32)
    lane = lax.broadcasted_iota(jnp.int32, (LIVE, BLK), 1)
    slot = lax.broadcasted_iota(jnp.int32, (NNZ, 1), 0)
    merged = jnp.full((LIVE, BLK), -1, jnp.int32)
    for d in range(C * GROUPS):
        offs = offsets(live_ref, d * PAIRS)
        for p in range(PAIRS):
            q = d * PAIRS + p
            spot = jnp.where(slot < seen_ref[q], table[:, q : q + 1] + p * BLK, -1)
            rows_ref[d, pl.ds(offs[p], NNZ), :] = jnp.broadcast_to(spot, (NNZ, BLK))
        merged = jnp.where(lane == d, rows_ref[d, :LIVE, :], merged)
    out_ref[...] = merged


def select_kernel(turn_ref, block_ref, place_ref, gram_ref, *refs):
    piece_refs, out_ref = refs[:-1], refs[-1]
    gram_hi, gram_lo = split(gram_ref[...])
    lane = lax.broadcasted_iota(jnp.int32, (LIVE, PAIRS * BLK), 1)
    for d in range(C * GROUPS):
        blocks = []
        for p in range(PAIRS):
            q = d * PAIRS + p
            turn, spot = turn_ref[q], block_ref[q]
            block = piece_refs[0][spot]
            for t in range(1, Y):
                block = jnp.where(turn == t, piece_refs[t][spot], block)
            blocks.append(block)
        onehot = jnp.where(place_ref[:, d : d + 1] == lane, 1.0, 0.0).astype(bf16)
        rows = dot(onehot, jnp.concatenate(blocks, axis=0))
        out_ref[d, :LIVE, :] = rows.astype(bf16)
        out_ref[d, LIVE : LIVE + GRAM, :] = gram_hi
        out_ref[d, LIVE + GRAM :, :] = gram_lo


def solve_kernel(recv_ref, weight_ref, start_ref, out_ref):
    items = (recv_ref[:X, :LIVE, :] + recv_ref[X:, :LIVE, :]).reshape(X * LIVE, E)
    items_t = items.T
    weight = weight_ref[...]
    conf = weight.astype(f32) * conf_rate
    full = jnp.where(weight > 0, 1.0 + conf, 0.0).astype(bf16)
    gram = recv_ref[:, LIVE : LIVE + GRAM, :].astype(f32) + recv_ref[:, LIVE + GRAM :, :].astype(f32)
    gram = gram.reshape(E, E)
    eye = lax.broadcasted_iota(jnp.int32, (E, E), 0) == lax.broadcasted_iota(jnp.int32, (E, E), 1)
    base_hi, base_lo = split(
        gram * (E / (X * Z * Y * C * BLK)) + jnp.where(eye, ridge_weight, 0.0)
    )

    def operator(vectors):
        hi, lo = split(vectors)
        both = jnp.concatenate([hi, lo], axis=1)
        table = dot(items, both)
        table = conf * (table[:, :BLK] + table[:, BLK:])
        table_hi, table_lo = split(table)
        summed = dot(items_t, jnp.concatenate([table_hi, table_lo], axis=1))
        dense = dot(base_hi, both)
        return (
            (summed[:, :BLK] + summed[:, BLK:])
            + (dense[:, :BLK] + dense[:, BLK:])
            + dot(base_lo, hi)
        )

    x = start_ref[...].T
    remain = dot(items_t, full) - operator(x)
    direction = remain
    norm_now = jnp.sum(remain * remain, axis=0, keepdims=True)
    for turn in range(ITERS):
        image = operator(direction)
        step = norm_now / jnp.sum(direction * image, axis=0, keepdims=True)
        x = x + step * direction
        if turn < ITERS - 1:
            remain = remain - step * image
            norm_next = jnp.sum(remain * remain, axis=0, keepdims=True)
            direction = remain + norm_next / norm_now * direction
            norm_now = norm_next
    out_ref[...] = x.T


def vmem():
    return pl.BlockSpec(memory_space=pltpu.VMEM)


def smem():
    return pl.BlockSpec(memory_space=pltpu.SMEM)


def spread(value, axis, size):
    return lax.all_to_all(jnp.broadcast_to(value[None], (size,) + value.shape), axis, 0, 0, tiled=True)


def from_next(value):
    return lax.ppermute(value, "y", [(i, (i - 1) % Y) for i in range(Y)])


def from_last(value):
    return lax.ppermute(value, "y", [(i, (i + 1) % Y) for i in range(Y)])


def call(kernel, out, ins, scratch=(), flops=1_000_000, nbytes=400_000):
    return pl.pallas_call(
        kernel,
        out_shape=out,
        in_specs=ins,
        out_specs=vmem(),
        scratch_shapes=list(scratch),
        compiler_params=pltpu.CompilerParams(vmem_limit_bytes=24 * 1024 * 1024),
        cost_estimate=pl.CostEstimate(flops=flops, bytes_accessed=nbytes, transcendentals=0),
    )


def local(block_ids, pair_live, user_rows, item_rows, counts, item_emb, user_emb):
    core = lax.axis_index("core")
    part = lax.axis_index("x")
    own_block = item_emb[0].astype(bf16)
    with jax.named_scope("gather_z"):
        column = lax.all_gather(own_block, "z", axis=0, tiled=True)
    with jax.named_scope("gather_y"):
        ups, downs = [column], [column]
        for _ in range(Y // 2 - 1):
            ups.append(from_next(ups[-1]))
            downs.append(from_last(downs[-1]))
        ups.append(from_next(ups[-1]))
        pieces = [piece.reshape(Z, BLK, E) for piece in ups + downs[:0:-1]]

    with jax.named_scope("gramian"):
        gram = lax.dot_general(
            column, column, (((0,), (0,)), ((), ())), preferred_element_type=f32
        )
    with jax.named_scope("small_exchange"):
        pack = call(
            pack_kernel, jax.ShapeDtypeStruct((C * X, PACK, BLK), f32), [vmem()] * 6
        )(
            gram,
            block_ids[:, 0],
            pair_live[:, 0],
            user_rows[:, 0],
            item_rows[:, 0],
            counts[:, 0],
        )
        pack, _ = lax.optimization_barrier((pack, ups[1]))
        pack = lax.all_to_all(pack, ("core", "x"), 0, 0, tiled=True)
    with jax.named_scope("gramian"):
        gram = jnp.sum(spread(jnp.sum(pack[:, :GRAM], axis=0), "y", Y), axis=0)

    with jax.named_scope("indices"):
        grid = pack.reshape(C, X, PACK, BLK)
        own = lax.dynamic_slice(grid, (0, part, BLOCK_AT, 0), (C, 1, 2 * GROUPS, PAIRS))
        own = own.reshape(C, 2 * GROUPS, PAIRS).astype(jnp.int32)
        ids, live = own[:, :GROUPS].reshape(-1), own[:, GROUPS:].reshape(-1)
        z_of, y_of, c_of = ids // (Y * C), ids // C % Y, ids % C
        turns = (y_of - lax.axis_index("y")) % Y
        spots = jnp.clip(z_of, 0, Z - 1)
        seen = jnp.where(c_of == core, live, 0)
        user_live = lax.dynamic_slice(grid, (core, 0, LIVE_AT + part, 0), (1, X, 1, PAIRS))
        user_live = user_live.reshape(-1).astype(jnp.int32)

    with jax.named_scope("place"):
        place = call(
            place_kernel,
            jax.ShapeDtypeStruct((LIVE, BLK), jnp.int32),
            [smem()] * 3 + [vmem()],
            [pltpu.VMEM((C * GROUPS, LIVE + NNZ, BLK), jnp.int32)],
        )(part.reshape(1), seen, live, pack)
    with jax.named_scope("weights"):
        weight = call(
            weight_kernel,
            jax.ShapeDtypeStruct((X * LIVE, BLK), bf16),
            [smem()] * 2 + [vmem()],
            [pltpu.VMEM((X, LIVE + NNZ, BLK), f32)],
        )(core.reshape(1), user_live, pack)
    with jax.named_scope("select"):
        chosen = call(
            select_kernel,
            jax.ShapeDtypeStruct((C * GROUPS, LIVE + 2 * GRAM, E), bf16),
            [smem()] * 2 + [vmem()] * (2 + len(pieces)),
            flops=700_000_000,
            nbytes=4_000_000,
        )(turns, spots, place, gram, *pieces)
    with jax.named_scope("exchange"):
        received = lax.all_to_all(chosen, ("core", "x"), 0, 0, tiled=True)
    with jax.named_scope("solve"):
        start = lax.dynamic_slice_in_dim(user_emb, part * BLK, BLK, 0)
        solved = call(
            solve_kernel,
            jax.ShapeDtypeStruct((BLK, E), f32),
            [vmem()] * 3,
            flops=800_000_000,
            nbytes=1_200_000,
        )(received, weight, start)
    with jax.named_scope("gather_x"):
        return spread(solved, "x", X).reshape(X * BLK, E)


def solution(mesh):
    grid = Mesh(mesh.devices.reshape(Z, Y, C, X), ("z", "y", "core", "x"))
    users = ("z", "y", "core")
    return jax.shard_map(
        local,
        mesh=grid,
        in_specs=(
            P(users, "x", None),
            P(users, "x", None),
            P(users, "x", None, None),
            P(users, "x", None, None),
            P(users, "x", None, None),
            P("x", users, None),
            P(users, None),
        ),
        out_specs=P(users, None),
        check_vma=False,
    )
```

time: 140 us -> 132 us (0.943)
  the two profiles are of different devices: /device:TPU:24 before, /device:TPU:1 now
where the time goes in v4:
time: 132 us; the launch traced here: 131 us
  starting transfers between devices  49 us (37%)
  blocking collectives  38.3 us (29%)
  waiting for transfers between devices  28.8 us (22%)
  Pallas kernels  11.1 us (8%)
  local copies, waits for them, and re-layouts  2.33 us (2%)
    all_gather x1, blocking collectives, local(): column = lax.all_gather(own_block, 'z', axis=0, tiled=True)  30.3 us
    ppermute x4, starting transfers between devices, from_next(): return lax.ppermute(value, 'y', [(i, (i - 1) % Y) for i in range(Y)])  19.7 us
    all_to_all x1, starting transfers between devices, local(): pack = lax.all_to_all(pack, ('core', 'x'), 0, 0, tiled=True)  13.9 us
    all_to_all x1, waiting for transfers between devices, local(): received = lax.all_to_all(chosen, ('core', 'x'), 0, 0, tiled=True)  9.99 us
    all_to_all x1, blocking collectives, spread(): lax.all_to_all(jnp.broadcast_to(value[None], (size,) + value.shape), axis...  8 us
    all_to_all x1, waiting for transfers between devices, local(): pack = lax.all_to_all(pack, ('core', 'x'), 0, 0, tiled=True)  6.91 us
    ppermute x4, waiting for transfers between devices, from_next(): return lax.ppermute(value, 'y', [(i, (i - 1) % Y) for i in range(Y)])  6.06 us
    all_to_all x1, starting transfers between devices, local(): received = lax.all_to_all(chosen, ('core', 'x'), 0, 0, tiled=True)  5.81 us
  transfers between devices with their start and end apart: 10, of which 5 were waited for; matrix products, arithmetic and copies ran while one was open for 1% of the time, Pallas kernels for 3%

profile of v4, /device:TPU:1, one launch (start us, length us, event | category | flops | bytes accessed | tf_op | source)
XLA Modules:
  0.0 130.9 jit_solution(16230128917248229275)
XLA Ops:
  0.0 0.0 copy-start
  0.0 0.9 convert_element_type.17
  0.9 30.3 %all-gather = bf16[1,1536,128]{2,1,0:T(8,128)(2,1)S(1)} all-gather(bf16[1,128,128]{2,1,0:T(8,128)(2,1)S(1)} %convert_element_type.17), channel_id=2, replica_groups=mesh['z'=12,'y'=8,'core'=2,'x'=4] {'z'}, dimensions={1}, use_global_device_ids=true | all-gather | bytes 425984 | tf_op jit(solution)/shard_map/gather_z/all_gather | solution.py:198
  31.2 5.1 %collective-permute-start = (bf16[1536,128]{1,0:T(8,128)(2,1)S(1)}, bf16[1536,128]{1,0:T(8,128)(2,1)S(1)}, u32[]{:S(2)}, u32[]{:S(2)}) collective-permute-start(bf16[1536,128]{1,0:T(8,128)(2,1)S(1)} %bitcast.29), channel_id=1, source_target_pairs={{0,56},{8,0},{16,8},{24,16},{32,24},{40,32},{48,40},{56,48},{1,57}... | collective-permute-start | bytes 1179656 | tf_op jit(solution)/shard_map/gather_y/ppermute | solution.py:174
  36.3 1.9 %collective-permute-start.4 = (bf16[1536,128]{1,0:T(8,128)(2,1)S(1)}, bf16[1536,128]{1,0:T(8,128)(2,1)S(1)}, u32[]{:S(2)}, u32[]{:S(2)}) collective-permute-start(bf16[1536,128]{1,0:T(8,128)(2,1)S(1)} %bitcast.30), channel_id=1, source_target_pairs={{0,8},{8,16},{16,24},{24,32},{32,40},{40,48},{48,56},{56,0},{1,9},... | collective-permute-start | bytes 1179656 | tf_op jit(solution)/shard_map/gather_y/ppermute | solution.py:178
  38.2 2.8 %collective-permute-done = bf16[1536,128]{1,0:T(8,128)(2,1)S(1)} collective-permute-done((bf16[1536,128]{1,0:T(8,128)(2,1)S(1)}, bf16[1536,128]{1,0:T(8,128)(2,1)S(1)}, u32[]{:S(2)}, u32[]{:S(2)}) %collective-permute-start) | collective-permute-done | bytes 393248 | tf_op jit(solution)/shard_map/gather_y/ppermute | solution.py:174
  41.0 5.0 %collective-permute-start.1 = (bf16[1536,128]{1,0:T(8,128)(2,1)S(1)}, bf16[1536,128]{1,0:T(8,128)(2,1)S(1)}, u32[]{:S(2)}, u32[]{:S(2)}) collective-permute-start(bf16[1536,128]{1,0:T(8,128)(2,1)S(1)} %collective-permute-done), channel_id=1, source_target_pairs={{0,56},{8,0},{16,8},{24,16},{32,24},{40,32},{48,40},{56,48},{1,57}... | collective-permute-start | bytes 1179656 | tf_op jit(solution)/shard_map/gather_y/ppermute | solution.py:174
  46.0 0.0 collective-permute-done.4
  46.0 1.9 %collective-permute-start.5 = (bf16[1536,128]{1,0:T(8,128)(2,1)S(1)}, bf16[1536,128]{1,0:T(8,128)(2,1)S(1)}, u32[]{:S(2)}, u32[]{:S(2)}) collective-permute-start(bf16[1536,128]{1,0:T(8,128)(2,1)S(1)} %collective-permute-done.4), channel_id=1, source_target_pairs={{0,8},{8,16},{16,24},{24,32},{32,40},{40,48},{48,56},{56,0},{1,9},... | collective-permute-start | bytes 1179656 | tf_op jit(solution)/shard_map/gather_y/ppermute | solution.py:178
  47.9 3.3 %collective-permute-done.1 = bf16[1536,128]{1,0:T(8,128)(2,1)S(1)} collective-permute-done((bf16[1536,128]{1,0:T(8,128)(2,1)S(1)}, bf16[1536,128]{1,0:T(8,128)(2,1)S(1)}, u32[]{:S(2)}, u32[]{:S(2)}) %collective-permute-start.1) | collective-permute-done | bytes 393248 | tf_op jit(solution)/shard_map/gather_y/ppermute | solution.py:174
  51.2 5.0 %collective-permute-start.2 = (bf16[1536,128]{1,0:T(8,128)(2,1)S(1)}, bf16[1536,128]{1,0:T(8,128)(2,1)S(1)}, u32[]{:S(2)}, u32[]{:S(2)}) collective-permute-start(bf16[1536,128]{1,0:T(8,128)(2,1)S(1)} %collective-permute-done.1), channel_id=1, source_target_pairs={{0,56},{8,0},{16,8},{24,16},{32,24},{40,32},{48,40},{56,48},{1,57}... | collective-permute-start | bytes 1179656 | tf_op jit(solution)/shard_map/gather_y/ppermute | solution.py:174
  56.2 0.0 copy-start.1
  56.2 0.0 copy-start.2
  56.3 0.0 copy-start.3
  56.3 0.3 fusion.5.gram_ref
  56.6 0.0 copy-start.5
  56.6 0.0 copy-start.4
  56.6 0.3 copy-done.1
  57.0 0.0 copy-done.2
  57.0 0.0 copy-done.3
  57.0 0.3 copy-done.5
  57.3 0.0 copy-done.4
  57.3 0.7 small_exchange.1
  58.0 13.9 %all-to-all-start = ((f32[8,72,128]{2,1,0:T(8,128)}), f32[8,72,128]{2,1,0:T(8,128)S(1)}, u32[]{:S(2)}, u32[]{:S(2)}) async-start(f32[8,72,128]{2,1,0:T(8,128)} %small_exchange.1), calls=%async_computation | async-start | bytes 589824 | tf_op jit(solution)/shard_map/small_exchange/all_to_all | solution.py:223
  71.9 6.9 %all-to-all-done.pack_ref = f32[8,72,128]{2,1,0:T(8,128)S(1)} async-done(((f32[8,72,128]{2,1,0:T(8,128)}), f32[8,72,128]{2,1,0:T(8,128)S(1)}, u32[]{:S(2)}, u32[]{:S(2)}) %all-to-all-start) | async-done | bytes 294944 | tf_op jit(solution)/shard_map/small_exchange/all_to_all | solution.py:223
  78.9 0.0 collective-permute-done.5
  78.9 1.9 %collective-permute-start.6 = (bf16[1536,128]{1,0:T(8,128)(2,1)S(1)}, bf16[1536,128]{1,0:T(8,128)(2,1)S(1)}, u32[]{:S(2)}, u32[]{:S(2)}) collective-permute-start(bf16[1536,128]{1,0:T(8,128)(2,1)S(1)} %collective-permute-done.5), channel_id=1, source_target_pairs={{0,8},{8,16},{16,24},{24,32},{32,40},{40,48},{48,56},{56,0},{1,9},... | collective-permute-start | bytes 1179656 | tf_op jit(solution)/shard_map/gather_y/ppermute | solution.py:178
  80.8 0.0 collective-permute-done.2
  80.8 4.6 %collective-permute-start.3 = (bf16[1536,128]{1,0:T(8,128)(2,1)S(1)}, bf16[1536,128]{1,0:T(8,128)(2,1)}, u32[]{:S(2)}, u32[]{:S(2)}) collective-permute-start(bf16[1536,128]{1,0:T(8,128)(2,1)S(1)} %collective-permute-done.2), channel_id=1, source_target_pairs={{0,56},{8,0},{16,8},{24,16},{32,24},{40,32},{48,40},{56,48},{1,57}... | collective-permute-start | bytes 1179656 | tf_op jit(solution)/shard_map/gather_y/ppermute | solution.py:174
  85.4 0.1 reshape.52.live_ref
  85.5 0.1 reshape.50
  85.6 0.6 broadcast_in_dim.6
  86.2 3.8 %all-to-all-start.1 = ((f32[8,16,128]{2,1,0:T(8,128)}), f32[8,16,128]{2,1,0:T(8,128)S(1)}, u32[]{:S(2)}, u32[]{:S(2)}) async-start(f32[8,16,128]{2,1,0:T(8,128)} %broadcast_in_dim.6), calls=%async_computation.1 | async-start | bytes 131072 | tf_op jit(solution)/shard_map/gramian/all_to_all | solution.py:170
  90.0 1.4 %place.1.place_ref = s32[320,128]{1,0:T(8,128)S(1)} custom-call(s32[1]{0:T(128)} %bitcast.8.part_ref, s32[64]{0:T(128)S(1)} %get-tuple-element.9.seen_ref, s32[64]{0:T(128)S(1)} %reshape.52.live_ref, f32[8,72,128]{2,1,0:T(8,128)S(1)} %all-to-all-done.pack_ref), custom_call_target="tpu_custom_call" | custom-call | flops 1000000 | bytes 400000 | tf_op jit(solution)/shard_map/place/pallas_call | solution.py:240
  91.4 5.8 %all-to-all-done.1 = f32[8,16,128]{2,1,0:T(8,128)S(1)} async-done(((f32[8,16,128]{2,1,0:T(8,128)}), f32[8,16,128]{2,1,0:T(8,128)S(1)}, u32[]{:S(2)}, u32[]{:S(2)}) %all-to-all-start.1) | async-done | bytes 65568 | tf_op jit(solution)/shard_map/gramian/all_to_all | solution.py:170
  97.3 0.0 collective-permute-done.6
  97.3 0.0 collective-permute-done.3
  97.3 4.4 %select.15 = bf16[8,352,128]{2,1,0:T(8,128)(2,1)} custom-call(s32[64]{0:T(128)S(1)} %get-tuple-element.11.turn_ref, s32[64]{0:T(128)S(1)} %get-tuple-element.10.block_ref, s32[320,128]{1,0:T(8,128)S(1)} %place.1.place_ref, f32[16,128]{1,0:T(8,128)S(1)} %reduce_sum.19.gram_ref, bf16[12,128,128]{2,1,0:T(8,128)(2,1)S(1)} %bitcast.31, ...), custom_call_target="tpu_custom_call" | custom-call | flops 700000000 | bytes 4000000 | tf_op jit(solution)/shard_map/select/pallas_call | solution.py:254
  101.7 5.8 %all-to-all-start.2 = ((bf16[8,352,128]{2,1,0:T(8,128)(2,1)}), bf16[8,352,128]{2,1,0:T(8,128)(2,1)S(1)}, u32[]{:S(2)}, u32[]{:S(2)}) async-start(bf16[8,352,128]{2,1,0:T(8,128)(2,1)} %select.15), calls=%async_computation.2 | async-start | bytes 1441792 | tf_op jit(solution)/shard_map/exchange/all_to_all | solution.py:262
  107.5 0.0 copy-done
  107.5 0.1 convert_element_type.22.live_ref
  107.6 1.4 %weights.1.weight_ref = bf16[1280,128]{1,0:T(8,128)(2,1)S(1)} custom-call(s32[1]{0:T(128)} %bitcast.17.core_ref, s32[32]{0:T(128)S(1)} %convert_element_type.22.live_ref, f32[8,72,128]{2,1,0:T(8,128)S(1)} %all-to-all-done.pack_ref), custom_call_target="tpu_custom_call" | custom-call | flops 1000000 | bytes 400000 | tf_op jit(solution)/shard_map/weights/pallas_call | solution.py:247
  109.0 10.0 %all-to-all-done.2.recv_ref = bf16[8,352,128]{2,1,0:T(8,128)(2,1)S(1)} async-done(((bf16[8,352,128]{2,1,0:T(8,128)(2,1)}), bf16[8,352,128]{2,1,0:T(8,128)(2,1)S(1)}, u32[]{:S(2)}, u32[]{:S(2)}) %all-to-all-start.2) | async-done | bytes 720928 | tf_op jit(solution)/shard_map/exchange/all_to_all | solution.py:262
  119.0 3.2 %solve.1 = f32[128,128]{1,0:T(8,128)S(1)} custom-call(bf16[8,352,128]{2,1,0:T(8,128)(2,1)S(1)} %all-to-all-done.2.recv_ref, bf16[1280,128]{1,0:T(8,128)(2,1)S(1)} %weights.1.weight_ref, f32[128,128]{1,0:T(8,128)S(1)} %constant_dynamic-slice_fusion.start_ref), custom_call_target="tpu_custom_call" | custom-call | flops 800000000 | bytes 1200000 | tf_op jit(solution)/shard_map/solve/pallas_call | solution.py:265
  122.2 8.0 %all_to_all.20 = f32[4,128,128]{2,1,0:T(8,128)S(1)} all-to-all(f32[4,128,128]{2,1,0:T(8,128)S(1)} %broadcast_in_dim.7), channel_id=1, replica_groups=mesh['z'=12,'y'=8,'core'=2,'x'=4] {'x'}, dimensions={0} | all-to-all | bytes 524288 | tf_op jit(solution)/shard_map/gather_x/all_to_all | solution.py:170
  130.2 0.7 copy.15
  (9 shorter events, 0.1 us)
Async XLA Ops:
  0.0 107.5 %copy-start = (f32[512,128]{1,0:T(8,128)S(1)}, f32[512,128]{1,0:T(8,128)}, u32[]{:S(2)}) copy-start(f32[512,128]{1,0:T(8,128)} %param.13) | copy-start | bytes 786436
  31.2 9.8 %collective-permute-start = (bf16[1536,128]{1,0:T(8,128)(2,1)S(1)}, bf16[1536,128]{1,0:T(8,128)(2,1)S(1)}, u32[]{:S(2)}, u32[]{:S(2)}) collective-permute-start(bf16[1536,128]{1,0:T(8,128)(2,1)S(1)} %bitcast.29), channel_id=1, source_target_pairs={{0,56},{8,0},{16,8},{24,16},{32,24},{40,32},{48,40},{56,48},{1,57}... | collective-permute-start | bytes 1179656 | tf_op jit(solution)/shard_map/gather_y/ppermute | solution.py:174
  36.3 9.7 %collective-permute-start.4 = (bf16[1536,128]{1,0:T(8,128)(2,1)S(1)}, bf16[1536,128]{1,0:T(8,128)(2,1)S(1)}, u32[]{:S(2)}, u32[]{:S(2)}) collective-permute-start(bf16[1536,128]{1,0:T(8,128)(2,1)S(1)} %bitcast.30), channel_id=1, source_target_pairs={{0,8},{8,16},{16,24},{24,32},{32,40},{40,48},{48,56},{56,0},{1,9},... | collective-permute-start | bytes 1179656 | tf_op jit(solution)/shard_map/gather_y/ppermute | solution.py:178
  41.0 10.2 %collective-permute-start.1 = (bf16[1536,128]{1,0:T(8,128)(2,1)S(1)}, bf16[1536,128]{1,0:T(8,128)(2,1)S(1)}, u32[]{:S(2)}, u32[]{:S(2)}) collective-permute-start(bf16[1536,128]{1,0:T(8,128)(2,1)S(1)} %collective-permute-done), channel_id=1, source_target_pairs={{0,56},{8,0},{16,8},{24,16},{32,24},{40,32},{48,40},{56,48},{1,57}... | collective-permute-start | bytes 1179656 | tf_op jit(solution)/shard_map/gather_y/ppermute | solution.py:174
  46.0 32.9 %collective-permute-start.5 = (bf16[1536,128]{1,0:T(8,128)(2,1)S(1)}, bf16[1536,128]{1,0:T(8,128)(2,1)S(1)}, u32[]{:S(2)}, u32[]{:S(2)}) collective-permute-start(bf16[1536,128]{1,0:T(8,128)(2,1)S(1)} %collective-permute-done.4), channel_id=1, source_target_pairs={{0,8},{8,16},{16,24},{24,32},{32,40},{40,48},{48,56},{56,0},{1,9},... | collective-permute-start | bytes 1179656 | tf_op jit(solution)/shard_map/gather_y/ppermute | solution.py:178
  51.2 29.6 %collective-permute-start.2 = (bf16[1536,128]{1,0:T(8,128)(2,1)S(1)}, bf16[1536,128]{1,0:T(8,128)(2,1)S(1)}, u32[]{:S(2)}, u32[]{:S(2)}) collective-permute-start(bf16[1536,128]{1,0:T(8,128)(2,1)S(1)} %collective-permute-done.1), channel_id=1, source_target_pairs={{0,56},{8,0},{16,8},{24,16},{32,24},{40,32},{48,40},{56,48},{1,57}... | collective-permute-start | bytes 1179656 | tf_op jit(solution)/shard_map/gather_y/ppermute | solution.py:174
  56.2 0.7 copy-start.1
  56.2 0.7 copy-start.2
  56.3 0.7 copy-start.3
  56.6 0.7 copy-start.5
  56.6 0.7 copy-start.4
  58.0 20.8 %all-to-all-start = ((f32[8,72,128]{2,1,0:T(8,128)}), f32[8,72,128]{2,1,0:T(8,128)S(1)}, u32[]{:S(2)}, u32[]{:S(2)}) async-start(f32[8,72,128]{2,1,0:T(8,128)} %small_exchange.1), calls=%async_computation | async-start | bytes 589824 | tf_op jit(solution)/shard_map/small_exchange/all_to_all | solution.py:223
  78.9 18.4 %collective-permute-start.6 = (bf16[1536,128]{1,0:T(8,128)(2,1)S(1)}, bf16[1536,128]{1,0:T(8,128)(2,1)S(1)}, u32[]{:S(2)}, u32[]{:S(2)}) collective-permute-start(bf16[1536,128]{1,0:T(8,128)(2,1)S(1)} %collective-permute-done.5), channel_id=1, source_target_pairs={{0,8},{8,16},{16,24},{24,32},{32,40},{40,48},{48,56},{56,0},{1,9},... | collective-permute-start | bytes 1179656 | tf_op jit(solution)/shard_map/gather_y/ppermute | solution.py:178
  80.8 16.5 %collective-permute-start.3 = (bf16[1536,128]{1,0:T(8,128)(2,1)S(1)}, bf16[1536,128]{1,0:T(8,128)(2,1)}, u32[]{:S(2)}, u32[]{:S(2)}) collective-permute-start(bf16[1536,128]{1,0:T(8,128)(2,1)S(1)} %collective-permute-done.2), channel_id=1, source_target_pairs={{0,56},{8,0},{16,8},{24,16},{32,24},{40,32},{48,40},{56,48},{1,57}... | collective-permute-start | bytes 1179656 | tf_op jit(solution)/shard_map/gather_y/ppermute | solution.py:174
  86.2 11.0 %all-to-all-start.1 = ((f32[8,16,128]{2,1,0:T(8,128)}), f32[8,16,128]{2,1,0:T(8,128)S(1)}, u32[]{:S(2)}, u32[]{:S(2)}) async-start(f32[8,16,128]{2,1,0:T(8,128)} %broadcast_in_dim.6), calls=%async_computation.1 | async-start | bytes 131072 | tf_op jit(solution)/shard_map/gramian/all_to_all | solution.py:170
  101.7 17.3 %all-to-all-start.2 = ((bf16[8,352,128]{2,1,0:T(8,128)(2,1)}), bf16[8,352,128]{2,1,0:T(8,128)(2,1)S(1)}, u32[]{:S(2)}, u32[]{:S(2)}) async-start(bf16[8,352,128]{2,1,0:T(8,128)(2,1)} %select.15), calls=%async_computation.2 | async-start | bytes 1441792 | tf_op jit(solution)/shard_map/exchange/all_to_all | solution.py:262

commit v5 on v4

--- a/solution.py
+++ b/solution.py
@@ -58,6 +58,18 @@
         out_ref[d, ITEM_AT : ITEM_AT + GROUPS * PAIRS, :NNZ] = items
         out_ref[d, BLOCK_AT : BLOCK_AT + GROUPS, :PAIRS] = block_ref[...].astype(f32)
         out_ref[d, LIVE_AT : LIVE_AT + GROUPS, :PAIRS] = live_ref[...].astype(f32)
+
+
+def unpack_kernel(core_ref, part_ref, pack_ref, after_ref, gram_ref, own_ref, live_ref):
+    gram = pack_ref[0, :GRAM, :]
+    for d in range(1, C * X):
+        gram = gram + pack_ref[d, :GRAM, :]
+    gram_ref[...] = jnp.broadcast_to(gram[None], gram_ref.shape)
+    for c in range(C):
+        own_ref[c] = pack_ref[c * X + part_ref[0], BLOCK_AT:PACK, :].astype(jnp.int32)
+    for s in range(X):
+        row = pack_ref[core_ref[0] * X + s, pl.ds(LIVE_AT + part_ref[0], 1), :]
+        live_ref[s : s + 1, :] = row.astype(jnp.int32)
 
 
 def weight_kernel(core_ref, live_ref, pack_ref, out_ref, rows_ref):
@@ -95,19 +107,30 @@
     out_ref[...] = merged
 
 
-def select_kernel(turn_ref, block_ref, place_ref, gram_ref, *refs):
+def collect_kernel(turn_ref, block_ref, *refs):
     piece_refs, out_ref = refs[:-1], refs[-1]
-    gram_hi, gram_lo = split(gram_ref[...])
+    turns = [t for t in range(Y) if t != Y // 2]
+    for q in range(C * GROUPS * PAIRS):
+        turn, spot = turn_ref[q], block_ref[q]
+        block = piece_refs[0][spot]
+        for t, piece_ref in zip(turns[1:], piece_refs[1:]):
+            block = jnp.where(turn == t, piece_ref[spot], block)
+        out_ref[q] = block
+
+
+def select_kernel(turn_ref, block_ref, place_ref, gram_ref, held_ref, last_ref, out_ref):
+    gram = gram_ref[0]
+    for d in range(1, Y):
+        gram = gram + gram_ref[d]
+    gram_hi, gram_lo = split(gram)
     lane = lax.broadcasted_iota(jnp.int32, (LIVE, PAIRS * BLK), 1)
     for d in range(C * GROUPS):
         blocks = []
         for p in range(PAIRS):
             q = d * PAIRS + p
-            turn, spot = turn_ref[q], block_ref[q]
-            block = piece_refs[0][spot]
-            for t in range(1, Y):
-                block = jnp.where(turn == t, piece_refs[t][spot], block)
-            blocks.append(block)
+            blocks.append(
+                jnp.where(turn_ref[q] == Y // 2, last_ref[block_ref[q]], held_ref[q])
+            )
         onehot = jnp.where(place_ref[:, d : d + 1] == lane, 1.0, 0.0).astype(bf16)
         rows = dot(onehot, jnp.concatenate(blocks, axis=0))
         out_ref[d, :LIVE, :] = rows.astype(bf16)
@@ -183,7 +206,7 @@
         kernel,
         out_shape=out,
         in_specs=ins,
-        out_specs=vmem(),
+        out_specs=[vmem() for _ in out] if isinstance(out, tuple) else vmem(),
         scratch_shapes=list(scratch),
         compiler_params=pltpu.CompilerParams(vmem_limit_bytes=24 * 1024 * 1024),
         cost_estimate=pl.CostEstimate(flops=flops, bytes_accessed=nbytes, transcendentals=0),
@@ -219,22 +242,26 @@
             item_rows[:, 0],
             counts[:, 0],
         )
-        pack, _ = lax.optimization_barrier((pack, ups[1]))
         pack = lax.all_to_all(pack, ("core", "x"), 0, 0, tiled=True)
+        gram, own, user_live = call(
+            unpack_kernel,
+            (
+                jax.ShapeDtypeStruct((Y, GRAM, E), f32),
+                jax.ShapeDtypeStruct((C, PACK - BLOCK_AT, BLK), jnp.int32),
+                jax.ShapeDtypeStruct((X, BLK), jnp.int32),
+            ),
+            [smem()] * 2 + [vmem(), pl.BlockSpec(memory_space=pl.ANY)],
+        )(core.reshape(1), part.reshape(1), pack, downs[-2])
     with jax.named_scope("gramian"):
-        gram = jnp.sum(spread(jnp.sum(pack[:, :GRAM], axis=0), "y", Y), axis=0)
+        gram = lax.all_to_all(gram, "y", 0, 0, tiled=True)
 
     with jax.named_scope("indices"):
-        grid = pack.reshape(C, X, PACK, BLK)
-        own = lax.dynamic_slice(grid, (0, part, BLOCK_AT, 0), (C, 1, 2 * GROUPS, PAIRS))
-        own = own.reshape(C, 2 * GROUPS, PAIRS).astype(jnp.int32)
+        own, user_live = own[:, :, :PAIRS], user_live[:, :PAIRS].reshape(-1)
         ids, live = own[:, :GROUPS].reshape(-1), own[:, GROUPS:].reshape(-1)
         z_of, y_of, c_of = ids // (Y * C), ids // C % Y, ids % C
         turns = (y_of - lax.axis_index("y")) % Y
         spots = jnp.clip(z_of, 0, Z - 1)
         seen = jnp.where(c_of == core, live, 0)
-        user_live = lax.dynamic_slice(grid, (core, 0, LIVE_AT + part, 0), (1, X, 1, PAIRS))
-        user_live = user_live.reshape(-1).astype(jnp.int32)
 
     with jax.named_scope("place"):
         place = call(
@@ -250,14 +277,22 @@
             [smem()] * 2 + [vmem()],
             [pltpu.VMEM((X, LIVE + NNZ, BLK), f32)],
         )(core.reshape(1), user_live, pack)
+    with jax.named_scope("collect"):
+        last = pieces.pop(Y // 2)
+        held = call(
+            collect_kernel,
+            jax.ShapeDtypeStruct((C * GROUPS * PAIRS, BLK, E), bf16),
+            [smem()] * 2 + [vmem()] * len(pieces),
+            nbytes=4_000_000,
+        )(turns, spots, *pieces)
     with jax.named_scope("select"):
         chosen = call(
             select_kernel,
             jax.ShapeDtypeStruct((C * GROUPS, LIVE + 2 * GRAM, E), bf16),
-            [smem()] * 2 + [vmem()] * (2 + len(pieces)),
+            [smem()] * 2 + [vmem()] * 4,
             flops=700_000_000,
             nbytes=4_000_000,
-        )(turns, spots, place, gram, *pieces)
+        )(turns, spots, place, gram, held, last)
     with jax.named_scope("exchange"):
         received = lax.all_to_all(chosen, ("core", "x"), 0, 0, tiled=True)
     with jax.named_scope("solve"):

time: 132 us -> 132 us (level)
  the two profiles are of different devices: /device:TPU:1 before, /device:TPU:8 now
where the time goes in v5:
time: 132 us; the launch traced here: 131 us
  blocking collectives  44 us (33%)
  starting transfers between devices  35.1 us (27%)
  waiting for transfers between devices  26.3 us (20%)
  Pallas kernels  13.5 us (10%)
  local copies, waits for them, and re-layouts  10.8 us (8%)
    all_gather x1, blocking collectives, local(): column = lax.all_gather(own_block, 'z', axis=0, tiled=True)  34.4 us
    ppermute x4, starting transfers between devices, from_next(): return lax.ppermute(value, 'y', [(i, (i - 1) % Y) for i in range(Y)])  12.5 us
    ppermute x4, waiting for transfers between devices, from_next(): return lax.ppermute(value, 'y', [(i, (i - 1) % Y) for i in range(Y)])  11.7 us
    unnamed x33, local copies, waits for them, and re-layouts  10.5 us
    all_to_all x1, waiting for transfers between devices, local(): received = lax.all_to_all(chosen, ('core', 'x'), 0, 0, tiled=True)  10.3 us
    ppermute x3, starting transfers between devices, from_last(): return lax.ppermute(value, 'y', [(i, (i + 1) % Y) for i in range(Y)])  10.2 us
    all_to_all x1, blocking collectives, spread(): lax.all_to_all(jnp.broadcast_to(value[None], (size,) + value.shape), axis...  9.65 us
    all_to_all x1, starting transfers between devices, local(): gram = lax.all_to_all(gram, 'y', 0, 0, tiled=True)  4.65 us
  transfers between devices with their start and end apart: 10, of which 5 were waited for; matrix products, arithmetic and copies ran while one was open for 0% of the time, Pallas kernels for 5%

profile of v5, /device:TPU:8, one launch (start us, length us, event | category | flops | bytes accessed | tf_op | source)
XLA Modules:
  0.0 131.1 jit_solution(13786146180723446558)
XLA Ops:
  0.0 0.0 copy-start
  0.0 0.9 convert_element_type.6
  0.9 34.4 %all-gather = bf16[1,1536,128]{2,1,0:T(8,128)(2,1)S(1)} all-gather(bf16[1,128,128]{2,1,0:T(8,128)(2,1)S(1)} %convert_element_type.6), channel_id=2, replica_groups=mesh['z'=12,'y'=8,'core'=2,'x'=4] {'z'}, dimensions={1}, use_global_device_ids=true | all-gather | bytes 425984 | tf_op jit(solution)/shard_map/gather_z/all_gather | solution.py:221
  35.2 2.3 %collective-permute-start.2 = (bf16[1536,128]{1,0:T(8,128)(2,1)S(1)}, bf16[1536,128]{1,0:T(8,128)(2,1)S(1)}, u32[]{:S(2)}, u32[]{:S(2)}) collective-permute-start(bf16[1536,128]{1,0:T(8,128)(2,1)S(1)} %bitcast.20), channel_id=1, source_target_pairs={{0,56},{8,0},{16,8},{24,16},{32,24},{40,32},{48,40},{56,48},{1,57}... | collective-permute-start | bytes 1179656 | tf_op jit(solution)/shard_map/gather_y/ppermute | solution.py:197
  37.6 3.5 %collective-permute-start = (bf16[1536,128]{1,0:T(8,128)(2,1)S(1)}, bf16[1536,128]{1,0:T(8,128)(2,1)S(1)}, u32[]{:S(2)}, u32[]{:S(2)}) collective-permute-start(bf16[1536,128]{1,0:T(8,128)(2,1)S(1)} %bitcast.21), channel_id=1, source_target_pairs={{0,8},{8,16},{16,24},{24,32},{32,40},{40,48},{48,56},{56,0},{1,9},... | collective-permute-start | bytes 1179656 | tf_op jit(solution)/shard_map/gather_y/ppermute | solution.py:201
  41.1 5.5 %collective-permute-done.2 = bf16[1536,128]{1,0:T(8,128)(2,1)S(1)} collective-permute-done((bf16[1536,128]{1,0:T(8,128)(2,1)S(1)}, bf16[1536,128]{1,0:T(8,128)(2,1)S(1)}, u32[]{:S(2)}, u32[]{:S(2)}) %collective-permute-start.2) | collective-permute-done | bytes 393248 | tf_op jit(solution)/shard_map/gather_y/ppermute | solution.py:197
  46.6 2.1 %collective-permute-start.3 = (bf16[1536,128]{1,0:T(8,128)(2,1)S(1)}, bf16[1536,128]{1,0:T(8,128)(2,1)S(1)}, u32[]{:S(2)}, u32[]{:S(2)}) collective-permute-start(bf16[1536,128]{1,0:T(8,128)(2,1)S(1)} %collective-permute-done.2), channel_id=1, source_target_pairs={{0,56},{8,0},{16,8},{24,16},{32,24},{40,32},{48,40},{56,48},{1,57}... | collective-permute-start | bytes 1179656 | tf_op jit(solution)/shard_map/gather_y/ppermute | solution.py:197
  48.7 0.5 collective-permute-done
  49.2 0.0 copy-start.5
  49.2 3.3 %collective-permute-start.1 = (bf16[1536,128]{1,0:T(8,128)(2,1)S(1)}, bf16[1536,128]{1,0:T(8,128)(2,1)S(1)}, u32[]{:S(2)}, u32[]{:S(2)}) collective-permute-start(bf16[1536,128]{1,0:T(8,128)(2,1)S(1)} %collective-permute-done), channel_id=1, source_target_pairs={{0,8},{8,16},{16,24},{24,32},{32,40},{40,48},{48,56},{56,0},{1,9},... | collective-permute-start | bytes 1179656 | tf_op jit(solution)/shard_map/gather_y/ppermute | solution.py:201
  52.4 6.2 %collective-permute-done.3 = bf16[1536,128]{1,0:T(8,128)(2,1)S(1)} collective-permute-done((bf16[1536,128]{1,0:T(8,128)(2,1)S(1)}, bf16[1536,128]{1,0:T(8,128)(2,1)S(1)}, u32[]{:S(2)}, u32[]{:S(2)}) %collective-permute-start.3) | collective-permute-done | bytes 393248 | tf_op jit(solution)/shard_map/gather_y/ppermute | solution.py:197
  58.7 0.0 copy-start.7
  58.7 2.4 %collective-permute-start.4 = (bf16[1536,128]{1,0:T(8,128)(2,1)S(1)}, bf16[1536,128]{1,0:T(8,128)(2,1)}, u32[]{:S(2)}, u32[]{:S(2)}) collective-permute-start(bf16[1536,128]{1,0:T(8,128)(2,1)S(1)} %collective-permute-done.3), channel_id=1, source_target_pairs={{0,56},{8,0},{16,8},{24,16},{32,24},{40,32},{48,40},{56,48},{1,57}... | collective-permute-start | bytes 1179656 | tf_op jit(solution)/shard_map/gather_y/ppermute | solution.py:197
  61.1 0.3 fusion.4.gram_ref
  61.4 0.0 copy-start.11
  61.4 0.7 copy-done.11
  62.1 0.0 copy-start.12
  62.1 0.7 copy-done.12
  62.8 0.0 copy-start.13
  62.8 0.7 copy-done.13
  63.6 0.0 copy-start.14
  63.6 0.7 copy-done.14
  64.2 0.0 copy-start.15
  64.2 0.7 copy-done.15
  64.9 0.8 small_exchange.2
  65.7 4.3 %all-to-all-start = ((f32[8,72,128]{2,1,0:T(8,128)}), f32[8,72,128]{2,1,0:T(8,128)S(1)}, u32[]{:S(2)}, u32[]{:S(2)}) async-start(f32[8,72,128]{2,1,0:T(8,128)} %small_exchange.2), calls=%async_computation | async-start | bytes 589824 | tf_op jit(solution)/shard_map/small_exchange/all_to_all | solution.py:245
  70.0 0.0 collective-permute-done.1.after_ref
  70.0 3.4 %collective-permute-start.5 = (bf16[1536,128]{1,0:T(8,128)(2,1)S(1)}, bf16[1536,128]{1,0:T(8,128)(2,1)S(1)}, u32[]{:S(2)}, u32[]{:S(2)}) collective-permute-start(bf16[1536,128]{1,0:T(8,128)(2,1)S(1)} %collective-permute-done.1.after_ref), channel_id=1, source_target_pairs={{0,8},{8,16},{16,24},{24,32},{32,40},{40,48},{48,56},{56,0},{1,9},... | collective-permute-start | bytes 1179656 | tf_op jit(solution)/shard_map/gather_y/ppermute | solution.py:201
  73.4 3.8 %all-to-all-done.pack_ref = f32[8,72,128]{2,1,0:T(8,128)S(1)} async-done(((f32[8,72,128]{2,1,0:T(8,128)}), f32[8,72,128]{2,1,0:T(8,128)S(1)}, u32[]{:S(2)}, u32[]{:S(2)}) %all-to-all-start) | async-done | bytes 294944 | tf_op jit(solution)/shard_map/small_exchange/all_to_all | solution.py:245
  77.3 0.6 small_exchange.3
  77.9 0.0 collective-permute-done.4
  77.9 5.6 %collective-permute-start.6 = (bf16[1536,128]{1,0:T(8,128)(2,1)}, bf16[1536,128]{1,0:T(8,128)(2,1)}, u32[]{:S(2)}, u32[]{:S(2)}) collective-permute-start(bf16[1536,128]{1,0:T(8,128)(2,1)} %collective-permute-done.4), channel_id=1, source_target_pairs={{0,56},{8,0},{16,8},{24,16},{32,24},{40,32},{48,40},{56,48},{1,57}... | collective-permute-start | bytes 1179656 | tf_op jit(solution)/shard_map/gather_y/ppermute | solution.py:197
  83.5 0.1 reshape.49.live_ref
  83.6 0.1 reshape.48
  83.7 4.6 %all-to-all-start.1 = ((f32[8,16,128]{2,1,0:T(8,128)}), f32[8,16,128]{2,1,0:T(8,128)S(1)}, u32[]{:S(2)}, u32[]{:S(2)}) async-start(f32[8,16,128]{2,1,0:T(8,128)} %get-tuple-element.9), calls=%async_computation.1 | async-start | bytes 131072 | tf_op jit(solution)/shard_map/gramian/all_to_all | solution.py:256
  88.4 1.4 %place.1.place_ref = s32[320,128]{1,0:T(8,128)S(1)} custom-call(s32[1]{0:T(128)} %bitcast.1.part_ref, s32[64]{0:T(128)S(1)} %get-tuple-element.13.seen_ref, s32[64]{0:T(128)S(1)} %reshape.49.live_ref, f32[8,72,128]{2,1,0:T(8,128)S(1)} %all-to-all-done.pack_ref), custom_call_target="tpu_custom_call" | custom-call | flops 1000000 | bytes 400000 | tf_op jit(solution)/shard_map/place/pallas_call | solution.py:267
  89.8 0.0 copy-start.1
  89.8 0.7 copy-done.1
  90.4 0.0 collective-permute-done.5
  90.4 0.0 copy-start.9
  90.4 0.7 copy-done.9
  91.2 0.0 copy-done.3
  91.2 0.0 copy-done.5
  91.2 0.0 copy-done.7
  91.2 0.0 copy-start.4
  91.2 1.0 copy-done.4
  92.2 0.0 copy-start.6
  92.2 1.0 copy-done.6
  93.2 1.0 copy-done.8
  94.2 1.0 copy-done.10
  95.2 2.7 %collect.1.held_ref = bf16[64,128,128]{2,1,0:T(8,128)(2,1)S(1)} custom-call(s32[64]{0:T(128)S(1)} %get-tuple-element.15.turn_ref, s32[64]{0:T(128)S(1)} %get-tuple-element.14.block_ref, bf16[12,128,128]{2,1,0:T(8,128)(2,1)S(1)} %bitcast.22, bf16[12,128,128]{2,1,0:T(8,128)(2,1)S(1)} %bitcast.24, bf16[12,128,128]{2,1,0:T(8,128)(2,1)S(1)} %bitcast.26, ...), custom_call_target="tpu_custom_call" | custom-call | flops 1000000 | bytes 4000000 | tf_op jit(solution)/shard_map/collect/pallas_call | solution.py:282
  97.8 0.0 all-to-all-done.1.gram_ref
  97.9 0.0 collective-permute-done.6
  97.9 0.0 copy-start.2
  97.9 0.9 copy-done.2
  98.8 3.5 %select.15 = bf16[8,352,128]{2,1,0:T(8,128)(2,1)} custom-call(s32[64]{0:T(128)S(1)} %get-tuple-element.15.turn_ref, s32[64]{0:T(128)S(1)} %get-tuple-element.14.block_ref, s32[320,128]{1,0:T(8,128)S(1)} %copy-done.2, f32[8,16,128]{2,1,0:T(8,128)S(1)} %all-to-all-done.1.gram_ref, bf16[64,128,128]{2,1,0:T(8,128)(2,1)S(1)} %collect.1.held_ref, ...), custom_call_target="tpu_custom_call" | custom-call | flops 700000000 | bytes 4000000 | tf_op jit(solution)/shard_map/select/pallas_call | solution.py:289
  102.2 3.5 %all-to-all-start.2 = ((bf16[8,352,128]{2,1,0:T(8,128)(2,1)}), bf16[8,352,128]{2,1,0:T(8,128)(2,1)S(1)}, u32[]{:S(2)}, u32[]{:S(2)}) async-start(bf16[8,352,128]{2,1,0:T(8,128)(2,1)} %select.15), calls=%async_computation.2 | async-start | bytes 1441792 | tf_op jit(solution)/shard_map/exchange/all_to_all | solution.py:297
  105.8 0.0 copy-done
  105.8 0.1 reshape.58.live_ref
  105.9 1.4 %weights.1.weight_ref = bf16[1280,128]{1,0:T(8,128)(2,1)S(1)} custom-call(s32[1]{0:T(128)} %bitcast.core_ref, s32[32]{0:T(128)S(1)} %reshape.58.live_ref, f32[8,72,128]{2,1,0:T(8,128)S(1)} %all-to-all-done.pack_ref), custom_call_target="tpu_custom_call" | custom-call | flops 1000000 | bytes 400000 | tf_op jit(solution)/shard_map/weights/pallas_call | solution.py:274
  107.3 10.3 %all-to-all-done.2.recv_ref = bf16[8,352,128]{2,1,0:T(8,128)(2,1)S(1)} async-done(((bf16[8,352,128]{2,1,0:T(8,128)(2,1)}), bf16[8,352,128]{2,1,0:T(8,128)(2,1)S(1)}, u32[]{:S(2)}, u32[]{:S(2)}) %all-to-all-start.2) | async-done | bytes 720928 | tf_op jit(solution)/shard_map/exchange/all_to_all | solution.py:297
  117.6 3.2 %solve.1 = f32[128,128]{1,0:T(8,128)S(1)} custom-call(bf16[8,352,128]{2,1,0:T(8,128)(2,1)S(1)} %all-to-all-done.2.recv_ref, bf16[1280,128]{1,0:T(8,128)(2,1)S(1)} %weights.1.weight_ref, f32[128,128]{1,0:T(8,128)S(1)} %constant_dynamic-slice_fusion.start_ref), custom_call_target="tpu_custom_call" | custom-call | flops 800000000 | bytes 1200000 | tf_op jit(solution)/shard_map/solve/pallas_call | solution.py:300
  120.8 9.6 %all_to_all.20 = f32[4,128,128]{2,1,0:T(8,128)S(1)} all-to-all(f32[4,128,128]{2,1,0:T(8,128)S(1)} %broadcast_in_dim.4), channel_id=1, replica_groups=mesh['z'=12,'y'=8,'core'=2,'x'=4] {'x'}, dimensions={0} | all-to-all | bytes 524288 | tf_op jit(solution)/shard_map/gather_x/all_to_all | solution.py:193
  130.4 0.7 copy.9
  (7 shorter events, 0.1 us)
Async XLA Ops:
  0.0 105.8 %copy-start = (f32[512,128]{1,0:T(8,128)S(1)}, f32[512,128]{1,0:T(8,128)}, u32[]{:S(2)}) copy-start(f32[512,128]{1,0:T(8,128)} %param.13) | copy-start | bytes 786436
  35.2 11.3 %collective-permute-start.2 = (bf16[1536,128]{1,0:T(8,128)(2,1)S(1)}, bf16[1536,128]{1,0:T(8,128)(2,1)S(1)}, u32[]{:S(2)}, u32[]{:S(2)}) collective-permute-start(bf16[1536,128]{1,0:T(8,128)(2,1)S(1)} %bitcast.20), channel_id=1, source_target_pairs={{0,56},{8,0},{16,8},{24,16},{32,24},{40,32},{48,40},{56,48},{1,57}... | collective-permute-start | bytes 1179656 | tf_op jit(solution)/shard_map/gather_y/ppermute | solution.py:197
  37.6 11.6 %collective-permute-start = (bf16[1536,128]{1,0:T(8,128)(2,1)S(1)}, bf16[1536,128]{1,0:T(8,128)(2,1)S(1)}, u32[]{:S(2)}, u32[]{:S(2)}) collective-permute-start(bf16[1536,128]{1,0:T(8,128)(2,1)S(1)} %bitcast.21), channel_id=1, source_target_pairs={{0,8},{8,16},{16,24},{24,32},{32,40},{40,48},{48,56},{56,0},{1,9},... | collective-permute-start | bytes 1179656 | tf_op jit(solution)/shard_map/gather_y/ppermute | solution.py:201
  46.6 44.6 %copy-start.3 = (bf16[1536,128]{1,0:T(8,128)(2,1)}, bf16[1536,128]{1,0:T(8,128)(2,1)S(1)}, u32[]{:S(2)}) copy-start(bf16[1536,128]{1,0:T(8,128)(2,1)S(1)} %collective-permute-done.2) | copy-start | bytes 1179652
  46.6 12.1 %collective-permute-start.3 = (bf16[1536,128]{1,0:T(8,128)(2,1)S(1)}, bf16[1536,128]{1,0:T(8,128)(2,1)S(1)}, u32[]{:S(2)}, u32[]{:S(2)}) collective-permute-start(bf16[1536,128]{1,0:T(8,128)(2,1)S(1)} %collective-permute-done.2), channel_id=1, source_target_pairs={{0,56},{8,0},{16,8},{24,16},{32,24},{40,32},{48,40},{56,48},{1,57}... | collective-permute-start | bytes 1179656 | tf_op jit(solution)/shard_map/gather_y/ppermute | solution.py:197
  49.2 42.0 %copy-start.5 = (bf16[1536,128]{1,0:T(8,128)(2,1)}, bf16[1536,128]{1,0:T(8,128)(2,1)S(1)}, u32[]{:S(2)}) copy-start(bf16[1536,128]{1,0:T(8,128)(2,1)S(1)} %collective-permute-done) | copy-start | bytes 1179652
  49.2 20.9 %collective-permute-start.1 = (bf16[1536,128]{1,0:T(8,128)(2,1)S(1)}, bf16[1536,128]{1,0:T(8,128)(2,1)S(1)}, u32[]{:S(2)}, u32[]{:S(2)}) collective-permute-start(bf16[1536,128]{1,0:T(8,128)(2,1)S(1)} %collective-permute-done), channel_id=1, source_target_pairs={{0,8},{8,16},{16,24},{24,32},{32,40},{40,48},{48,56},{56,0},{1,9},... | collective-permute-start | bytes 1179656 | tf_op jit(solution)/shard_map/gather_y/ppermute | solution.py:201
  58.7 32.5 %copy-start.7 = (bf16[1536,128]{1,0:T(8,128)(2,1)}, bf16[1536,128]{1,0:T(8,128)(2,1)S(1)}, u32[]{:S(2)}) copy-start(bf16[1536,128]{1,0:T(8,128)(2,1)S(1)} %collective-permute-done.3) | copy-start | bytes 1179652
  58.7 19.2 %collective-permute-start.4 = (bf16[1536,128]{1,0:T(8,128)(2,1)S(1)}, bf16[1536,128]{1,0:T(8,128)(2,1)}, u32[]{:S(2)}, u32[]{:S(2)}) collective-permute-start(bf16[1536,128]{1,0:T(8,128)(2,1)S(1)} %collective-permute-done.3), channel_id=1, source_target_pairs={{0,56},{8,0},{16,8},{24,16},{32,24},{40,32},{48,40},{56,48},{1,57}... | collective-permute-start | bytes 1179656 | tf_op jit(solution)/shard_map/gather_y/ppermute | solution.py:197
  61.4 0.7 copy-start.11
  62.1 0.7 copy-start.12
  62.8 0.7 copy-start.13
  63.6 0.7 copy-start.14
  64.2 0.7 copy-start.15
  65.7 11.6 %all-to-all-start = ((f32[8,72,128]{2,1,0:T(8,128)}), f32[8,72,128]{2,1,0:T(8,128)S(1)}, u32[]{:S(2)}, u32[]{:S(2)}) async-start(f32[8,72,128]{2,1,0:T(8,128)} %small_exchange.2), calls=%async_computation | async-start | bytes 589824 | tf_op jit(solution)/shard_map/small_exchange/all_to_all | solution.py:245
  70.0 20.4 %collective-permute-start.5 = (bf16[1536,128]{1,0:T(8,128)(2,1)S(1)}, bf16[1536,128]{1,0:T(8,128)(2,1)S(1)}, u32[]{:S(2)}, u32[]{:S(2)}) collective-permute-start(bf16[1536,128]{1,0:T(8,128)(2,1)S(1)} %collective-permute-done.1.after_ref), channel_id=1, source_target_pairs={{0,8},{8,16},{16,24},{24,32},{32,40},{40,48},{48,56},{56,0},{1,9},... | collective-permute-start | bytes 1179656 | tf_op jit(solution)/shard_map/gather_y/ppermute | solution.py:201
  77.9 19.9 %collective-permute-start.6 = (bf16[1536,128]{1,0:T(8,128)(2,1)}, bf16[1536,128]{1,0:T(8,128)(2,1)}, u32[]{:S(2)}, u32[]{:S(2)}) collective-permute-start(bf16[1536,128]{1,0:T(8,128)(2,1)} %collective-permute-done.4), channel_id=1, source_target_pairs={{0,56},{8,0},{16,8},{24,16},{32,24},{40,32},{48,40},{56,48},{1,57}... | collective-permute-start | bytes 1179656 | tf_op jit(solution)/shard_map/gather_y/ppermute | solution.py:197
  83.7 14.2 %all-to-all-start.1 = ((f32[8,16,128]{2,1,0:T(8,128)}), f32[8,16,128]{2,1,0:T(8,128)S(1)}, u32[]{:S(2)}, u32[]{:S(2)}) async-start(f32[8,16,128]{2,1,0:T(8,128)} %get-tuple-element.9), calls=%async_computation.1 | async-start | bytes 131072 | tf_op jit(solution)/shard_map/gramian/all_to_all | solution.py:256
  89.8 0.7 copy-start.1
  90.4 0.7 copy-start.9
  91.2 1.0 copy-start.4
  92.2 1.0 copy-start.6
  93.2 1.0 copy-start.8
  94.2 1.0 copy-start.10
  97.9 0.9 copy-start.2
  102.2 15.3 %all-to-all-start.2 = ((bf16[8,352,128]{2,1,0:T(8,128)(2,1)}), bf16[8,352,128]{2,1,0:T(8,128)(2,1)S(1)}, u32[]{:S(2)}, u32[]{:S(2)}) async-start(bf16[8,352,128]{2,1,0:T(8,128)(2,1)} %select.15), calls=%async_computation.2 | async-start | bytes 1441792 | tf_op jit(solution)/shard_map/exchange/all_to_all | solution.py:297

commit v6 on v5

--- a/solution.py
+++ b/solution.py
@@ -15,7 +15,8 @@
 LIVE = 320
 ITERS = 3
 GROUPS = 4
-GRAM = E // (C * X)
+HALF = E // 2
+GRAM = HALF + HALF // 2
 
 conf_rate = 0.5
 ridge_weight = 0.5
@@ -40,31 +41,40 @@
     return out
 
 
-USER_AT = GRAM
-COUNT_AT = USER_AT + PAIRS
+COUNT_AT = PAIRS
 ITEM_AT = COUNT_AT + PAIRS
 BLOCK_AT = ITEM_AT + GROUPS * PAIRS
 LIVE_AT = BLOCK_AT + GROUPS
 PACK = LIVE_AT + GROUPS
 
 
-def pack_kernel(gram_ref, block_ref, live_ref, user_ref, item_ref, count_ref, out_ref):
+def fetch(pairs, sems):
+    copies = [pltpu.make_async_copy(src, dst, sems.at[i]) for i, (src, dst) in enumerate(pairs)]
+    for copy in copies:
+        copy.start()
+    for copy in copies:
+        copy.wait()
+
+
+def square(rows):
+    return lax.dot_general(rows, rows, (((0,), (0,)), ((), ())), preferred_element_type=f32)
+
+
+def pack_kernel(block_hbm, live_hbm, user_hbm, item_hbm, count_hbm, out_ref, *scratch):
+    block_ref, live_ref, user_ref, item_ref, count_ref, sems = scratch
+    sources = (block_hbm, live_hbm, user_hbm, item_hbm, count_hbm)
+    fetch(list(zip(sources, scratch[:-1])), sems)
     out_ref[...] = jnp.zeros(out_ref.shape, f32)
     items = item_ref[...].reshape(GROUPS * PAIRS, NNZ).astype(f32)
     for d in range(C * X):
-        out_ref[d, :GRAM, :] = gram_ref[d * GRAM : (d + 1) * GRAM, :]
-        out_ref[d, USER_AT : USER_AT + PAIRS, :NNZ] = user_ref[d % X].astype(f32)
+        out_ref[d, :PAIRS, :NNZ] = user_ref[d % X].astype(f32)
         out_ref[d, COUNT_AT : COUNT_AT + PAIRS, :NNZ] = count_ref[d % X].astype(f32)
         out_ref[d, ITEM_AT : ITEM_AT + GROUPS * PAIRS, :NNZ] = items
         out_ref[d, BLOCK_AT : BLOCK_AT + GROUPS, :PAIRS] = block_ref[...].astype(f32)
         out_ref[d, LIVE_AT : LIVE_AT + GROUPS, :PAIRS] = live_ref[...].astype(f32)
 
 
-def unpack_kernel(core_ref, part_ref, pack_ref, after_ref, gram_ref, own_ref, live_ref):
-    gram = pack_ref[0, :GRAM, :]
-    for d in range(1, C * X):
-        gram = gram + pack_ref[d, :GRAM, :]
-    gram_ref[...] = jnp.broadcast_to(gram[None], gram_ref.shape)
+def unpack_kernel(core_ref, part_ref, pack_ref, after_ref, own_ref, live_ref):
     for c in range(C):
         own_ref[c] = pack_ref[c * X + part_ref[0], BLOCK_AT:PACK, :].astype(jnp.int32)
     for s in range(X):
@@ -74,7 +84,7 @@
 
 def weight_kernel(core_ref, live_ref, pack_ref, out_ref, rows_ref):
     packs = [pack_ref[core_ref[0] * X + s] for s in range(X)]
-    users = [pack[USER_AT : USER_AT + PAIRS] for pack in packs]
+    users = [pack[:PAIRS] for pack in packs]
     counts = [pack[COUNT_AT : COUNT_AT + PAIRS] for pack in packs]
     table = jnp.concatenate(users + counts, axis=0).T[:NNZ]
     lane = lax.broadcasted_iota(jnp.int32, (NNZ, BLK), 1).astype(f32)
@@ -108,20 +118,31 @@
 
 
 def collect_kernel(turn_ref, block_ref, *refs):
-    piece_refs, out_ref = refs[:-1], refs[-1]
-    turns = [t for t in range(Y) if t != Y // 2]
+    piece_refs, (out_ref, gram_ref, held, sems) = refs[:-4], refs[-4:]
+    fetch([(piece_ref, held.at[i]) for i, piece_ref in enumerate(piece_refs)], sems)
     for q in range(C * GROUPS * PAIRS):
-        turn, spot = turn_ref[q], block_ref[q]
-        block = piece_refs[0][spot]
-        for t, piece_ref in zip(turns[1:], piece_refs[1:]):
-            block = jnp.where(turn == t, piece_ref[spot], block)
-        out_ref[q] = block
-
-
-def select_kernel(turn_ref, block_ref, place_ref, gram_ref, held_ref, last_ref, out_ref):
-    gram = gram_ref[0]
-    for d in range(1, Y):
-        gram = gram + gram_ref[d]
+        turn = turn_ref[q]
+        place = jnp.minimum(jnp.where(turn > Y // 2, turn - 1, turn), Y - 2)
+        out_ref[q] = held[place, block_ref[q]]
+    gram = square(held[0].reshape(Z * BLK, E))
+    for i in range(1, Y - 1):
+        gram = gram + square(held[i].reshape(Z * BLK, E))
+    gram_ref[...] = gram
+
+
+def select_kernel(
+    turn_ref, block_ref, place_ref, gram_ref, held_ref, last_hbm, out_ref, last_ref, sems
+):
+    fetch([(last_hbm, last_ref)], sems)
+    gram = gram_ref[...] + square(last_ref[...].reshape(Z * BLK, E))
+    corner = gram[:HALF, HALF:]
+    gram = jnp.concatenate(
+        [
+            jnp.concatenate([gram[:HALF, :HALF], gram[HALF:, HALF:]], axis=1),
+            jnp.concatenate([corner[: HALF // 2], corner[HALF // 2 :]], axis=1),
+        ],
+        axis=0,
+    )
     gram_hi, gram_lo = split(gram)
     lane = lax.broadcasted_iota(jnp.int32, (LIVE, PAIRS * BLK), 1)
     for d in range(C * GROUPS):
@@ -145,7 +166,15 @@
     conf = weight.astype(f32) * conf_rate
     full = jnp.where(weight > 0, 1.0 + conf, 0.0).astype(bf16)
     gram = recv_ref[:, LIVE : LIVE + GRAM, :].astype(f32) + recv_ref[:, LIVE + GRAM :, :].astype(f32)
-    gram = gram.reshape(E, E)
+    gram = jnp.sum(gram, axis=0)
+    corner = jnp.concatenate([gram[HALF:, :HALF], gram[HALF:, HALF:]], axis=0)
+    gram = jnp.concatenate(
+        [
+            jnp.concatenate([gram[:HALF, :HALF], corner], axis=1),
+            jnp.concatenate([corner.T, gram[:HALF, HALF:]], axis=1),
+        ],
+        axis=0,
+    )
     eye = lax.broadcasted_iota(jnp.int32, (E, E), 0) == lax.broadcasted_iota(jnp.int32, (E, E), 1)
     base_hi, base_lo = split(
         gram * (E / (X * Z * Y * C * BLK)) + jnp.where(eye, ridge_weight, 0.0)
@@ -189,6 +218,10 @@
     return pl.BlockSpec(memory_space=pltpu.SMEM)
 
 
+def hbm():
+    return pl.BlockSpec(memory_space=pl.ANY)
+
+
 def spread(value, axis, size):
     return lax.all_to_all(jnp.broadcast_to(value[None], (size,) + value.shape), axis, 0, 0, tiled=True)
 
@@ -227,33 +260,30 @@
         ups.append(from_next(ups[-1]))
         pieces = [piece.reshape(Z, BLK, E) for piece in ups + downs[:0:-1]]
 
-    with jax.named_scope("gramian"):
-        gram = lax.dot_general(
-            column, column, (((0,), (0,)), ((), ())), preferred_element_type=f32
-        )
     with jax.named_scope("small_exchange"):
-        pack = call(
-            pack_kernel, jax.ShapeDtypeStruct((C * X, PACK, BLK), f32), [vmem()] * 6
-        )(
-            gram,
+        ints = (
             block_ids[:, 0],
             pair_live[:, 0],
             user_rows[:, 0],
             item_rows[:, 0],
             counts[:, 0],
         )
+        pack = call(
+            pack_kernel,
+            jax.ShapeDtypeStruct((C * X, PACK, BLK), f32),
+            [hbm()] * len(ints),
+            [pltpu.VMEM(value.shape, value.dtype) for value in ints]
+            + [pltpu.SemaphoreType.DMA((len(ints),))],
+        )(*ints)
         pack = lax.all_to_all(pack, ("core", "x"), 0, 0, tiled=True)
-        gram, own, user_live = call(
+        own, user_live = call(
             unpack_kernel,
             (
-                jax.ShapeDtypeStruct((Y, GRAM, E), f32),
                 jax.ShapeDtypeStruct((C, PACK - BLOCK_AT, BLK), jnp.int32),
                 jax.ShapeDtypeStruct((X, BLK), jnp.int32),
             ),
-            [smem()] * 2 + [vmem(), pl.BlockSpec(memory_space=pl.ANY)],
-        )(core.reshape(1), part.reshape(1), pack, downs[-2])
-    with jax.named_scope("gramian"):
-        gram = lax.all_to_all(gram, "y", 0, 0, tiled=True)
+            [smem()] * 2 + [vmem(), hbm()],
+        )(core.reshape(1), part.reshape(1), pack, ups[-2])
 
     with jax.named_scope("indices"):
         own, user_live = own[:, :, :PAIRS], user_live[:, :PAIRS].reshape(-1)
@@ -279,17 +309,25 @@
         )(core.reshape(1), user_live, pack)
     with jax.named_scope("collect"):
         last = pieces.pop(Y // 2)
-        held = call(
+        held, gram = call(
             collect_kernel,
-            jax.ShapeDtypeStruct((C * GROUPS * PAIRS, BLK, E), bf16),
-            [smem()] * 2 + [vmem()] * len(pieces),
+            (
+                jax.ShapeDtypeStruct((C * GROUPS * PAIRS, BLK, E), bf16),
+                jax.ShapeDtypeStruct((E, E), f32),
+            ),
+            [smem()] * 2 + [hbm()] * len(pieces),
+            [
+                pltpu.VMEM((Y - 1, Z, BLK, E), bf16),
+                pltpu.SemaphoreType.DMA((Y - 1,)),
+            ],
             nbytes=4_000_000,
         )(turns, spots, *pieces)
     with jax.named_scope("select"):
         chosen = call(
             select_kernel,
             jax.ShapeDtypeStruct((C * GROUPS, LIVE + 2 * GRAM, E), bf16),
-            [smem()] * 2 + [vmem()] * 4,
+            [smem()] * 2 + [vmem()] * 3 + [hbm()],
+            [pltpu.VMEM((Z, BLK, E), bf16), pltpu.SemaphoreType.DMA((1,))],
             flops=700_000_000,
             nbytes=4_000_000,
         )(turns, spots, place, gram, held, last)

time: 132 us -> 130 us (0.985)
  the two profiles are of different devices: /device:TPU:8 before, /device:TPU:1 now
where the time goes in v6:
time: 130 us; the launch traced here: 129 us
  starting transfers between devices  44.6 us (34%)
  blocking collectives  38.3 us (29%)
  waiting for transfers between devices  26.7 us (21%)
  Pallas kernels  13.9 us (11%)
  local copies, waits for them, and re-layouts  4.49 us (3%)
    all_gather x1, blocking collectives, local(): column = lax.all_gather(own_block, 'z', axis=0, tiled=True)  30.3 us
    ppermute x4, starting transfers between devices, from_next(): return lax.ppermute(value, 'y', [(i, (i - 1) % Y) for i in range(Y)])  19.7 us
    all_to_all x1, starting transfers between devices, local(): pack = lax.all_to_all(pack, ('core', 'x'), 0, 0, tiled=True)  13.9 us
    all_to_all x1, waiting for transfers between devices, local(): received = lax.all_to_all(chosen, ('core', 'x'), 0, 0, tiled=True)  13.5 us
    all_to_all x1, blocking collectives, spread(): lax.all_to_all(jnp.broadcast_to(value[None], (size,) + value.shape), axis...  7.99 us
    ppermute x3, waiting for transfers between devices, from_last(): return lax.ppermute(value, 'y', [(i, (i + 1) % Y) for i in range(Y)])  7.09 us
    ppermute x4, waiting for transfers between devices, from_next(): return lax.ppermute(value, 'y', [(i, (i - 1) % Y) for i in range(Y)])  6.06 us
    ppermute x3, starting transfers between devices, from_last(): return lax.ppermute(value, 'y', [(i, (i + 1) % Y) for i in range(Y)])  5.75 us
  transfers between devices with their start and end apart: 9, of which 4 were waited for; matrix products, arithmetic and copies ran while one was open for 0% of the time, Pallas kernels for 5%

profile of v6, /device:TPU:1, one launch (start us, length us, event | category | flops | bytes accessed | tf_op | source)
XLA Modules:
  0.0 129.1 jit_solution(8997623420310557352)
XLA Ops:
  0.0 0.0 copy-start
  0.0 0.9 convert_element_type.6
  0.9 30.3 %all-gather = bf16[1,1536,128]{2,1,0:T(8,128)(2,1)S(1)} all-gather(bf16[1,128,128]{2,1,0:T(8,128)(2,1)S(1)} %convert_element_type.6), channel_id=2, replica_groups=mesh['z'=12,'y'=8,'core'=2,'x'=4] {'z'}, dimensions={1}, use_global_device_ids=true | all-gather | bytes 425984 | tf_op jit(solution)/shard_map/gather_z/all_gather | solution.py:254
  31.2 5.1 %collective-permute-start = (bf16[1536,128]{1,0:T(8,128)(2,1)S(1)}, bf16[1536,128]{1,0:T(8,128)(2,1)S(1)}, u32[]{:S(2)}, u32[]{:S(2)}) collective-permute-start(bf16[1536,128]{1,0:T(8,128)(2,1)S(1)} %bitcast.18), channel_id=1, source_target_pairs={{0,56},{8,0},{16,8},{24,16},{32,24},{40,32},{48,40},{56,48},{1,57}... | collective-permute-start | bytes 1179656 | tf_op jit(solution)/shard_map/gather_y/ppermute | solution.py:230
  36.3 1.9 %collective-permute-start.3 = (bf16[1536,128]{1,0:T(8,128)(2,1)S(1)}, bf16[1536,128]{1,0:T(8,128)(2,1)S(1)}, u32[]{:S(2)}, u32[]{:S(2)}) collective-permute-start(bf16[1536,128]{1,0:T(8,128)(2,1)S(1)} %bitcast.19), channel_id=1, source_target_pairs={{0,8},{8,16},{16,24},{24,32},{32,40},{40,48},{48,56},{56,0},{1,9},... | collective-permute-start | bytes 1179656 | tf_op jit(solution)/shard_map/gather_y/ppermute | solution.py:234
  38.2 2.8 %collective-permute-done = bf16[1536,128]{1,0:T(8,128)(2,1)S(1)} collective-permute-done((bf16[1536,128]{1,0:T(8,128)(2,1)S(1)}, bf16[1536,128]{1,0:T(8,128)(2,1)S(1)}, u32[]{:S(2)}, u32[]{:S(2)}) %collective-permute-start) | collective-permute-done | bytes 393248 | tf_op jit(solution)/shard_map/gather_y/ppermute | solution.py:230
  41.0 5.0 %collective-permute-start.1 = (bf16[1536,128]{1,0:T(8,128)(2,1)S(1)}, bf16[1536,128]{1,0:T(8,128)(2,1)S(1)}, u32[]{:S(2)}, u32[]{:S(2)}) collective-permute-start(bf16[1536,128]{1,0:T(8,128)(2,1)S(1)} %collective-permute-done), channel_id=1, source_target_pairs={{0,56},{8,0},{16,8},{24,16},{32,24},{40,32},{48,40},{56,48},{1,57}... | collective-permute-start | bytes 1179656 | tf_op jit(solution)/shard_map/gather_y/ppermute | solution.py:230
  46.0 0.0 collective-permute-done.3
  46.0 1.9 %collective-permute-start.4 = (bf16[1536,128]{1,0:T(8,128)(2,1)S(1)}, bf16[1536,128]{1,0:T(8,128)(2,1)S(1)}, u32[]{:S(2)}, u32[]{:S(2)}) collective-permute-start(bf16[1536,128]{1,0:T(8,128)(2,1)S(1)} %collective-permute-done.3), channel_id=1, source_target_pairs={{0,8},{8,16},{16,24},{24,32},{32,40},{40,48},{48,56},{56,0},{1,9},... | collective-permute-start | bytes 1179656 | tf_op jit(solution)/shard_map/gather_y/ppermute | solution.py:234
  47.9 3.3 %collective-permute-done.1 = bf16[1536,128]{1,0:T(8,128)(2,1)S(1)} collective-permute-done((bf16[1536,128]{1,0:T(8,128)(2,1)S(1)}, bf16[1536,128]{1,0:T(8,128)(2,1)S(1)}, u32[]{:S(2)}, u32[]{:S(2)}) %collective-permute-start.1) | collective-permute-done | bytes 393248 | tf_op jit(solution)/shard_map/gather_y/ppermute | solution.py:230
  51.2 5.0 %collective-permute-start.2 = (bf16[1536,128]{1,0:T(8,128)(2,1)S(1)}, bf16[1536,128]{1,0:T(8,128)(2,1)S(1)}, u32[]{:S(2)}, u32[]{:S(2)}) collective-permute-start(bf16[1536,128]{1,0:T(8,128)(2,1)S(1)} %collective-permute-done.1), channel_id=1, source_target_pairs={{0,56},{8,0},{16,8},{24,16},{32,24},{40,32},{48,40},{56,48},{1,57}... | collective-permute-start | bytes 1179656 | tf_op jit(solution)/shard_map/gather_y/ppermute | solution.py:230
  56.2 0.0 copy-start.1
  56.2 0.7 copy-done.1
  57.0 0.0 copy-start.2
  57.0 0.7 copy-done.2
  57.7 0.0 copy-start.3
  57.7 0.7 copy-done.3
  58.4 0.0 copy-start.4
  58.4 0.7 copy-done.4
  59.1 0.0 copy-start.5
  59.1 0.7 copy-done.5
  59.8 0.8 small_exchange.2
  60.6 13.9 %all-to-all-start = ((f32[8,56,128]{2,1,0:T(8,128)}), f32[8,56,128]{2,1,0:T(8,128)S(1)}, u32[]{:S(2)}, u32[]{:S(2)}) async-start(f32[8,56,128]{2,1,0:T(8,128)} %small_exchange.2), calls=%async_computation | async-start | bytes 458752 | tf_op jit(solution)/shard_map/small_exchange/all_to_all | solution.py:278
  74.5 0.0 collective-permute-done.4
  74.5 1.9 %collective-permute-start.5 = (bf16[1536,128]{1,0:T(8,128)(2,1)S(1)}, bf16[1536,128]{1,0:T(8,128)(2,1)S(1)}, u32[]{:S(2)}, u32[]{:S(2)}) collective-permute-start(bf16[1536,128]{1,0:T(8,128)(2,1)S(1)} %collective-permute-done.4), channel_id=1, source_target_pairs={{0,8},{8,16},{16,24},{24,32},{32,40},{40,48},{48,56},{56,0},{1,9},... | collective-permute-start | bytes 1179656 | tf_op jit(solution)/shard_map/gather_y/ppermute | solution.py:234
  76.4 0.0 collective-permute-done.2.after_ref
  76.4 4.6 %collective-permute-start.6 = (bf16[1536,128]{1,0:T(8,128)(2,1)S(1)}, bf16[1536,128]{1,0:T(8,128)(2,1)}, u32[]{:S(2)}, u32[]{:S(2)}) collective-permute-start(bf16[1536,128]{1,0:T(8,128)(2,1)S(1)} %collective-permute-done.2.after_ref), channel_id=1, source_target_pairs={{0,56},{8,0},{16,8},{24,16},{32,24},{40,32},{48,40},{56,48},{1,57}... | collective-permute-start | bytes 1179656 | tf_op jit(solution)/shard_map/gather_y/ppermute | solution.py:230
  81.0 0.0 all-to-all-done.pack_ref
  81.1 0.1 reshape.49.live_ref
  81.1 0.1 reshape.48
  81.3 7.1 %collective-permute-done.5 = bf16[1536,128]{1,0:T(8,128)(2,1)S(1)} collective-permute-done((bf16[1536,128]{1,0:T(8,128)(2,1)S(1)}, bf16[1536,128]{1,0:T(8,128)(2,1)S(1)}, u32[]{:S(2)}, u32[]{:S(2)}) %collective-permute-start.5) | collective-permute-done | bytes 393248 | tf_op jit(solution)/shard_map/gather_y/ppermute | solution.py:234
  88.3 2.9 %collect.1 = (bf16[64,128,128]{2,1,0:T(8,128)(2,1)S(1)}, f32[128,128]{1,0:T(8,128)S(1)}) custom-call(s32[64]{0:T(128)S(1)} %get-tuple-element.17.turn_ref, s32[64]{0:T(128)S(1)} %get-tuple-element.16.block_ref, bf16[12,128,128]{2,1,0:T(8,128)(2,1)S(1)} %bitcast.20, bf16[12,128,128]{2,1,0:T(8,128)(2,1)S(1)} %bitcast.22, bf16[12,128,128]{2,1,0:T(8,128)(2,1)S(1)} %bitcast.24, ...), custom_call_target="tpu_custom_call" | custom-call | flops 1000000 | bytes 4000000 | tf_op jit(solution)/shard_map/collect/pallas_call | solution.py:312
  91.2 1.4 %place.1.place_ref = s32[320,128]{1,0:T(8,128)S(1)} custom-call(s32[1]{0:T(128)} %bitcast.1.part_ref, s32[64]{0:T(128)S(1)} %get-tuple-element.15.seen_ref, s32[64]{0:T(128)S(1)} %reshape.49.live_ref, f32[8,56,128]{2,1,0:T(8,128)S(1)} %all-to-all-done.pack_ref), custom_call_target="tpu_custom_call" | custom-call | flops 1000000 | bytes 400000 | tf_op jit(solution)/shard_map/place/pallas_call | solution.py:297
  92.6 0.0 collective-permute-done.6
  92.6 4.3 %select.15 = bf16[8,512,128]{2,1,0:T(8,128)(2,1)} custom-call(s32[64]{0:T(128)S(1)} %get-tuple-element.17.turn_ref, s32[64]{0:T(128)S(1)} %get-tuple-element.16.block_ref, s32[320,128]{1,0:T(8,128)S(1)} %place.1.place_ref, f32[128,128]{1,0:T(8,128)S(1)} %get-tuple-element.10.gram_ref, bf16[64,128,128]{2,1,0:T(8,128)(2,1)S(1)} %get-tuple-element.11.held_ref, ...), custom_call_target="tpu_custom_call" | custom-call | flops 700000000 | bytes 4000000 | tf_op jit(solution)/shard_map/select/pallas_call | solution.py:326
  96.9 5.2 %all-to-all-start.1 = ((bf16[8,512,128]{2,1,0:T(8,128)(2,1)}), bf16[8,512,128]{2,1,0:T(8,128)(2,1)S(1)}, u32[]{:S(2)}, u32[]{:S(2)}) async-start(bf16[8,512,128]{2,1,0:T(8,128)(2,1)} %select.15), calls=%async_computation.1 | async-start | bytes 2097152 | tf_op jit(solution)/shard_map/exchange/all_to_all | solution.py:335
  102.2 0.0 copy-done
  102.2 0.1 reshape.58.live_ref
  102.3 1.4 %weights.1.weight_ref = bf16[1280,128]{1,0:T(8,128)(2,1)S(1)} custom-call(s32[1]{0:T(128)} %bitcast.core_ref, s32[32]{0:T(128)S(1)} %reshape.58.live_ref, f32[8,56,128]{2,1,0:T(8,128)S(1)} %all-to-all-done.pack_ref), custom_call_target="tpu_custom_call" | custom-call | flops 1000000 | bytes 400000 | tf_op jit(solution)/shard_map/weights/pallas_call | solution.py:304
  103.6 13.5 %all-to-all-done.1.recv_ref = bf16[8,512,128]{2,1,0:T(8,128)(2,1)S(1)} async-done(((bf16[8,512,128]{2,1,0:T(8,128)(2,1)}), bf16[8,512,128]{2,1,0:T(8,128)(2,1)S(1)}, u32[]{:S(2)}, u32[]{:S(2)}) %all-to-all-start.1) | async-done | bytes 1048608 | tf_op jit(solution)/shard_map/exchange/all_to_all | solution.py:335
  117.2 3.2 %solve.1 = f32[128,128]{1,0:T(8,128)S(1)} custom-call(bf16[8,512,128]{2,1,0:T(8,128)(2,1)S(1)} %all-to-all-done.1.recv_ref, bf16[1280,128]{1,0:T(8,128)(2,1)S(1)} %weights.1.weight_ref, f32[128,128]{1,0:T(8,128)S(1)} %constant_dynamic-slice_fusion.start_ref), custom_call_target="tpu_custom_call" | custom-call | flops 800000000 | bytes 1200000 | tf_op jit(solution)/shard_map/solve/pallas_call | solution.py:338
  120.4 8.0 %all_to_all.15 = f32[4,128,128]{2,1,0:T(8,128)S(1)} all-to-all(f32[4,128,128]{2,1,0:T(8,128)S(1)} %broadcast_in_dim.4), channel_id=1, replica_groups=mesh['z'=12,'y'=8,'core'=2,'x'=4] {'x'}, dimensions={0} | all-to-all | bytes 524288 | tf_op jit(solution)/shard_map/gather_x/all_to_all | solution.py:226
  128.4 0.7 copy.9
  (5 shorter events, 0.1 us)
Async XLA Ops:
  0.0 102.2 %copy-start = (f32[512,128]{1,0:T(8,128)S(1)}, f32[512,128]{1,0:T(8,128)}, u32[]{:S(2)}) copy-start(f32[512,128]{1,0:T(8,128)} %param.13) | copy-start | bytes 786436
  31.2 9.8 %collective-permute-start = (bf16[1536,128]{1,0:T(8,128)(2,1)S(1)}, bf16[1536,128]{1,0:T(8,128)(2,1)S(1)}, u32[]{:S(2)}, u32[]{:S(2)}) collective-permute-start(bf16[1536,128]{1,0:T(8,128)(2,1)S(1)} %bitcast.18), channel_id=1, source_target_pairs={{0,56},{8,0},{16,8},{24,16},{32,24},{40,32},{48,40},{56,48},{1,57}... | collective-permute-start | bytes 1179656 | tf_op jit(solution)/shard_map/gather_y/ppermute | solution.py:230
  36.3 9.7 %collective-permute-start.3 = (bf16[1536,128]{1,0:T(8,128)(2,1)S(1)}, bf16[1536,128]{1,0:T(8,128)(2,1)S(1)}, u32[]{:S(2)}, u32[]{:S(2)}) collective-permute-start(bf16[1536,128]{1,0:T(8,128)(2,1)S(1)} %bitcast.19), channel_id=1, source_target_pairs={{0,8},{8,16},{16,24},{24,32},{32,40},{40,48},{48,56},{56,0},{1,9},... | collective-permute-start | bytes 1179656 | tf_op jit(solution)/shard_map/gather_y/ppermute | solution.py:234
  41.0 10.2 %collective-permute-start.1 = (bf16[1536,128]{1,0:T(8,128)(2,1)S(1)}, bf16[1536,128]{1,0:T(8,128)(2,1)S(1)}, u32[]{:S(2)}, u32[]{:S(2)}) collective-permute-start(bf16[1536,128]{1,0:T(8,128)(2,1)S(1)} %collective-permute-done), channel_id=1, source_target_pairs={{0,56},{8,0},{16,8},{24,16},{32,24},{40,32},{48,40},{56,48},{1,57}... | collective-permute-start | bytes 1179656 | tf_op jit(solution)/shard_map/gather_y/ppermute | solution.py:230
  46.0 28.5 %collective-permute-start.4 = (bf16[1536,128]{1,0:T(8,128)(2,1)S(1)}, bf16[1536,128]{1,0:T(8,128)(2,1)S(1)}, u32[]{:S(2)}, u32[]{:S(2)}) collective-permute-start(bf16[1536,128]{1,0:T(8,128)(2,1)S(1)} %collective-permute-done.3), channel_id=1, source_target_pairs={{0,8},{8,16},{16,24},{24,32},{32,40},{40,48},{48,56},{56,0},{1,9},... | collective-permute-start | bytes 1179656 | tf_op jit(solution)/shard_map/gather_y/ppermute | solution.py:234
  51.2 25.2 %collective-permute-start.2 = (bf16[1536,128]{1,0:T(8,128)(2,1)S(1)}, bf16[1536,128]{1,0:T(8,128)(2,1)S(1)}, u32[]{:S(2)}, u32[]{:S(2)}) collective-permute-start(bf16[1536,128]{1,0:T(8,128)(2,1)S(1)} %collective-permute-done.1), channel_id=1, source_target_pairs={{0,56},{8,0},{16,8},{24,16},{32,24},{40,32},{48,40},{56,48},{1,57}... | collective-permute-start | bytes 1179656 | tf_op jit(solution)/shard_map/gather_y/ppermute | solution.py:230
  56.2 0.7 copy-start.1
  57.0 0.7 copy-start.2
  57.7 0.7 copy-start.3
  58.4 0.7 copy-start.4
  59.1 0.7 copy-start.5
  60.6 20.4 %all-to-all-start = ((f32[8,56,128]{2,1,0:T(8,128)}), f32[8,56,128]{2,1,0:T(8,128)S(1)}, u32[]{:S(2)}, u32[]{:S(2)}) async-start(f32[8,56,128]{2,1,0:T(8,128)} %small_exchange.2), calls=%async_computation | async-start | bytes 458752 | tf_op jit(solution)/shard_map/small_exchange/all_to_all | solution.py:278
  74.5 13.8 %collective-permute-start.5 = (bf16[1536,128]{1,0:T(8,128)(2,1)S(1)}, bf16[1536,128]{1,0:T(8,128)(2,1)S(1)}, u32[]{:S(2)}, u32[]{:S(2)}) collective-permute-start(bf16[1536,128]{1,0:T(8,128)(2,1)S(1)} %collective-permute-done.4), channel_id=1, source_target_pairs={{0,8},{8,16},{16,24},{24,32},{32,40},{40,48},{48,56},{56,0},{1,9},... | collective-permute-start | bytes 1179656 | tf_op jit(solution)/shard_map/gather_y/ppermute | solution.py:234
  76.4 16.2 %collective-permute-start.6 = (bf16[1536,128]{1,0:T(8,128)(2,1)S(1)}, bf16[1536,128]{1,0:T(8,128)(2,1)}, u32[]{:S(2)}, u32[]{:S(2)}) collective-permute-start(bf16[1536,128]{1,0:T(8,128)(2,1)S(1)} %collective-permute-done.2.after_ref), channel_id=1, source_target_pairs={{0,56},{8,0},{16,8},{24,16},{32,24},{40,32},{48,40},{56,48},{1,57}... | collective-permute-start | bytes 1179656 | tf_op jit(solution)/shard_map/gather_y/ppermute | solution.py:230
  96.9 20.2 %all-to-all-start.1 = ((bf16[8,512,128]{2,1,0:T(8,128)(2,1)}), bf16[8,512,128]{2,1,0:T(8,128)(2,1)S(1)}, u32[]{:S(2)}, u32[]{:S(2)}) async-start(bf16[8,512,128]{2,1,0:T(8,128)(2,1)} %select.15), calls=%async_computation.1 | async-start | bytes 2097152 | tf_op jit(solution)/shard_map/exchange/all_to_all | solution.py:335

commit v7 on v6

--- a/solution.py
+++ b/solution.py
@@ -60,18 +60,13 @@
     return lax.dot_general(rows, rows, (((0,), (0,)), ((), ())), preferred_element_type=f32)
 
 
-def pack_kernel(block_hbm, live_hbm, user_hbm, item_hbm, count_hbm, out_ref, *scratch):
-    block_ref, live_ref, user_ref, item_ref, count_ref, sems = scratch
-    sources = (block_hbm, live_hbm, user_hbm, item_hbm, count_hbm)
-    fetch(list(zip(sources, scratch[:-1])), sems)
+def pack_kernel(slots_ref, blocks_ref, out_ref):
     out_ref[...] = jnp.zeros(out_ref.shape, f32)
-    items = item_ref[...].reshape(GROUPS * PAIRS, NNZ).astype(f32)
+    items = slots_ref[:, 2 * PAIRS :, :].reshape(GROUPS * PAIRS, NNZ)
     for d in range(C * X):
-        out_ref[d, :PAIRS, :NNZ] = user_ref[d % X].astype(f32)
-        out_ref[d, COUNT_AT : COUNT_AT + PAIRS, :NNZ] = count_ref[d % X].astype(f32)
+        out_ref[d, : 2 * PAIRS, :NNZ] = slots_ref[d % X, : 2 * PAIRS, :]
         out_ref[d, ITEM_AT : ITEM_AT + GROUPS * PAIRS, :NNZ] = items
-        out_ref[d, BLOCK_AT : BLOCK_AT + GROUPS, :PAIRS] = block_ref[...].astype(f32)
-        out_ref[d, LIVE_AT : LIVE_AT + GROUPS, :PAIRS] = live_ref[...].astype(f32)
+        out_ref[d, BLOCK_AT:, :PAIRS] = blocks_ref[...]
 
 
 def unpack_kernel(core_ref, part_ref, pack_ref, after_ref, own_ref, live_ref):
@@ -257,24 +252,15 @@
         for _ in range(Y // 2 - 1):
             ups.append(from_next(ups[-1]))
             downs.append(from_last(downs[-1]))
-        ups.append(from_next(ups[-1]))
+        downs.append(from_last(downs[-1]))
         pieces = [piece.reshape(Z, BLK, E) for piece in ups + downs[:0:-1]]
 
     with jax.named_scope("small_exchange"):
-        ints = (
-            block_ids[:, 0],
-            pair_live[:, 0],
-            user_rows[:, 0],
-            item_rows[:, 0],
-            counts[:, 0],
-        )
+        slots = jnp.concatenate([user_rows[:, 0], counts[:, 0], item_rows[:, 0]], axis=1)
+        blocks = jnp.concatenate([block_ids[:, 0], pair_live[:, 0]], axis=0)
         pack = call(
-            pack_kernel,
-            jax.ShapeDtypeStruct((C * X, PACK, BLK), f32),
-            [hbm()] * len(ints),
-            [pltpu.VMEM(value.shape, value.dtype) for value in ints]
-            + [pltpu.SemaphoreType.DMA((len(ints),))],
-        )(*ints)
+            pack_kernel, jax.ShapeDtypeStruct((C * X, PACK, BLK), f32), [vmem()] * 2
+        )(slots.astype(f32), blocks.astype(f32))
         pack = lax.all_to_all(pack, ("core", "x"), 0, 0, tiled=True)
         own, user_live = call(
             unpack_kernel,
@@ -283,7 +269,7 @@
                 jax.ShapeDtypeStruct((X, BLK), jnp.int32),
             ),
             [smem()] * 2 + [vmem(), hbm()],
-        )(core.reshape(1), part.reshape(1), pack, ups[-2])
+        )(core.reshape(1), part.reshape(1), pack, downs[-2])
 
     with jax.named_scope("indices"):
         own, user_live = own[:, :, :PAIRS], user_live[:, :PAIRS].reshape(-1)

time: 130 us -> 127 us (0.977)
  the two profiles are of different devices: /device:TPU:1 before, /device:TPU:24 now
where the time goes in v7:
time: 127 us
  blocking collectives  44 us (35%)
  starting transfers between devices  35.2 us (28%)
  waiting for transfers between devices  30.2 us (24%)
  Pallas kernels  13.8 us (11%)
  other arithmetic  2.39 us (2%)
    all_gather x1, blocking collectives, local(): column = lax.all_gather(own_block, 'z', axis=0, tiled=True)  34.4 us
    ppermute x4, starting transfers between devices, from_last(): return lax.ppermute(value, 'y', [(i, (i + 1) % Y) for i in range(Y)])  20.7 us
    all_to_all x1, waiting for transfers between devices, local(): received = lax.all_to_all(chosen, ('core', 'x'), 0, 0, tiled=True)  13.9 us
    all_to_all x1, blocking collectives, spread(): lax.all_to_all(jnp.broadcast_to(value[None], (size,) + value.shape), axis...  9.65 us
    ppermute x4, waiting for transfers between devices, from_last(): return lax.ppermute(value, 'y', [(i, (i + 1) % Y) for i in range(Y)])  8.72 us
    ppermute x3, waiting for transfers between devices, from_next(): return lax.ppermute(value, 'y', [(i, (i - 1) % Y) for i in range(Y)])  7.57 us
    ppermute x3, starting transfers between devices, from_next(): return lax.ppermute(value, 'y', [(i, (i - 1) % Y) for i in range(Y)])  5.75 us
    all_to_all x1, starting transfers between devices, local(): received = lax.all_to_all(chosen, ('core', 'x'), 0, 0, tiled=True)  4.46 us
  transfers between devices with their start and end apart: 9, of which 5 were waited for; matrix products, arithmetic and copies ran while one was open for 1% of the time, Pallas kernels for 5%

profile of v7, /device:TPU:24, one launch (start us, length us, event | category | flops | bytes accessed | tf_op | source)
XLA Modules:
  0.0 126.7 jit_solution(16951785024264944527)
XLA Ops:
  0.0 0.0 copy-start
  0.0 0.9 convert_element_type.14
  0.9 34.4 %all-gather = bf16[1,1536,128]{2,1,0:T(8,128)(2,1)S(1)} all-gather(bf16[1,128,128]{2,1,0:T(8,128)(2,1)S(1)} %convert_element_type.14), channel_id=2, replica_groups=mesh['z'=12,'y'=8,'core'=2,'x'=4] {'z'}, dimensions={1}, use_global_device_ids=true | all-gather | bytes 425984 | tf_op jit(solution)/shard_map/gather_z/all_gather | solution.py:249
  35.2 4.7 %collective-permute-start = (bf16[1536,128]{1,0:T(8,128)(2,1)S(1)}, bf16[1536,128]{1,0:T(8,128)(2,1)S(1)}, u32[]{:S(2)}, u32[]{:S(2)}) collective-permute-start(bf16[1536,128]{1,0:T(8,128)(2,1)S(1)} %bitcast.18), channel_id=1, source_target_pairs={{0,8},{8,16},{16,24},{24,32},{32,40},{40,48},{48,56},{56,0},{1,9},... | collective-permute-start | bytes 1179656 | tf_op jit(solution)/shard_map/gather_y/ppermute | solution.py:229
  39.9 1.9 %collective-permute-start.3 = (bf16[1536,128]{1,0:T(8,128)(2,1)S(1)}, bf16[1536,128]{1,0:T(8,128)(2,1)S(1)}, u32[]{:S(2)}, u32[]{:S(2)}) collective-permute-start(bf16[1536,128]{1,0:T(8,128)(2,1)S(1)} %bitcast.19), channel_id=1, source_target_pairs={{0,56},{8,0},{16,8},{24,16},{32,24},{40,32},{48,40},{56,48},{1,57}... | collective-permute-start | bytes 1179656 | tf_op jit(solution)/shard_map/gather_y/ppermute | solution.py:225
  41.9 4.1 %collective-permute-done = bf16[1536,128]{1,0:T(8,128)(2,1)S(1)} collective-permute-done((bf16[1536,128]{1,0:T(8,128)(2,1)S(1)}, bf16[1536,128]{1,0:T(8,128)(2,1)S(1)}, u32[]{:S(2)}, u32[]{:S(2)}) %collective-permute-start) | collective-permute-done | bytes 393248 | tf_op jit(solution)/shard_map/gather_y/ppermute | solution.py:229
  46.0 5.3 %collective-permute-start.1 = (bf16[1536,128]{1,0:T(8,128)(2,1)S(1)}, bf16[1536,128]{1,0:T(8,128)(2,1)S(1)}, u32[]{:S(2)}, u32[]{:S(2)}) collective-permute-start(bf16[1536,128]{1,0:T(8,128)(2,1)S(1)} %collective-permute-done), channel_id=1, source_target_pairs={{0,8},{8,16},{16,24},{24,32},{32,40},{40,48},{48,56},{56,0},{1,9},... | collective-permute-start | bytes 1179656 | tf_op jit(solution)/shard_map/gather_y/ppermute | solution.py:229
  51.3 0.3 collective-permute-done.3
  51.5 1.9 %collective-permute-start.4 = (bf16[1536,128]{1,0:T(8,128)(2,1)S(1)}, bf16[1536,128]{1,0:T(8,128)(2,1)S(1)}, u32[]{:S(2)}, u32[]{:S(2)}) collective-permute-start(bf16[1536,128]{1,0:T(8,128)(2,1)S(1)} %collective-permute-done.3), channel_id=1, source_target_pairs={{0,56},{8,0},{16,8},{24,16},{32,24},{40,32},{48,40},{56,48},{1,57}... | collective-permute-start | bytes 1179656 | tf_op jit(solution)/shard_map/gather_y/ppermute | solution.py:225
  53.5 4.6 %collective-permute-done.1 = bf16[1536,128]{1,0:T(8,128)(2,1)S(1)} collective-permute-done((bf16[1536,128]{1,0:T(8,128)(2,1)S(1)}, bf16[1536,128]{1,0:T(8,128)(2,1)S(1)}, u32[]{:S(2)}, u32[]{:S(2)}) %collective-permute-start.1) | collective-permute-done | bytes 393248 | tf_op jit(solution)/shard_map/gather_y/ppermute | solution.py:229
  58.1 5.6 %collective-permute-start.2 = (bf16[1536,128]{1,0:T(8,128)(2,1)S(1)}, bf16[1536,128]{1,0:T(8,128)(2,1)S(1)}, u32[]{:S(2)}, u32[]{:S(2)}) collective-permute-start(bf16[1536,128]{1,0:T(8,128)(2,1)S(1)} %collective-permute-done.1), channel_id=1, source_target_pairs={{0,8},{8,16},{16,24},{24,32},{32,40},{40,48},{48,56},{56,0},{1,9},... | collective-permute-start | bytes 1179656 | tf_op jit(solution)/shard_map/gather_y/ppermute | solution.py:229
  63.7 0.7 add_convert_fusion.1.blocks_ref
  64.4 0.8 add_convert_fusion.slots_ref
  65.1 0.7 small_exchange.2
  65.9 4.3 %all-to-all-start = ((f32[8,56,128]{2,1,0:T(8,128)}), f32[8,56,128]{2,1,0:T(8,128)S(1)}, u32[]{:S(2)}, u32[]{:S(2)}) async-start(f32[8,56,128]{2,1,0:T(8,128)} %small_exchange.2), calls=%async_computation | async-start | bytes 458752 | tf_op jit(solution)/shard_map/small_exchange/all_to_all | solution.py:264
  70.2 0.0 collective-permute-done.4
  70.2 1.9 %collective-permute-start.5 = (bf16[1536,128]{1,0:T(8,128)(2,1)S(1)}, bf16[1536,128]{1,0:T(8,128)(2,1)S(1)}, u32[]{:S(2)}, u32[]{:S(2)}) collective-permute-start(bf16[1536,128]{1,0:T(8,128)(2,1)S(1)} %collective-permute-done.4), channel_id=1, source_target_pairs={{0,56},{8,0},{16,8},{24,16},{32,24},{40,32},{48,40},{56,48},{1,57}... | collective-permute-start | bytes 1179656 | tf_op jit(solution)/shard_map/gather_y/ppermute | solution.py:225
  72.1 0.0 collective-permute-done.2.after_ref
  72.1 5.1 %collective-permute-start.6 = (bf16[1536,128]{1,0:T(8,128)(2,1)S(1)}, bf16[1536,128]{1,0:T(8,128)(2,1)}, u32[]{:S(2)}, u32[]{:S(2)}) collective-permute-start(bf16[1536,128]{1,0:T(8,128)(2,1)S(1)} %collective-permute-done.2.after_ref), channel_id=1, source_target_pairs={{0,8},{8,16},{16,24},{24,32},{32,40},{40,48},{48,56},{56,0},{1,9},... | collective-permute-start | bytes 1179656 | tf_op jit(solution)/shard_map/gather_y/ppermute | solution.py:229
  77.2 0.0 all-to-all-done.pack_ref
  77.3 0.1 reshape.49.live_ref
  77.4 0.1 reshape.48
  77.5 7.3 %collective-permute-done.5 = bf16[1536,128]{1,0:T(8,128)(2,1)S(1)} collective-permute-done((bf16[1536,128]{1,0:T(8,128)(2,1)S(1)}, bf16[1536,128]{1,0:T(8,128)(2,1)S(1)}, u32[]{:S(2)}, u32[]{:S(2)}) %collective-permute-start.5) | collective-permute-done | bytes 393248 | tf_op jit(solution)/shard_map/gather_y/ppermute | solution.py:225
  84.8 2.9 %collect.1 = (bf16[64,128,128]{2,1,0:T(8,128)(2,1)S(1)}, f32[128,128]{1,0:T(8,128)S(1)}) custom-call(s32[64]{0:T(128)S(1)} %get-tuple-element.17.turn_ref, s32[64]{0:T(128)S(1)} %get-tuple-element.16.block_ref, bf16[12,128,128]{2,1,0:T(8,128)(2,1)S(1)} %bitcast.20, bf16[12,128,128]{2,1,0:T(8,128)(2,1)S(1)} %bitcast.23, bf16[12,128,128]{2,1,0:T(8,128)(2,1)S(1)} %bitcast.25, ...), custom_call_target="tpu_custom_call" | custom-call | flops 1000000 | bytes 4000000 | tf_op jit(solution)/shard_map/collect/pallas_call | solution.py:298
  87.6 1.4 %place.1.place_ref = s32[320,128]{1,0:T(8,128)S(1)} custom-call(s32[1]{0:T(128)} %bitcast.1.part_ref, s32[64]{0:T(128)S(1)} %get-tuple-element.15.seen_ref, s32[64]{0:T(128)S(1)} %reshape.49.live_ref, f32[8,56,128]{2,1,0:T(8,128)S(1)} %all-to-all-done.pack_ref), custom_call_target="tpu_custom_call" | custom-call | flops 1000000 | bytes 400000 | tf_op jit(solution)/shard_map/place/pallas_call | solution.py:283
  89.0 0.0 collective-permute-done.6
  89.1 4.3 %select.15 = bf16[8,512,128]{2,1,0:T(8,128)(2,1)} custom-call(s32[64]{0:T(128)S(1)} %get-tuple-element.17.turn_ref, s32[64]{0:T(128)S(1)} %get-tuple-element.16.block_ref, s32[320,128]{1,0:T(8,128)S(1)} %place.1.place_ref, f32[128,128]{1,0:T(8,128)S(1)} %get-tuple-element.10.gram_ref, bf16[64,128,128]{2,1,0:T(8,128)(2,1)S(1)} %get-tuple-element.11.held_ref, ...), custom_call_target="tpu_custom_call" | custom-call | flops 700000000 | bytes 4000000 | tf_op jit(solution)/shard_map/select/pallas_call | solution.py:312
  93.4 4.5 %all-to-all-start.1 = ((bf16[8,512,128]{2,1,0:T(8,128)(2,1)}), bf16[8,512,128]{2,1,0:T(8,128)(2,1)S(1)}, u32[]{:S(2)}, u32[]{:S(2)}) async-start(bf16[8,512,128]{2,1,0:T(8,128)(2,1)} %select.15), calls=%async_computation.1 | async-start | bytes 2097152 | tf_op jit(solution)/shard_map/exchange/all_to_all | solution.py:321
  97.8 0.0 copy-done
  97.8 0.1 reshape.58.live_ref
  97.9 1.4 %weights.1.weight_ref = bf16[1280,128]{1,0:T(8,128)(2,1)S(1)} custom-call(s32[1]{0:T(128)} %bitcast.core_ref, s32[32]{0:T(128)S(1)} %reshape.58.live_ref, f32[8,56,128]{2,1,0:T(8,128)S(1)} %all-to-all-done.pack_ref), custom_call_target="tpu_custom_call" | custom-call | flops 1000000 | bytes 400000 | tf_op jit(solution)/shard_map/weights/pallas_call | solution.py:290
  99.3 13.9 %all-to-all-done.1.recv_ref = bf16[8,512,128]{2,1,0:T(8,128)(2,1)S(1)} async-done(((bf16[8,512,128]{2,1,0:T(8,128)(2,1)}), bf16[8,512,128]{2,1,0:T(8,128)(2,1)S(1)}, u32[]{:S(2)}, u32[]{:S(2)}) %all-to-all-start.1) | async-done | bytes 1048608 | tf_op jit(solution)/shard_map/exchange/all_to_all | solution.py:321
  113.2 3.2 %solve.1 = f32[128,128]{1,0:T(8,128)S(1)} custom-call(bf16[8,512,128]{2,1,0:T(8,128)(2,1)S(1)} %all-to-all-done.1.recv_ref, bf16[1280,128]{1,0:T(8,128)(2,1)S(1)} %weights.1.weight_ref, f32[128,128]{1,0:T(8,128)S(1)} %constant_dynamic-slice_fusion.start_ref), custom_call_target="tpu_custom_call" | custom-call | flops 800000000 | bytes 1200000 | tf_op jit(solution)/shard_map/solve/pallas_call | solution.py:324
  116.4 9.7 %all_to_all.15 = f32[4,128,128]{2,1,0:T(8,128)S(1)} all-to-all(f32[4,128,128]{2,1,0:T(8,128)S(1)} %broadcast_in_dim.4), channel_id=1, replica_groups=mesh['z'=12,'y'=8,'core'=2,'x'=4] {'x'}, dimensions={0} | all-to-all | bytes 524288 | tf_op jit(solution)/shard_map/gather_x/all_to_all | solution.py:221
  126.0 0.7 copy.9
  (5 shorter events, 0.1 us)
Async XLA Ops:
  0.0 97.8 %copy-start = (f32[512,128]{1,0:T(8,128)S(1)}, f32[512,128]{1,0:T(8,128)}, u32[]{:S(2)}) copy-start(f32[512,128]{1,0:T(8,128)} %param.13) | copy-start | bytes 786436
  35.2 10.7 %collective-permute-start = (bf16[1536,128]{1,0:T(8,128)(2,1)S(1)}, bf16[1536,128]{1,0:T(8,128)(2,1)S(1)}, u32[]{:S(2)}, u32[]{:S(2)}) collective-permute-start(bf16[1536,128]{1,0:T(8,128)(2,1)S(1)} %bitcast.18), channel_id=1, source_target_pairs={{0,8},{8,16},{16,24},{24,32},{32,40},{40,48},{48,56},{56,0},{1,9},... | collective-permute-start | bytes 1179656 | tf_op jit(solution)/shard_map/gather_y/ppermute | solution.py:229
  39.9 11.6 %collective-permute-start.3 = (bf16[1536,128]{1,0:T(8,128)(2,1)S(1)}, bf16[1536,128]{1,0:T(8,128)(2,1)S(1)}, u32[]{:S(2)}, u32[]{:S(2)}) collective-permute-start(bf16[1536,128]{1,0:T(8,128)(2,1)S(1)} %bitcast.19), channel_id=1, source_target_pairs={{0,56},{8,0},{16,8},{24,16},{32,24},{40,32},{48,40},{56,48},{1,57}... | collective-permute-start | bytes 1179656 | tf_op jit(solution)/shard_map/gather_y/ppermute | solution.py:225
  46.0 12.1 %collective-permute-start.1 = (bf16[1536,128]{1,0:T(8,128)(2,1)S(1)}, bf16[1536,128]{1,0:T(8,128)(2,1)S(1)}, u32[]{:S(2)}, u32[]{:S(2)}) collective-permute-start(bf16[1536,128]{1,0:T(8,128)(2,1)S(1)} %collective-permute-done), channel_id=1, source_target_pairs={{0,8},{8,16},{16,24},{24,32},{32,40},{40,48},{48,56},{56,0},{1,9},... | collective-permute-start | bytes 1179656 | tf_op jit(solution)/shard_map/gather_y/ppermute | solution.py:229
  51.5 18.6 %collective-permute-start.4 = (bf16[1536,128]{1,0:T(8,128)(2,1)S(1)}, bf16[1536,128]{1,0:T(8,128)(2,1)S(1)}, u32[]{:S(2)}, u32[]{:S(2)}) collective-permute-start(bf16[1536,128]{1,0:T(8,128)(2,1)S(1)} %collective-permute-done.3), channel_id=1, source_target_pairs={{0,56},{8,0},{16,8},{24,16},{32,24},{40,32},{48,40},{56,48},{1,57}... | collective-permute-start | bytes 1179656 | tf_op jit(solution)/shard_map/gather_y/ppermute | solution.py:225
  58.1 14.0 %collective-permute-start.2 = (bf16[1536,128]{1,0:T(8,128)(2,1)S(1)}, bf16[1536,128]{1,0:T(8,128)(2,1)S(1)}, u32[]{:S(2)}, u32[]{:S(2)}) collective-permute-start(bf16[1536,128]{1,0:T(8,128)(2,1)S(1)} %collective-permute-done.1), channel_id=1, source_target_pairs={{0,8},{8,16},{16,24},{24,32},{32,40},{40,48},{48,56},{56,0},{1,9},... | collective-permute-start | bytes 1179656 | tf_op jit(solution)/shard_map/gather_y/ppermute | solution.py:229
  65.9 11.4 %all-to-all-start = ((f32[8,56,128]{2,1,0:T(8,128)}), f32[8,56,128]{2,1,0:T(8,128)S(1)}, u32[]{:S(2)}, u32[]{:S(2)}) async-start(f32[8,56,128]{2,1,0:T(8,128)} %small_exchange.2), calls=%async_computation | async-start | bytes 458752 | tf_op jit(solution)/shard_map/small_exchange/all_to_all | solution.py:264
  70.2 14.6 %collective-permute-start.5 = (bf16[1536,128]{1,0:T(8,128)(2,1)S(1)}, bf16[1536,128]{1,0:T(8,128)(2,1)S(1)}, u32[]{:S(2)}, u32[]{:S(2)}) collective-permute-start(bf16[1536,128]{1,0:T(8,128)(2,1)S(1)} %collective-permute-done.4), channel_id=1, source_target_pairs={{0,56},{8,0},{16,8},{24,16},{32,24},{40,32},{48,40},{56,48},{1,57}... | collective-permute-start | bytes 1179656 | tf_op jit(solution)/shard_map/gather_y/ppermute | solution.py:225
  72.1 16.9 %collective-permute-start.6 = (bf16[1536,128]{1,0:T(8,128)(2,1)S(1)}, bf16[1536,128]{1,0:T(8,128)(2,1)}, u32[]{:S(2)}, u32[]{:S(2)}) collective-permute-start(bf16[1536,128]{1,0:T(8,128)(2,1)S(1)} %collective-permute-done.2.after_ref), channel_id=1, source_target_pairs={{0,8},{8,16},{16,24},{24,32},{32,40},{40,48},{48,56},{56,0},{1,9},... | collective-permute-start | bytes 1179656 | tf_op jit(solution)/shard_map/gather_y/ppermute | solution.py:229
  93.4 19.8 %all-to-all-start.1 = ((bf16[8,512,128]{2,1,0:T(8,128)(2,1)}), bf16[8,512,128]{2,1,0:T(8,128)(2,1)S(1)}, u32[]{:S(2)}, u32[]{:S(2)}) async-start(bf16[8,512,128]{2,1,0:T(8,128)(2,1)} %select.15), calls=%async_computation.1 | async-start | bytes 2097152 | tf_op jit(solution)/shard_map/exchange/all_to_all | solution.py:321

commit v8 on v7

--- a/solution.py
+++ b/solution.py
@@ -154,8 +154,21 @@
         out_ref[d, LIVE + GRAM :, :] = gram_lo
 
 
+def merge_kernel(halves_ref, out_ref):
+    gram = jnp.zeros((GRAM, E), f32)
+    for c in range(C):
+        for part in range(2):
+            at = LIVE + part * GRAM
+            gram = gram + halves_ref[c, 0, at : at + GRAM, :].astype(f32)
+    gram_hi, gram_lo = split(gram)
+    for g in range(GROUPS):
+        out_ref[g, :LIVE, :] = halves_ref[0, g, :LIVE, :] + halves_ref[1, g, :LIVE, :]
+        out_ref[g, LIVE : LIVE + GRAM, :] = gram_hi
+        out_ref[g, LIVE + GRAM :, :] = gram_lo
+
+
 def solve_kernel(recv_ref, weight_ref, start_ref, out_ref):
-    items = (recv_ref[:X, :LIVE, :] + recv_ref[X:, :LIVE, :]).reshape(X * LIVE, E)
+    items = recv_ref[:, :LIVE, :].reshape(X * LIVE, E)
     items_t = items.T
     weight = weight_ref[...]
     conf = weight.astype(f32) * conf_rate
@@ -202,7 +215,7 @@
             norm_next = jnp.sum(remain * remain, axis=0, keepdims=True)
             direction = remain + norm_next / norm_now * direction
             norm_now = norm_next
-    out_ref[...] = x.T
+    out_ref[...] = x.T.astype(out_ref.dtype)
 
 
 def vmem():
@@ -318,18 +331,22 @@
             nbytes=4_000_000,
         )(turns, spots, place, gram, held, last)
     with jax.named_scope("exchange"):
-        received = lax.all_to_all(chosen, ("core", "x"), 0, 0, tiled=True)
+        halves = lax.all_to_all(
+            chosen.reshape((C, GROUPS) + chosen.shape[1:]), "core", 0, 0, tiled=True
+        )
+        merged = call(merge_kernel, jax.ShapeDtypeStruct(halves.shape[1:], bf16), [vmem()])(halves)
+        received = lax.all_to_all(merged, "x", 0, 0, tiled=True)
     with jax.named_scope("solve"):
         start = lax.dynamic_slice_in_dim(user_emb, part * BLK, BLK, 0)
         solved = call(
             solve_kernel,
-            jax.ShapeDtypeStruct((BLK, E), f32),
+            jax.ShapeDtypeStruct((BLK, E), bf16),
             [vmem()] * 3,
             flops=800_000_000,
             nbytes=1_200_000,
         )(received, weight, start)
     with jax.named_scope("gather_x"):
-        return spread(solved, "x", X).reshape(X * BLK, E)
+        return spread(solved, "x", X).reshape(X * BLK, E).astype(f32)
 
 
 def solution(mesh):

time: 127 us -> 125 us (0.984)
  waiting for transfers between devices: 30.2 us -> 24.6 us
  blocking collectives: 44 us -> 47.3 us
    all_to_all x1, waiting for transfers between devices: 13.9 us -> 8.32 us  [local(): received = lax.all_to_all(merged, 'x', 0, 0, tiled=True)]
    all_to_all x0 -> x1, blocking collectives: none -> 4.58 us  [local(): lax.all_to_all(chosen.reshape((C, GROUPS) + chosen.shape[1:]), 'core', 0,...]
    all_to_all x1, blocking collectives: 9.65 us -> 8.36 us  [spread(): lax.all_to_all(jnp.broadcast_to(value[None], (size,) + value.shape), axis...]
    pallas_call x1 -> x2, Pallas kernels: 3.19 us -> 4.02 us  [the longest x1 3.16 us: local(): call(solve_kernel, jax.ShapeDtypeStruct((BLK, E), bf16), [vmem()] * 3, fl...]
where the time goes in v8:
time: 125 us; the launch traced here: 124 us
  blocking collectives  47.3 us (38%)
  starting transfers between devices  35.2 us (28%)
  waiting for transfers between devices  24.6 us (20%)
  Pallas kernels  13.7 us (11%)
  other arithmetic  3.12 us (2%)
    all_gather x1, blocking collectives, local(): column = lax.all_gather(own_block, 'z', axis=0, tiled=True)  34.4 us
    ppermute x4, starting transfers between devices, from_last(): return lax.ppermute(value, 'y', [(i, (i + 1) % Y) for i in range(Y)])  20.7 us
    ppermute x4, waiting for transfers between devices, from_last(): return lax.ppermute(value, 'y', [(i, (i + 1) % Y) for i in range(Y)])  8.72 us
    all_to_all x1, blocking collectives, spread(): lax.all_to_all(jnp.broadcast_to(value[None], (size,) + value.shape), axis...  8.36 us
    all_to_all x1, waiting for transfers between devices, local(): received = lax.all_to_all(merged, 'x', 0, 0, tiled=True)  8.32 us
    ppermute x3, waiting for transfers between devices, from_next(): return lax.ppermute(value, 'y', [(i, (i - 1) % Y) for i in range(Y)])  7.57 us
    ppermute x3, starting transfers between devices, from_next(): return lax.ppermute(value, 'y', [(i, (i - 1) % Y) for i in range(Y)])  5.75 us
    all_to_all x1, blocking collectives, local(): lax.all_to_all(chosen.reshape((C, GROUPS) + chosen.shape[1:]), 'core', 0,...  4.58 us
  transfers between devices with their start and end apart: 9, of which 5 were waited for; matrix products, arithmetic and copies ran while one was open for 1% of the time, Pallas kernels for 5%

profile of v8, /device:TPU:24, one launch (start us, length us, event | category | flops | bytes accessed | tf_op | source)
XLA Modules:
  0.0 124.3 jit_solution(1193322965029735622)
XLA Ops:
  0.0 0.0 copy-start
  0.0 0.9 convert_element_type.20
  0.9 34.4 %all-gather = bf16[1,1536,128]{2,1,0:T(8,128)(2,1)S(1)} all-gather(bf16[1,128,128]{2,1,0:T(8,128)(2,1)S(1)} %convert_element_type.20), channel_id=2, replica_groups=mesh['z'=12,'y'=8,'core'=2,'x'=4] {'z'}, dimensions={1}, use_global_device_ids=true | all-gather | bytes 425984 | tf_op jit(solution)/shard_map/gather_z/all_gather | solution.py:262
  35.2 4.7 %collective-permute-start = (bf16[1536,128]{1,0:T(8,128)(2,1)S(1)}, bf16[1536,128]{1,0:T(8,128)(2,1)S(1)}, u32[]{:S(2)}, u32[]{:S(2)}) collective-permute-start(bf16[1536,128]{1,0:T(8,128)(2,1)S(1)} %bitcast.22), channel_id=1, source_target_pairs={{0,8},{8,16},{16,24},{24,32},{32,40},{40,48},{48,56},{56,0},{1,9},... | collective-permute-start | bytes 1179656 | tf_op jit(solution)/shard_map/gather_y/ppermute | solution.py:242
  39.9 1.9 %collective-permute-start.3 = (bf16[1536,128]{1,0:T(8,128)(2,1)S(1)}, bf16[1536,128]{1,0:T(8,128)(2,1)S(1)}, u32[]{:S(2)}, u32[]{:S(2)}) collective-permute-start(bf16[1536,128]{1,0:T(8,128)(2,1)S(1)} %bitcast.23), channel_id=1, source_target_pairs={{0,56},{8,0},{16,8},{24,16},{32,24},{40,32},{48,40},{56,48},{1,57}... | collective-permute-start | bytes 1179656 | tf_op jit(solution)/shard_map/gather_y/ppermute | solution.py:238
  41.9 4.1 %collective-permute-done = bf16[1536,128]{1,0:T(8,128)(2,1)S(1)} collective-permute-done((bf16[1536,128]{1,0:T(8,128)(2,1)S(1)}, bf16[1536,128]{1,0:T(8,128)(2,1)S(1)}, u32[]{:S(2)}, u32[]{:S(2)}) %collective-permute-start) | collective-permute-done | bytes 393248 | tf_op jit(solution)/shard_map/gather_y/ppermute | solution.py:242
  46.0 5.3 %collective-permute-start.1 = (bf16[1536,128]{1,0:T(8,128)(2,1)S(1)}, bf16[1536,128]{1,0:T(8,128)(2,1)S(1)}, u32[]{:S(2)}, u32[]{:S(2)}) collective-permute-start(bf16[1536,128]{1,0:T(8,128)(2,1)S(1)} %collective-permute-done), channel_id=1, source_target_pairs={{0,8},{8,16},{16,24},{24,32},{32,40},{40,48},{48,56},{56,0},{1,9},... | collective-permute-start | bytes 1179656 | tf_op jit(solution)/shard_map/gather_y/ppermute | solution.py:242
  51.3 0.3 collective-permute-done.3
  51.5 1.9 %collective-permute-start.4 = (bf16[1536,128]{1,0:T(8,128)(2,1)S(1)}, bf16[1536,128]{1,0:T(8,128)(2,1)S(1)}, u32[]{:S(2)}, u32[]{:S(2)}) collective-permute-start(bf16[1536,128]{1,0:T(8,128)(2,1)S(1)} %collective-permute-done.3), channel_id=1, source_target_pairs={{0,56},{8,0},{16,8},{24,16},{32,24},{40,32},{48,40},{56,48},{1,57}... | collective-permute-start | bytes 1179656 | tf_op jit(solution)/shard_map/gather_y/ppermute | solution.py:238
  53.5 4.6 %collective-permute-done.1 = bf16[1536,128]{1,0:T(8,128)(2,1)S(1)} collective-permute-done((bf16[1536,128]{1,0:T(8,128)(2,1)S(1)}, bf16[1536,128]{1,0:T(8,128)(2,1)S(1)}, u32[]{:S(2)}, u32[]{:S(2)}) %collective-permute-start.1) | collective-permute-done | bytes 393248 | tf_op jit(solution)/shard_map/gather_y/ppermute | solution.py:242
  58.1 5.6 %collective-permute-start.2 = (bf16[1536,128]{1,0:T(8,128)(2,1)S(1)}, bf16[1536,128]{1,0:T(8,128)(2,1)S(1)}, u32[]{:S(2)}, u32[]{:S(2)}) collective-permute-start(bf16[1536,128]{1,0:T(8,128)(2,1)S(1)} %collective-permute-done.1), channel_id=1, source_target_pairs={{0,8},{8,16},{16,24},{24,32},{32,40},{40,48},{48,56},{56,0},{1,9},... | collective-permute-start | bytes 1179656 | tf_op jit(solution)/shard_map/gather_y/ppermute | solution.py:242
  63.7 0.7 add_convert_fusion.1.blocks_ref
  64.4 0.8 add_convert_fusion.slots_ref
  65.1 0.7 small_exchange.2
  65.9 4.3 %all-to-all-start = ((f32[8,56,128]{2,1,0:T(8,128)}), f32[8,56,128]{2,1,0:T(8,128)S(1)}, u32[]{:S(2)}, u32[]{:S(2)}) async-start(f32[8,56,128]{2,1,0:T(8,128)} %small_exchange.2), calls=%async_computation | async-start | bytes 458752 | tf_op jit(solution)/shard_map/small_exchange/all_to_all | solution.py:277
  70.2 0.0 collective-permute-done.4
  70.2 1.9 %collective-permute-start.5 = (bf16[1536,128]{1,0:T(8,128)(2,1)S(1)}, bf16[1536,128]{1,0:T(8,128)(2,1)S(1)}, u32[]{:S(2)}, u32[]{:S(2)}) collective-permute-start(bf16[1536,128]{1,0:T(8,128)(2,1)S(1)} %collective-permute-done.4), channel_id=1, source_target_pairs={{0,56},{8,0},{16,8},{24,16},{32,24},{40,32},{48,40},{56,48},{1,57}... | collective-permute-start | bytes 1179656 | tf_op jit(solution)/shard_map/gather_y/ppermute | solution.py:238
  72.1 0.0 collective-permute-done.2.after_ref
  72.1 5.1 %collective-permute-start.6 = (bf16[1536,128]{1,0:T(8,128)(2,1)S(1)}, bf16[1536,128]{1,0:T(8,128)(2,1)}, u32[]{:S(2)}, u32[]{:S(2)}) collective-permute-start(bf16[1536,128]{1,0:T(8,128)(2,1)S(1)} %collective-permute-done.2.after_ref), channel_id=1, source_target_pairs={{0,8},{8,16},{16,24},{24,32},{32,40},{40,48},{48,56},{56,0},{1,9},... | collective-permute-start | bytes 1179656 | tf_op jit(solution)/shard_map/gather_y/ppermute | solution.py:242
  77.2 0.0 all-to-all-done.pack_ref
  77.3 0.1 reshape.52.live_ref
  77.4 0.1 reshape.51
  77.5 7.3 %collective-permute-done.5 = bf16[1536,128]{1,0:T(8,128)(2,1)S(1)} collective-permute-done((bf16[1536,128]{1,0:T(8,128)(2,1)S(1)}, bf16[1536,128]{1,0:T(8,128)(2,1)S(1)}, u32[]{:S(2)}, u32[]{:S(2)}) %collective-permute-start.5) | collective-permute-done | bytes 393248 | tf_op jit(solution)/shard_map/gather_y/ppermute | solution.py:238
  84.8 2.9 %collect.1 = (bf16[64,128,128]{2,1,0:T(8,128)(2,1)S(1)}, f32[128,128]{1,0:T(8,128)S(1)}) custom-call(s32[64]{0:T(128)S(1)} %get-tuple-element.17.turn_ref, s32[64]{0:T(128)S(1)} %get-tuple-element.16.block_ref, bf16[12,128,128]{2,1,0:T(8,128)(2,1)S(1)} %bitcast.24, bf16[12,128,128]{2,1,0:T(8,128)(2,1)S(1)} %bitcast.27, bf16[12,128,128]{2,1,0:T(8,128)(2,1)S(1)} %bitcast.29, ...), custom_call_target="tpu_custom_call" | custom-call | flops 1000000 | bytes 4000000 | tf_op jit(solution)/shard_map/collect/pallas_call | solution.py:311
  87.6 1.4 %place.1.place_ref = s32[320,128]{1,0:T(8,128)S(1)} custom-call(s32[1]{0:T(128)} %bitcast.1.part_ref, s32[64]{0:T(128)S(1)} %get-tuple-element.15.seen_ref, s32[64]{0:T(128)S(1)} %reshape.52.live_ref, f32[8,56,128]{2,1,0:T(8,128)S(1)} %all-to-all-done.pack_ref), custom_call_target="tpu_custom_call" | custom-call | flops 1000000 | bytes 400000 | tf_op jit(solution)/shard_map/place/pallas_call | solution.py:296
  89.0 0.0 collective-permute-done.6
  89.1 3.3 %select.15 = bf16[8,512,128]{2,1,0:T(8,128)(2,1)S(1)} custom-call(s32[64]{0:T(128)S(1)} %get-tuple-element.17.turn_ref, s32[64]{0:T(128)S(1)} %get-tuple-element.16.block_ref, s32[320,128]{1,0:T(8,128)S(1)} %place.1.place_ref, f32[128,128]{1,0:T(8,128)S(1)} %get-tuple-element.10.gram_ref, bf16[64,128,128]{2,1,0:T(8,128)(2,1)S(1)} %get-tuple-element.11.held_ref, ...), custom_call_target="tpu_custom_call" | custom-call | flops 700000000 | bytes 4000000 | tf_op jit(solution)/shard_map/select/pallas_call | solution.py:325
  92.4 4.6 %all_to_all.20.halves_ref = bf16[2,4,512,128]{3,2,1,0:T(8,128)(2,1)S(1)} all-to-all(bf16[2,4,512,128]{3,2,1,0:T(8,128)(2,1)S(1)} %bitcast.21), channel_id=1, replica_groups=mesh['z'=12,'y'=8,'core'=2,'x'=4] {'core'}, dimensions={0} | all-to-all | bytes 2097152 | tf_op jit(solution)/shard_map/exchange/all_to_all | solution.py:334
  96.9 0.9 exchange.1
  97.8 4.4 %all-to-all-start.2 = ((bf16[4,512,128]{2,1,0:T(8,128)(2,1)}), bf16[4,512,128]{2,1,0:T(8,128)(2,1)S(1)}, u32[]{:S(2)}, u32[]{:S(2)}) async-start(bf16[4,512,128]{2,1,0:T(8,128)(2,1)} %exchange.1), calls=%async_computation.2 | async-start | bytes 1048576 | tf_op jit(solution)/shard_map/exchange/all_to_all | solution.py:338
  102.3 0.0 copy-done
  102.3 0.1 reshape.62.live_ref
  102.3 1.4 %weights.1.weight_ref = bf16[1280,128]{1,0:T(8,128)(2,1)S(1)} custom-call(s32[1]{0:T(128)} %bitcast.core_ref, s32[32]{0:T(128)S(1)} %reshape.62.live_ref, f32[8,56,128]{2,1,0:T(8,128)S(1)} %all-to-all-done.pack_ref), custom_call_target="tpu_custom_call" | custom-call | flops 1000000 | bytes 400000 | tf_op jit(solution)/shard_map/weights/pallas_call | solution.py:303
  103.7 8.3 %all-to-all-done.2.recv_ref = bf16[4,512,128]{2,1,0:T(8,128)(2,1)S(1)} async-done(((bf16[4,512,128]{2,1,0:T(8,128)(2,1)}), bf16[4,512,128]{2,1,0:T(8,128)(2,1)S(1)}, u32[]{:S(2)}, u32[]{:S(2)}) %all-to-all-start.2) | async-done | bytes 524320 | tf_op jit(solution)/shard_map/exchange/all_to_all | solution.py:338
  112.0 3.2 %solve.1 = bf16[128,128]{1,0:T(8,128)(2,1)S(1)} custom-call(bf16[4,512,128]{2,1,0:T(8,128)(2,1)S(1)} %all-to-all-done.2.recv_ref, bf16[1280,128]{1,0:T(8,128)(2,1)S(1)} %weights.1.weight_ref, f32[128,128]{1,0:T(8,128)S(1)} %constant_dynamic-slice_fusion.start_ref), custom_call_target="tpu_custom_call" | custom-call | flops 800000000 | bytes 1200000 | tf_op jit(solution)/shard_map/solve/pallas_call | solution.py:341
  115.2 8.4 %all_to_all.21 = bf16[4,128,128]{2,1,0:T(8,128)(2,1)S(1)} all-to-all(bf16[4,128,128]{2,1,0:T(8,128)(2,1)S(1)} %broadcast_in_dim.4), channel_id=1, replica_groups=mesh['z'=12,'y'=8,'core'=2,'x'=4] {'x'}, dimensions={0} | all-to-all | bytes 262144 | tf_op jit(solution)/shard_map/gather_x/all_to_all | solution.py:234
  123.6 0.7 bitcast_convert_fusion
  (5 shorter events, 0.1 us)
Async XLA Ops:
  0.0 102.3 %copy-start = (f32[512,128]{1,0:T(8,128)S(1)}, f32[512,128]{1,0:T(8,128)}, u32[]{:S(2)}) copy-start(f32[512,128]{1,0:T(8,128)} %param.13) | copy-start | bytes 786436
  35.2 10.7 %collective-permute-start = (bf16[1536,128]{1,0:T(8,128)(2,1)S(1)}, bf16[1536,128]{1,0:T(8,128)(2,1)S(1)}, u32[]{:S(2)}, u32[]{:S(2)}) collective-permute-start(bf16[1536,128]{1,0:T(8,128)(2,1)S(1)} %bitcast.22), channel_id=1, source_target_pairs={{0,8},{8,16},{16,24},{24,32},{32,40},{40,48},{48,56},{56,0},{1,9},... | collective-permute-start | bytes 1179656 | tf_op jit(solution)/shard_map/gather_y/ppermute | solution.py:242
  39.9 11.6 %collective-permute-start.3 = (bf16[1536,128]{1,0:T(8,128)(2,1)S(1)}, bf16[1536,128]{1,0:T(8,128)(2,1)S(1)}, u32[]{:S(2)}, u32[]{:S(2)}) collective-permute-start(bf16[1536,128]{1,0:T(8,128)(2,1)S(1)} %bitcast.23), channel_id=1, source_target_pairs={{0,56},{8,0},{16,8},{24,16},{32,24},{40,32},{48,40},{56,48},{1,57}... | collective-permute-start | bytes 1179656 | tf_op jit(solution)/shard_map/gather_y/ppermute | solution.py:238
  46.0 12.1 %collective-permute-start.1 = (bf16[1536,128]{1,0:T(8,128)(2,1)S(1)}, bf16[1536,128]{1,0:T(8,128)(2,1)S(1)}, u32[]{:S(2)}, u32[]{:S(2)}) collective-permute-start(bf16[1536,128]{1,0:T(8,128)(2,1)S(1)} %collective-permute-done), channel_id=1, source_target_pairs={{0,8},{8,16},{16,24},{24,32},{32,40},{40,48},{48,56},{56,0},{1,9},... | collective-permute-start | bytes 1179656 | tf_op jit(solution)/shard_map/gather_y/ppermute | solution.py:242
  51.5 18.6 %collective-permute-start.4 = (bf16[1536,128]{1,0:T(8,128)(2,1)S(1)}, bf16[1536,128]{1,0:T(8,128)(2,1)S(1)}, u32[]{:S(2)}, u32[]{:S(2)}) collective-permute-start(bf16[1536,128]{1,0:T(8,128)(2,1)S(1)} %collective-permute-done.3), channel_id=1, source_target_pairs={{0,56},{8,0},{16,8},{24,16},{32,24},{40,32},{48,40},{56,48},{1,57}... | collective-permute-start | bytes 1179656 | tf_op jit(solution)/shard_map/gather_y/ppermute | solution.py:238
  58.1 14.0 %collective-permute-start.2 = (bf16[1536,128]{1,0:T(8,128)(2,1)S(1)}, bf16[1536,128]{1,0:T(8,128)(2,1)S(1)}, u32[]{:S(2)}, u32[]{:S(2)}) collective-permute-start(bf16[1536,128]{1,0:T(8,128)(2,1)S(1)} %collective-permute-done.1), channel_id=1, source_target_pairs={{0,8},{8,16},{16,24},{24,32},{32,40},{40,48},{48,56},{56,0},{1,9},... | collective-permute-start | bytes 1179656 | tf_op jit(solution)/shard_map/gather_y/ppermute | solution.py:242
  65.9 11.4 %all-to-all-start = ((f32[8,56,128]{2,1,0:T(8,128)}), f32[8,56,128]{2,1,0:T(8,128)S(1)}, u32[]{:S(2)}, u32[]{:S(2)}) async-start(f32[8,56,128]{2,1,0:T(8,128)} %small_exchange.2), calls=%async_computation | async-start | bytes 458752 | tf_op jit(solution)/shard_map/small_exchange/all_to_all | solution.py:277
  70.2 14.6 %collective-permute-start.5 = (bf16[1536,128]{1,0:T(8,128)(2,1)S(1)}, bf16[1536,128]{1,0:T(8,128)(2,1)S(1)}, u32[]{:S(2)}, u32[]{:S(2)}) collective-permute-start(bf16[1536,128]{1,0:T(8,128)(2,1)S(1)} %collective-permute-done.4), channel_id=1, source_target_pairs={{0,56},{8,0},{16,8},{24,16},{32,24},{40,32},{48,40},{56,48},{1,57}... | collective-permute-start | bytes 1179656 | tf_op jit(solution)/shard_map/gather_y/ppermute | solution.py:238
  72.1 16.9 %collective-permute-start.6 = (bf16[1536,128]{1,0:T(8,128)(2,1)S(1)}, bf16[1536,128]{1,0:T(8,128)(2,1)}, u32[]{:S(2)}, u32[]{:S(2)}) collective-permute-start(bf16[1536,128]{1,0:T(8,128)(2,1)S(1)} %collective-permute-done.2.after_ref), channel_id=1, source_target_pairs={{0,8},{8,16},{16,24},{24,32},{32,40},{40,48},{48,56},{56,0},{1,9},... | collective-permute-start | bytes 1179656 | tf_op jit(solution)/shard_map/gather_y/ppermute | solution.py:242
  97.8 14.2 %all-to-all-start.2 = ((bf16[4,512,128]{2,1,0:T(8,128)(2,1)}), bf16[4,512,128]{2,1,0:T(8,128)(2,1)S(1)}, u32[]{:S(2)}, u32[]{:S(2)}) async-start(bf16[4,512,128]{2,1,0:T(8,128)(2,1)} %exchange.1), calls=%async_computation.2 | async-start | bytes 1048576 | tf_op jit(solution)/shard_map/exchange/all_to_all | solution.py:338

commit v9 on v8

--- a/solution.py
+++ b/solution.py
@@ -71,7 +71,8 @@
 
 def unpack_kernel(core_ref, part_ref, pack_ref, after_ref, own_ref, live_ref):
     for c in range(C):
-        own_ref[c] = pack_ref[c * X + part_ref[0], BLOCK_AT:PACK, :].astype(jnp.int32)
+        source = (core_ref[0] + c) % C * X + part_ref[0]
+        own_ref[c] = pack_ref[source, BLOCK_AT:PACK, :].astype(jnp.int32)
     for s in range(X):
         row = pack_ref[core_ref[0] * X + s, pl.ds(LIVE_AT + part_ref[0], 1), :]
         live_ref[s : s + 1, :] = row.astype(jnp.int32)
@@ -94,9 +95,12 @@
         out_ref[s * LIVE : (s + 1) * LIVE, :] = rows_ref[s, :LIVE, :].astype(bf16)
 
 
-def place_kernel(part_ref, seen_ref, live_ref, pack_ref, out_ref, rows_ref):
+def place_kernel(core_ref, part_ref, seen_ref, live_ref, pack_ref, out_ref, rows_ref):
     items = [
-        pack_ref[c * X + part_ref[0], ITEM_AT : ITEM_AT + GROUPS * PAIRS, :] for c in range(C)
+        pack_ref[
+            (core_ref[0] + c) % C * X + part_ref[0], ITEM_AT : ITEM_AT + GROUPS * PAIRS, :
+        ]
+        for c in range(C)
     ]
     table = jnp.concatenate(items, axis=0).T[:NNZ].astype(jnp.int32)
     lane = lax.broadcasted_iota(jnp.int32, (LIVE, BLK), 1)
@@ -125,10 +129,25 @@
     gram_ref[...] = gram
 
 
-def select_kernel(
-    turn_ref, block_ref, place_ref, gram_ref, held_ref, last_hbm, out_ref, last_ref, sems
+def select_rows(first, turn_ref, block_ref, place_ref, held_ref, last_ref, out_ref):
+    lane = lax.broadcasted_iota(jnp.int32, (LIVE, PAIRS * BLK), 1)
+    for g in range(GROUPS):
+        blocks = []
+        for p in range(PAIRS):
+            q = (first + g) * PAIRS + p
+            blocks.append(
+                jnp.where(turn_ref[q] == Y // 2, last_ref[block_ref[q]], held_ref[q])
+            )
+        onehot = jnp.where(place_ref[:, first + g : first + g + 1] == lane, 1.0, 0.0).astype(bf16)
+        rows = dot(onehot, jnp.concatenate(blocks, axis=0))
+        out_ref[g, :LIVE, :] = rows.astype(bf16)
+
+
+def select_other_kernel(
+    turn_ref, block_ref, place_ref, gram_ref, held_ref, last_hbm, out_ref, packed_ref, last_ref, sems
 ):
     fetch([(last_hbm, last_ref)], sems)
+    select_rows(GROUPS, turn_ref, block_ref, place_ref, held_ref, last_ref, out_ref)
     gram = gram_ref[...] + square(last_ref[...].reshape(Z * BLK, E))
     corner = gram[:HALF, HALF:]
     gram = jnp.concatenate(
@@ -138,31 +157,23 @@
         ],
         axis=0,
     )
-    gram_hi, gram_lo = split(gram)
-    lane = lax.broadcasted_iota(jnp.int32, (LIVE, PAIRS * BLK), 1)
-    for d in range(C * GROUPS):
-        blocks = []
-        for p in range(PAIRS):
-            q = d * PAIRS + p
-            blocks.append(
-                jnp.where(turn_ref[q] == Y // 2, last_ref[block_ref[q]], held_ref[q])
-            )
-        onehot = jnp.where(place_ref[:, d : d + 1] == lane, 1.0, 0.0).astype(bf16)
-        rows = dot(onehot, jnp.concatenate(blocks, axis=0))
-        out_ref[d, :LIVE, :] = rows.astype(bf16)
-        out_ref[d, LIVE : LIVE + GRAM, :] = gram_hi
-        out_ref[d, LIVE + GRAM :, :] = gram_lo
-
-
-def merge_kernel(halves_ref, out_ref):
-    gram = jnp.zeros((GRAM, E), f32)
-    for c in range(C):
-        for part in range(2):
-            at = LIVE + part * GRAM
-            gram = gram + halves_ref[c, 0, at : at + GRAM, :].astype(f32)
+    packed_ref[...] = gram
     gram_hi, gram_lo = split(gram)
     for g in range(GROUPS):
-        out_ref[g, :LIVE, :] = halves_ref[0, g, :LIVE, :] + halves_ref[1, g, :LIVE, :]
+        out_ref[g, LIVE : LIVE + GRAM, :] = gram_hi
+        out_ref[g, LIVE + GRAM :, :] = gram_lo
+
+
+def select_own_kernel(turn_ref, block_ref, place_ref, held_ref, last_hbm, out_ref, last_ref, sems):
+    fetch([(last_hbm, last_ref)], sems)
+    select_rows(0, turn_ref, block_ref, place_ref, held_ref, last_ref, out_ref)
+
+
+def merge_kernel(own_ref, packed_ref, other_ref, out_ref):
+    gram = other_ref[0, LIVE : LIVE + GRAM, :].astype(f32) + other_ref[0, LIVE + GRAM :, :].astype(f32)
+    gram_hi, gram_lo = split(packed_ref[...] + gram)
+    for g in range(GROUPS):
+        out_ref[g, :LIVE, :] = own_ref[g] + other_ref[g, :LIVE, :]
         out_ref[g, LIVE : LIVE + GRAM, :] = gram_hi
         out_ref[g, LIVE + GRAM :, :] = gram_lo
 
@@ -296,9 +307,9 @@
         place = call(
             place_kernel,
             jax.ShapeDtypeStruct((LIVE, BLK), jnp.int32),
-            [smem()] * 3 + [vmem()],
+            [smem()] * 4 + [vmem()],
             [pltpu.VMEM((C * GROUPS, LIVE + NNZ, BLK), jnp.int32)],
-        )(part.reshape(1), seen, live, pack)
+        )(core.reshape(1), part.reshape(1), seen, live, pack)
     with jax.named_scope("weights"):
         weight = call(
             weight_kernel,
@@ -322,19 +333,27 @@
             nbytes=4_000_000,
         )(turns, spots, *pieces)
     with jax.named_scope("select"):
+        shape = jax.ShapeDtypeStruct((GROUPS, LIVE + 2 * GRAM, E), bf16)
+        scratch = [pltpu.VMEM((Z, BLK, E), bf16), pltpu.SemaphoreType.DMA((1,))]
+        other, packed = call(
+            select_other_kernel,
+            (shape, jax.ShapeDtypeStruct((GRAM, E), f32)),
+            [smem()] * 2 + [vmem()] * 3 + [hbm()],
+            scratch,
+            flops=350_000_000,
+            nbytes=2_000_000,
+        )(turns, spots, place, gram, held, last)
+        other = lax.ppermute(other, "core", [(c, (c + 1) % C) for c in range(C)])
         chosen = call(
-            select_kernel,
-            jax.ShapeDtypeStruct((C * GROUPS, LIVE + 2 * GRAM, E), bf16),
-            [smem()] * 2 + [vmem()] * 3 + [hbm()],
-            [pltpu.VMEM((Z, BLK, E), bf16), pltpu.SemaphoreType.DMA((1,))],
-            flops=700_000_000,
-            nbytes=4_000_000,
-        )(turns, spots, place, gram, held, last)
+            select_own_kernel,
+            jax.ShapeDtypeStruct((GROUPS, LIVE, E), bf16),
+            [smem()] * 2 + [vmem()] * 2 + [hbm()],
+            scratch,
+            flops=350_000_000,
+            nbytes=2_000_000,
+        )(turns, spots, place, held, last)
     with jax.named_scope("exchange"):
-        halves = lax.all_to_all(
-            chosen.reshape((C, GROUPS) + chosen.shape[1:]), "core", 0, 0, tiled=True
-        )
-        merged = call(merge_kernel, jax.ShapeDtypeStruct(halves.shape[1:], bf16), [vmem()])(halves)
+        merged = call(merge_kernel, shape, [vmem()] * 3)(chosen, packed, other)
         received = lax.all_to_all(merged, "x", 0, 0, tiled=True)
     with jax.named_scope("solve"):
         start = lax.dynamic_slice_in_dim(user_emb, part * BLK, BLK, 0)

time: 125 us -> 123 us (0.984)
  blocking collectives: 47.3 us -> 42.7 us
  starting transfers between devices: 35.2 us -> 37.1 us
    all_to_all x1 -> x0, blocking collectives: 4.58 us -> none  [local(): lax.all_to_all(chosen.reshape((C, GROUPS) + chosen.shape[1:]), 'core', 0,...]
    ppermute x0 -> x1, starting transfers between devices: none -> 1.92 us  [local(): other = lax.ppermute(other, 'core', [(c, (c + 1) % C) for c in range(C)])]
    pallas_call x2 -> x3, Pallas kernels: 4.18 us -> 4.36 us  [the longest x1 1.83 us: local(): call(select_other_kernel, (shape, jax.ShapeDtypeStruct((GRAM, E), f32)),...]
  transfers between devices with their start and end apart: 9 -> 10, of which waited for: 5 -> 6; matrix products, arithmetic and copies ran while one was open for 1% -> 1% of each run, Pallas kernels for 5% -> 7%
where the time goes in v9:
time: 123 us
  blocking collectives  42.7 us (35%)
  starting transfers between devices  37.1 us (30%)
  waiting for transfers between devices  25.1 us (20%)
  Pallas kernels  14.1 us (11%)
  other arithmetic  3.12 us (3%)
    all_gather x1, blocking collectives, local(): column = lax.all_gather(own_block, 'z', axis=0, tiled=True)  34.4 us
    ppermute x4, starting transfers between devices, from_last(): return lax.ppermute(value, 'y', [(i, (i + 1) % Y) for i in range(Y)])  20.7 us
    ppermute x4, waiting for transfers between devices, from_last(): return lax.ppermute(value, 'y', [(i, (i + 1) % Y) for i in range(Y)])  8.72 us
    all_to_all x1, waiting for transfers between devices, local(): received = lax.all_to_all(merged, 'x', 0, 0, tiled=True)  8.5 us
    all_to_all x1, blocking collectives, spread(): lax.all_to_all(jnp.broadcast_to(value[None], (size,) + value.shape), axis...  8.36 us
    ppermute x3, waiting for transfers between devices, from_next(): return lax.ppermute(value, 'y', [(i, (i - 1) % Y) for i in range(Y)])  7.68 us
    ppermute x3, starting transfers between devices, from_next(): return lax.ppermute(value, 'y', [(i, (i - 1) % Y) for i in range(Y)])  5.75 us
    all_to_all x1, starting transfers between devices, local(): received = lax.all_to_all(merged, 'x', 0, 0, tiled=True)  4.44 us
  transfers between devices with their start and end apart: 10, of which 6 were waited for; matrix products, arithmetic and copies ran while one was open for 1% of the time, Pallas kernels for 7%

profile of v9, /device:TPU:24, one launch (start us, length us, event | category | flops | bytes accessed | tf_op | source)
XLA Modules:
  0.0 122.6 jit_solution(4686672727638518104)
XLA Ops:
  0.0 0.0 copy-start
  0.0 0.9 convert_element_type.20
  0.9 34.4 %all-gather = bf16[1,1536,128]{2,1,0:T(8,128)(2,1)S(1)} all-gather(bf16[1,128,128]{2,1,0:T(8,128)(2,1)S(1)} %convert_element_type.20), channel_id=2, replica_groups=mesh['z'=12,'y'=8,'core'=2,'x'=4] {'z'}, dimensions={1}, use_global_device_ids=true | all-gather | bytes 425984 | tf_op jit(solution)/shard_map/gather_z/all_gather | solution.py:273
  35.2 4.7 %collective-permute-start = (bf16[1536,128]{1,0:T(8,128)(2,1)S(1)}, bf16[1536,128]{1,0:T(8,128)(2,1)S(1)}, u32[]{:S(2)}, u32[]{:S(2)}) collective-permute-start(bf16[1536,128]{1,0:T(8,128)(2,1)S(1)} %bitcast.20), channel_id=1, source_target_pairs={{0,8},{8,16},{16,24},{24,32},{32,40},{40,48},{48,56},{56,0},{1,9},... | collective-permute-start | bytes 1179656 | tf_op jit(solution)/shard_map/gather_y/ppermute | solution.py:253
  39.9 1.9 %collective-permute-start.3 = (bf16[1536,128]{1,0:T(8,128)(2,1)S(1)}, bf16[1536,128]{1,0:T(8,128)(2,1)S(1)}, u32[]{:S(2)}, u32[]{:S(2)}) collective-permute-start(bf16[1536,128]{1,0:T(8,128)(2,1)S(1)} %bitcast.21), channel_id=1, source_target_pairs={{0,56},{8,0},{16,8},{24,16},{32,24},{40,32},{48,40},{56,48},{1,57}... | collective-permute-start | bytes 1179656 | tf_op jit(solution)/shard_map/gather_y/ppermute | solution.py:249
  41.9 4.1 %collective-permute-done = bf16[1536,128]{1,0:T(8,128)(2,1)S(1)} collective-permute-done((bf16[1536,128]{1,0:T(8,128)(2,1)S(1)}, bf16[1536,128]{1,0:T(8,128)(2,1)S(1)}, u32[]{:S(2)}, u32[]{:S(2)}) %collective-permute-start) | collective-permute-done | bytes 393248 | tf_op jit(solution)/shard_map/gather_y/ppermute | solution.py:253
  46.0 5.3 %collective-permute-start.1 = (bf16[1536,128]{1,0:T(8,128)(2,1)S(1)}, bf16[1536,128]{1,0:T(8,128)(2,1)S(1)}, u32[]{:S(2)}, u32[]{:S(2)}) collective-permute-start(bf16[1536,128]{1,0:T(8,128)(2,1)S(1)} %collective-permute-done), channel_id=1, source_target_pairs={{0,8},{8,16},{16,24},{24,32},{32,40},{40,48},{48,56},{56,0},{1,9},... | collective-permute-start | bytes 1179656 | tf_op jit(solution)/shard_map/gather_y/ppermute | solution.py:253
  51.3 0.3 collective-permute-done.3
  51.5 1.9 %collective-permute-start.4 = (bf16[1536,128]{1,0:T(8,128)(2,1)S(1)}, bf16[1536,128]{1,0:T(8,128)(2,1)S(1)}, u32[]{:S(2)}, u32[]{:S(2)}) collective-permute-start(bf16[1536,128]{1,0:T(8,128)(2,1)S(1)} %collective-permute-done.3), channel_id=1, source_target_pairs={{0,56},{8,0},{16,8},{24,16},{32,24},{40,32},{48,40},{56,48},{1,57}... | collective-permute-start | bytes 1179656 | tf_op jit(solution)/shard_map/gather_y/ppermute | solution.py:249
  53.5 4.6 %collective-permute-done.1 = bf16[1536,128]{1,0:T(8,128)(2,1)S(1)} collective-permute-done((bf16[1536,128]{1,0:T(8,128)(2,1)S(1)}, bf16[1536,128]{1,0:T(8,128)(2,1)S(1)}, u32[]{:S(2)}, u32[]{:S(2)}) %collective-permute-start.1) | collective-permute-done | bytes 393248 | tf_op jit(solution)/shard_map/gather_y/ppermute | solution.py:253
  58.1 5.6 %collective-permute-start.2 = (bf16[1536,128]{1,0:T(8,128)(2,1)S(1)}, bf16[1536,128]{1,0:T(8,128)(2,1)S(1)}, u32[]{:S(2)}, u32[]{:S(2)}) collective-permute-start(bf16[1536,128]{1,0:T(8,128)(2,1)S(1)} %collective-permute-done.1), channel_id=1, source_target_pairs={{0,8},{8,16},{16,24},{24,32},{32,40},{40,48},{48,56},{56,0},{1,9},... | collective-permute-start | bytes 1179656 | tf_op jit(solution)/shard_map/gather_y/ppermute | solution.py:253
  63.7 0.7 add_convert_fusion.1.blocks_ref
  64.4 0.8 add_convert_fusion.slots_ref
  65.1 0.7 small_exchange.2
  65.9 4.3 %all-to-all-start = ((f32[8,56,128]{2,1,0:T(8,128)}), f32[8,56,128]{2,1,0:T(8,128)S(1)}, u32[]{:S(2)}, u32[]{:S(2)}) async-start(f32[8,56,128]{2,1,0:T(8,128)} %small_exchange.2), calls=%async_computation | async-start | bytes 458752 | tf_op jit(solution)/shard_map/small_exchange/all_to_all | solution.py:288
  70.2 0.0 collective-permute-done.4
  70.2 1.9 %collective-permute-start.5 = (bf16[1536,128]{1,0:T(8,128)(2,1)S(1)}, bf16[1536,128]{1,0:T(8,128)(2,1)}, u32[]{:S(2)}, u32[]{:S(2)}) collective-permute-start(bf16[1536,128]{1,0:T(8,128)(2,1)S(1)} %collective-permute-done.4), channel_id=1, source_target_pairs={{0,56},{8,0},{16,8},{24,16},{32,24},{40,32},{48,40},{56,48},{1,57}... | collective-permute-start | bytes 1179656 | tf_op jit(solution)/shard_map/gather_y/ppermute | solution.py:249
  72.1 0.0 collective-permute-done.2.after_ref
  72.1 5.1 %collective-permute-start.6 = (bf16[1536,128]{1,0:T(8,128)(2,1)S(1)}, bf16[1536,128]{1,0:T(8,128)(2,1)S(1)}, u32[]{:S(2)}, u32[]{:S(2)}) collective-permute-start(bf16[1536,128]{1,0:T(8,128)(2,1)S(1)} %collective-permute-done.2.after_ref), channel_id=1, source_target_pairs={{0,8},{8,16},{16,24},{24,32},{32,40},{40,48},{48,56},{56,0},{1,9},... | collective-permute-start | bytes 1179656 | tf_op jit(solution)/shard_map/gather_y/ppermute | solution.py:253
  77.2 0.0 all-to-all-done.pack_ref
  77.3 0.1 reshape.50.live_ref
  77.4 0.1 reshape.49
  77.5 7.4 %collective-permute-done.5 = bf16[1536,128]{1,0:T(8,128)(2,1)} collective-permute-done((bf16[1536,128]{1,0:T(8,128)(2,1)S(1)}, bf16[1536,128]{1,0:T(8,128)(2,1)}, u32[]{:S(2)}, u32[]{:S(2)}) %collective-permute-start.5) | collective-permute-done | bytes 393248 | tf_op jit(solution)/shard_map/gather_y/ppermute | solution.py:249
  84.9 3.1 %collect.1 = (bf16[64,128,128]{2,1,0:T(8,128)(2,1)S(1)}, f32[128,128]{1,0:T(8,128)S(1)}) custom-call(s32[64]{0:T(128)S(1)} %get-tuple-element.21.turn_ref, s32[64]{0:T(128)S(1)} %get-tuple-element.20.block_ref, bf16[12,128,128]{2,1,0:T(8,128)(2,1)S(1)} %bitcast.22, bf16[12,128,128]{2,1,0:T(8,128)(2,1)S(1)} %bitcast.27, bf16[12,128,128]{2,1,0:T(8,128)(2,1)S(1)} %bitcast.29, ...), custom_call_target="tpu_custom_call" | custom-call | flops 1000000 | bytes 4000000 | tf_op jit(solution)/shard_map/collect/pallas_call | solution.py:322
  88.0 1.4 %place.1.place_ref = s32[320,128]{1,0:T(8,128)S(1)} custom-call(s32[1]{0:T(128)} %bitcast.core_ref, s32[1]{0:T(128)} %bitcast.1.part_ref, s32[64]{0:T(128)S(1)} %get-tuple-element.19.seen_ref, s32[64]{0:T(128)S(1)} %reshape.50.live_ref, f32[8,56,128]{2,1,0:T(8,128)S(1)} %all-to-all-done.pack_ref), custom_call_target="tpu_custom_call" | custom-call | flops 1000000 | bytes 400000 | tf_op jit(solution)/shard_map/place/pallas_call | solution.py:307
  89.4 0.0 collective-permute-done.6
  89.4 1.8 %select.17 = (bf16[4,512,128]{2,1,0:T(8,128)(2,1)S(1)}, f32[96,128]{1,0:T(8,128)S(1)}) custom-call(s32[64]{0:T(128)S(1)} %get-tuple-element.21.turn_ref, s32[64]{0:T(128)S(1)} %get-tuple-element.20.block_ref, s32[320,128]{1,0:T(8,128)S(1)} %place.1.place_ref, f32[128,128]{1,0:T(8,128)S(1)} %get-tuple-element.13.gram_ref, ...), custom_call_target="tpu_custom_call" | custom-call | flops 350000000 | bytes 2000000 | tf_op jit(solution)/shard_map/select/pallas_call | solution.py:338
  91.2 1.9 %collective-permute-start.7 = (bf16[4,512,128]{2,1,0:T(8,128)(2,1)S(1)}, bf16[4,512,128]{2,1,0:T(8,128)(2,1)S(1)}, u32[]{:S(2)}, u32[]{:S(2)}) collective-permute-start(bf16[4,512,128]{2,1,0:T(8,128)(2,1)S(1)} %get-tuple-element.15), channel_id=1, source_target_pairs={{0,4},{4,0},{1,5},{5,1},{2,6},{6,2},{3,7},{7,3},{8,12},{12,8},{9,1... | collective-permute-start | bytes 1572872 | tf_op jit(solution)/shard_map/select/ppermute | solution.py:346
  93.2 1.7 %select.16.own_ref = bf16[4,320,128]{2,1,0:T(8,128)(2,1)S(1)} custom-call(s32[64]{0:T(128)S(1)} %get-tuple-element.21.turn_ref, s32[64]{0:T(128)S(1)} %get-tuple-element.20.block_ref, s32[320,128]{1,0:T(8,128)S(1)} %place.1.place_ref, bf16[64,128,128]{2,1,0:T(8,128)(2,1)S(1)} %get-tuple-element.12.held_ref, bf16[12,128,128]{2,1,0:T(8,128)(2,1)S(1)} %bitcast.25), custom_call_target="tpu_custom_call" | custom-call | flops 350000000 | bytes 2000000 | tf_op jit(solution)/shard_map/select/pallas_call | solution.py:347
  94.8 0.2 collective-permute-done.7.other_ref
  95.0 0.9 exchange.1
  95.9 4.4 %all-to-all-start.1 = ((bf16[4,512,128]{2,1,0:T(8,128)(2,1)}), bf16[4,512,128]{2,1,0:T(8,128)(2,1)S(1)}, u32[]{:S(2)}, u32[]{:S(2)}) async-start(bf16[4,512,128]{2,1,0:T(8,128)(2,1)} %exchange.1), calls=%async_computation.1 | async-start | bytes 1048576 | tf_op jit(solution)/shard_map/exchange/all_to_all | solution.py:357
  100.4 0.0 copy-done
  100.4 0.1 reshape.59.live_ref
  100.4 1.4 %weights.1.weight_ref = bf16[1280,128]{1,0:T(8,128)(2,1)S(1)} custom-call(s32[1]{0:T(128)} %bitcast.core_ref, s32[32]{0:T(128)S(1)} %reshape.59.live_ref, f32[8,56,128]{2,1,0:T(8,128)S(1)} %all-to-all-done.pack_ref), custom_call_target="tpu_custom_call" | custom-call | flops 1000000 | bytes 400000 | tf_op jit(solution)/shard_map/weights/pallas_call | solution.py:314
  101.8 8.5 %all-to-all-done.1.recv_ref = bf16[4,512,128]{2,1,0:T(8,128)(2,1)S(1)} async-done(((bf16[4,512,128]{2,1,0:T(8,128)(2,1)}), bf16[4,512,128]{2,1,0:T(8,128)(2,1)S(1)}, u32[]{:S(2)}, u32[]{:S(2)}) %all-to-all-start.1) | async-done | bytes 524320 | tf_op jit(solution)/shard_map/exchange/all_to_all | solution.py:357
  110.3 3.2 %solve.1 = bf16[128,128]{1,0:T(8,128)(2,1)S(1)} custom-call(bf16[4,512,128]{2,1,0:T(8,128)(2,1)S(1)} %all-to-all-done.1.recv_ref, bf16[1280,128]{1,0:T(8,128)(2,1)S(1)} %weights.1.weight_ref, f32[128,128]{1,0:T(8,128)S(1)} %constant_dynamic-slice_fusion.start_ref), custom_call_target="tpu_custom_call" | custom-call | flops 800000000 | bytes 1200000 | tf_op jit(solution)/shard_map/solve/pallas_call | solution.py:360
  113.5 8.4 %all_to_all.15 = bf16[4,128,128]{2,1,0:T(8,128)(2,1)S(1)} all-to-all(bf16[4,128,128]{2,1,0:T(8,128)(2,1)S(1)} %broadcast_in_dim.4), channel_id=1, replica_groups=mesh['z'=12,'y'=8,'core'=2,'x'=4] {'x'}, dimensions={0} | all-to-all | bytes 262144 | tf_op jit(solution)/shard_map/gather_x/all_to_all | solution.py:245
  121.9 0.7 bitcast_convert_fusion
  (5 shorter events, 0.1 us)
Async XLA Ops:
  0.0 100.4 %copy-start = (f32[512,128]{1,0:T(8,128)S(1)}, f32[512,128]{1,0:T(8,128)}, u32[]{:S(2)}) copy-start(f32[512,128]{1,0:T(8,128)} %param.13) | copy-start | bytes 786436
  35.2 10.7 %collective-permute-start = (bf16[1536,128]{1,0:T(8,128)(2,1)S(1)}, bf16[1536,128]{1,0:T(8,128)(2,1)S(1)}, u32[]{:S(2)}, u32[]{:S(2)}) collective-permute-start(bf16[1536,128]{1,0:T(8,128)(2,1)S(1)} %bitcast.20), channel_id=1, source_target_pairs={{0,8},{8,16},{16,24},{24,32},{32,40},{40,48},{48,56},{56,0},{1,9},... | collective-permute-start | bytes 1179656 | tf_op jit(solution)/shard_map/gather_y/ppermute | solution.py:253
  39.9 11.6 %collective-permute-start.3 = (bf16[1536,128]{1,0:T(8,128)(2,1)S(1)}, bf16[1536,128]{1,0:T(8,128)(2,1)S(1)}, u32[]{:S(2)}, u32[]{:S(2)}) collective-permute-start(bf16[1536,128]{1,0:T(8,128)(2,1)S(1)} %bitcast.21), channel_id=1, source_target_pairs={{0,56},{8,0},{16,8},{24,16},{32,24},{40,32},{48,40},{56,48},{1,57}... | collective-permute-start | bytes 1179656 | tf_op jit(solution)/shard_map/gather_y/ppermute | solution.py:249
  46.0 12.1 %collective-permute-start.1 = (bf16[1536,128]{1,0:T(8,128)(2,1)S(1)}, bf16[1536,128]{1,0:T(8,128)(2,1)S(1)}, u32[]{:S(2)}, u32[]{:S(2)}) collective-permute-start(bf16[1536,128]{1,0:T(8,128)(2,1)S(1)} %collective-permute-done), channel_id=1, source_target_pairs={{0,8},{8,16},{16,24},{24,32},{32,40},{40,48},{48,56},{56,0},{1,9},... | collective-permute-start | bytes 1179656 | tf_op jit(solution)/shard_map/gather_y/ppermute | solution.py:253
  51.5 18.6 %collective-permute-start.4 = (bf16[1536,128]{1,0:T(8,128)(2,1)S(1)}, bf16[1536,128]{1,0:T(8,128)(2,1)S(1)}, u32[]{:S(2)}, u32[]{:S(2)}) collective-permute-start(bf16[1536,128]{1,0:T(8,128)(2,1)S(1)} %collective-permute-done.3), channel_id=1, source_target_pairs={{0,56},{8,0},{16,8},{24,16},{32,24},{40,32},{48,40},{56,48},{1,57}... | collective-permute-start | bytes 1179656 | tf_op jit(solution)/shard_map/gather_y/ppermute | solution.py:249
  58.1 14.0 %collective-permute-start.2 = (bf16[1536,128]{1,0:T(8,128)(2,1)S(1)}, bf16[1536,128]{1,0:T(8,128)(2,1)S(1)}, u32[]{:S(2)}, u32[]{:S(2)}) collective-permute-start(bf16[1536,128]{1,0:T(8,128)(2,1)S(1)} %collective-permute-done.1), channel_id=1, source_target_pairs={{0,8},{8,16},{16,24},{24,32},{32,40},{40,48},{48,56},{56,0},{1,9},... | collective-permute-start | bytes 1179656 | tf_op jit(solution)/shard_map/gather_y/ppermute | solution.py:253
  65.9 11.4 %all-to-all-start = ((f32[8,56,128]{2,1,0:T(8,128)}), f32[8,56,128]{2,1,0:T(8,128)S(1)}, u32[]{:S(2)}, u32[]{:S(2)}) async-start(f32[8,56,128]{2,1,0:T(8,128)} %small_exchange.2), calls=%async_computation | async-start | bytes 458752 | tf_op jit(solution)/shard_map/small_exchange/all_to_all | solution.py:288
  70.2 14.7 %collective-permute-start.5 = (bf16[1536,128]{1,0:T(8,128)(2,1)S(1)}, bf16[1536,128]{1,0:T(8,128)(2,1)}, u32[]{:S(2)}, u32[]{:S(2)}) collective-permute-start(bf16[1536,128]{1,0:T(8,128)(2,1)S(1)} %collective-permute-done.4), channel_id=1, source_target_pairs={{0,56},{8,0},{16,8},{24,16},{32,24},{40,32},{48,40},{56,48},{1,57}... | collective-permute-start | bytes 1179656 | tf_op jit(solution)/shard_map/gather_y/ppermute | solution.py:249
  72.1 17.3 %collective-permute-start.6 = (bf16[1536,128]{1,0:T(8,128)(2,1)S(1)}, bf16[1536,128]{1,0:T(8,128)(2,1)S(1)}, u32[]{:S(2)}, u32[]{:S(2)}) collective-permute-start(bf16[1536,128]{1,0:T(8,128)(2,1)S(1)} %collective-permute-done.2.after_ref), channel_id=1, source_target_pairs={{0,8},{8,16},{16,24},{24,32},{32,40},{40,48},{48,56},{56,0},{1,9},... | collective-permute-start | bytes 1179656 | tf_op jit(solution)/shard_map/gather_y/ppermute | solution.py:253
  91.2 3.8 %collective-permute-start.7 = (bf16[4,512,128]{2,1,0:T(8,128)(2,1)S(1)}, bf16[4,512,128]{2,1,0:T(8,128)(2,1)S(1)}, u32[]{:S(2)}, u32[]{:S(2)}) collective-permute-start(bf16[4,512,128]{2,1,0:T(8,128)(2,1)S(1)} %get-tuple-element.15), channel_id=1, source_target_pairs={{0,4},{4,0},{1,5},{5,1},{2,6},{6,2},{3,7},{7,3},{8,12},{12,8},{9,1... | collective-permute-start | bytes 1572872 | tf_op jit(solution)/shard_map/select/ppermute | solution.py:346
  95.9 14.4 %all-to-all-start.1 = ((bf16[4,512,128]{2,1,0:T(8,128)(2,1)}), bf16[4,512,128]{2,1,0:T(8,128)(2,1)S(1)}, u32[]{:S(2)}, u32[]{:S(2)}) async-start(bf16[4,512,128]{2,1,0:T(8,128)(2,1)} %exchange.1), calls=%async_computation.1 | async-start | bytes 1048576 | tf_op jit(solution)/shard_map/exchange/all_to_all | solution.py:357

commit v10 on v9

--- a/solution.py
+++ b/solution.py
@@ -265,26 +265,43 @@
     )
 
 
+def pass_kernel(value_ref, after_ref, out_ref):
+    pass
+
+
+def pass_on(value, after):
+    return pl.pallas_call(
+        pass_kernel,
+        out_shape=jax.ShapeDtypeStruct(value.shape, value.dtype),
+        in_specs=[hbm(), hbm()],
+        out_specs=hbm(),
+        input_output_aliases={0: 0},
+    )(value, after)
+
+
 def local(block_ids, pair_live, user_rows, item_rows, counts, item_emb, user_emb):
     core = lax.axis_index("core")
     part = lax.axis_index("x")
     own_block = item_emb[0].astype(bf16)
     with jax.named_scope("gather_z"):
         column = lax.all_gather(own_block, "z", axis=0, tiled=True)
-    with jax.named_scope("gather_y"):
-        ups, downs = [column], [column]
-        for _ in range(Y // 2 - 1):
-            ups.append(from_next(ups[-1]))
-            downs.append(from_last(downs[-1]))
-        downs.append(from_last(downs[-1]))
-        pieces = [piece.reshape(Z, BLK, E) for piece in ups + downs[:0:-1]]
-
     with jax.named_scope("small_exchange"):
         slots = jnp.concatenate([user_rows[:, 0], counts[:, 0], item_rows[:, 0]], axis=1)
         blocks = jnp.concatenate([block_ids[:, 0], pair_live[:, 0]], axis=0)
         pack = call(
             pack_kernel, jax.ShapeDtypeStruct((C * X, PACK, BLK), f32), [vmem()] * 2
         )(slots.astype(f32), blocks.astype(f32))
+    with jax.named_scope("gather_y"):
+        ups, downs = [column], [column]
+        for _ in range(Y // 2 - 1):
+            ups.append(from_next(ups[-1]))
+            downs.append(from_last(downs[-1]))
+            if len(ups) == 2:
+                ups[1] = pass_on(ups[1], pack)
+        downs.append(from_last(downs[-1]))
+        pieces = [piece.reshape(Z, BLK, E) for piece in ups + downs[:0:-1]]
+
+    with jax.named_scope("small_exchange"):
         pack = lax.all_to_all(pack, ("core", "x"), 0, 0, tiled=True)
         own, user_live = call(
             unpack_kernel,

time: 123 us -> 122 us (level)
  waiting for transfers between devices: 25.1 us -> 22 us
  local copies, waits for them, and re-layouts: 0.28 us -> 2.71 us
    ppermute x4, waiting for transfers between devices: 8.72 us -> 6.05 us  [from_last(): return lax.ppermute(value, 'y', [(i, (i + 1) % Y) for i in range(Y)])]
    unnamed x2 -> x8, local copies, waits for them, and re-layouts: 0.01 us -> 2.44 us
  transfers between devices with their start and end apart: 10 -> 10, of which waited for: 6 -> 5; matrix products, arithmetic and copies ran while one was open for 1% -> 1% of each run, Pallas kernels for 7% -> 6%
where the time goes in v10:
time: 122 us; the launch traced here: 121 us
  blocking collectives  42.7 us (35%)
  starting transfers between devices  37.1 us (30%)
  waiting for transfers between devices  22 us (18%)
  Pallas kernels  13.2 us (11%)
  other arithmetic  3.12 us (3%)
  local copies, waits for them, and re-layouts  2.71 us (2%)
    all_gather x1, blocking collectives, local(): column = lax.all_gather(own_block, 'z', axis=0, tiled=True)  34.4 us
    ppermute x4, starting transfers between devices, from_last(): return lax.ppermute(value, 'y', [(i, (i + 1) % Y) for i in range(Y)])  20.7 us
    all_to_all x1, waiting for transfers between devices, local(): received = lax.all_to_all(merged, 'x', 0, 0, tiled=True)  8.49 us
    all_to_all x1, blocking collectives, spread(): lax.all_to_all(jnp.broadcast_to(value[None], (size,) + value.shape), axis...  8.36 us
    ppermute x3, waiting for transfers between devices, from_next(): return lax.ppermute(value, 'y', [(i, (i - 1) % Y) for i in range(Y)])  7.29 us
    ppermute x4, waiting for transfers between devices, from_last(): return lax.ppermute(value, 'y', [(i, (i + 1) % Y) for i in range(Y)])  6.05 us
    ppermute x3, starting transfers between devices, from_next(): return lax.ppermute(value, 'y', [(i, (i - 1) % Y) for i in range(Y)])  5.75 us
    all_to_all x1, starting transfers between devices, local(): received = lax.all_to_all(merged, 'x', 0, 0, tiled=True)  4.44 us
  transfers between devices with their start and end apart: 10, of which 5 were waited for; matrix products, arithmetic and copies ran while one was open for 1% of the time, Pallas kernels for 6%

profile of v10, /device:TPU:24, one launch (start us, length us, event | category | flops | bytes accessed | tf_op | source)
XLA Modules:
  0.0 121.0 jit_solution(1036107365809480125)
XLA Ops:
  0.0 0.0 copy-start
  0.0 0.9 convert_element_type.20
  0.9 34.4 %all-gather = bf16[1,1536,128]{2,1,0:T(8,128)(2,1)S(1)} all-gather(bf16[1,128,128]{2,1,0:T(8,128)(2,1)S(1)} %convert_element_type.20), channel_id=2, replica_groups=mesh['z'=12,'y'=8,'core'=2,'x'=4] {'z'}, dimensions={1}, use_global_device_ids=true | all-gather | bytes 425984 | tf_op jit(solution)/shard_map/gather_z/all_gather | solution.py:287
  35.2 4.7 %collective-permute-start = (bf16[1536,128]{1,0:T(8,128)(2,1)S(1)}, bf16[1536,128]{1,0:T(8,128)(2,1)S(1)}, u32[]{:S(2)}, u32[]{:S(2)}) collective-permute-start(bf16[1536,128]{1,0:T(8,128)(2,1)S(1)} %bitcast.20), channel_id=1, source_target_pairs={{0,8},{8,16},{16,24},{24,32},{32,40},{40,48},{48,56},{56,0},{1,9},... | collective-permute-start | bytes 1179656 | tf_op jit(solution)/shard_map/gather_y/ppermute | solution.py:253
  39.9 1.9 %collective-permute-start.3 = (bf16[1536,128]{1,0:T(8,128)(2,1)S(1)}, bf16[1536,128]{1,0:T(8,128)(2,1)S(1)}, u32[]{:S(2)}, u32[]{:S(2)}) collective-permute-start(bf16[1536,128]{1,0:T(8,128)(2,1)S(1)} %bitcast.21), channel_id=1, source_target_pairs={{0,56},{8,0},{16,8},{24,16},{32,24},{40,32},{48,40},{56,48},{1,57}... | collective-permute-start | bytes 1179656 | tf_op jit(solution)/shard_map/gather_y/ppermute | solution.py:249
  41.9 4.1 %collective-permute-done = bf16[1536,128]{1,0:T(8,128)(2,1)S(1)} collective-permute-done((bf16[1536,128]{1,0:T(8,128)(2,1)S(1)}, bf16[1536,128]{1,0:T(8,128)(2,1)S(1)}, u32[]{:S(2)}, u32[]{:S(2)}) %collective-permute-start) | collective-permute-done | bytes 393248 | tf_op jit(solution)/shard_map/gather_y/ppermute | solution.py:253
  46.0 5.3 %collective-permute-start.1 = (bf16[1536,128]{1,0:T(8,128)(2,1)S(1)}, bf16[1536,128]{1,0:T(8,128)(2,1)S(1)}, u32[]{:S(2)}, u32[]{:S(2)}) collective-permute-start(bf16[1536,128]{1,0:T(8,128)(2,1)S(1)} %collective-permute-done), channel_id=1, source_target_pairs={{0,8},{8,16},{16,24},{24,32},{32,40},{40,48},{48,56},{56,0},{1,9},... | collective-permute-start | bytes 1179656 | tf_op jit(solution)/shard_map/gather_y/ppermute | solution.py:253
  51.3 0.7 add_convert_fusion.1.blocks_ref
  52.0 0.8 add_convert_fusion.slots_ref
  52.8 0.0 copy-start.1
  52.8 0.7 copy-done.1
  53.5 0.0 collective-permute-done.3.value_ref
  53.5 0.0 copy-start.2
  53.5 0.8 copy-done.2
  54.2 1.9 %collective-permute-start.4 = (bf16[1536,128]{1,0:T(8,128)(2,1)}, bf16[1536,128]{1,0:T(8,128)(2,1)S(1)}, u32[]{:S(2)}, u32[]{:S(2)}) collective-permute-start(bf16[1536,128]{1,0:T(8,128)(2,1)} %gather_y.1), channel_id=1, source_target_pairs={{0,56},{8,0},{16,8},{24,16},{32,24},{40,32},{48,40},{56,48},{1,57}... | collective-permute-start | bytes 1179656 | tf_op jit(solution)/shard_map/gather_y/ppermute | solution.py:249
  56.1 1.9 %collective-permute-done.1 = bf16[1536,128]{1,0:T(8,128)(2,1)S(1)} collective-permute-done((bf16[1536,128]{1,0:T(8,128)(2,1)S(1)}, bf16[1536,128]{1,0:T(8,128)(2,1)S(1)}, u32[]{:S(2)}, u32[]{:S(2)}) %collective-permute-start.1) | collective-permute-done | bytes 393248 | tf_op jit(solution)/shard_map/gather_y/ppermute | solution.py:253
  58.1 5.6 %collective-permute-start.2 = (bf16[1536,128]{1,0:T(8,128)(2,1)S(1)}, bf16[1536,128]{1,0:T(8,128)(2,1)S(1)}, u32[]{:S(2)}, u32[]{:S(2)}) collective-permute-start(bf16[1536,128]{1,0:T(8,128)(2,1)S(1)} %collective-permute-done.1), channel_id=1, source_target_pairs={{0,8},{8,16},{16,24},{24,32},{32,40},{40,48},{48,56},{56,0},{1,9},... | collective-permute-start | bytes 1179656 | tf_op jit(solution)/shard_map/gather_y/ppermute | solution.py:253
  63.7 4.3 %all-to-all-start = ((f32[8,56,128]{2,1,0:T(8,128)}), f32[8,56,128]{2,1,0:T(8,128)S(1)}, u32[]{:S(2)}, u32[]{:S(2)}) async-start(f32[8,56,128]{2,1,0:T(8,128)} %copy-done.1), calls=%async_computation | async-start | bytes 458752 | tf_op jit(solution)/shard_map/small_exchange/all_to_all | solution.py:305
  68.0 0.0 collective-permute-done.4
  68.0 1.9 %collective-permute-start.5 = (bf16[1536,128]{1,0:T(8,128)(2,1)S(1)}, bf16[1536,128]{1,0:T(8,128)(2,1)S(1)}, u32[]{:S(2)}, u32[]{:S(2)}) collective-permute-start(bf16[1536,128]{1,0:T(8,128)(2,1)S(1)} %collective-permute-done.4), channel_id=1, source_target_pairs={{0,56},{8,0},{16,8},{24,16},{32,24},{40,32},{48,40},{56,48},{1,57}... | collective-permute-start | bytes 1179656 | tf_op jit(solution)/shard_map/gather_y/ppermute | solution.py:249
  69.9 0.0 collective-permute-done.2.after_ref
  69.9 5.1 %collective-permute-start.6 = (bf16[1536,128]{1,0:T(8,128)(2,1)S(1)}, bf16[1536,128]{1,0:T(8,128)(2,1)S(1)}, u32[]{:S(2)}, u32[]{:S(2)}) collective-permute-start(bf16[1536,128]{1,0:T(8,128)(2,1)S(1)} %collective-permute-done.2.after_ref), channel_id=1, source_target_pairs={{0,8},{8,16},{16,24},{24,32},{32,40},{40,48},{48,56},{56,0},{1,9},... | collective-permute-start | bytes 1179656 | tf_op jit(solution)/shard_map/gather_y/ppermute | solution.py:253
  75.1 0.0 all-to-all-done.pack_ref
  75.1 0.1 reshape.50.live_ref
  75.2 0.1 reshape.49
  75.3 7.3 %collective-permute-done.5 = bf16[1536,128]{1,0:T(8,128)(2,1)S(1)} collective-permute-done((bf16[1536,128]{1,0:T(8,128)(2,1)S(1)}, bf16[1536,128]{1,0:T(8,128)(2,1)S(1)}, u32[]{:S(2)}, u32[]{:S(2)}) %collective-permute-start.5) | collective-permute-done | bytes 393248 | tf_op jit(solution)/shard_map/gather_y/ppermute | solution.py:249
  82.6 0.0 copy-start.3
  82.6 1.0 copy-done.3
  83.6 2.9 %collect.1 = (bf16[64,128,128]{2,1,0:T(8,128)(2,1)S(1)}, f32[128,128]{1,0:T(8,128)S(1)}) custom-call(s32[64]{0:T(128)S(1)} %get-tuple-element.21.turn_ref, s32[64]{0:T(128)S(1)} %get-tuple-element.20.block_ref, bf16[12,128,128]{2,1,0:T(8,128)(2,1)S(1)} %bitcast.22, bf16[12,128,128]{2,1,0:T(8,128)(2,1)S(1)} %bitcast.24, bf16[12,128,128]{2,1,0:T(8,128)(2,1)S(1)} %bitcast.29, ...), custom_call_target="tpu_custom_call" | custom-call | flops 1000000 | bytes 4000000 | tf_op jit(solution)/shard_map/collect/pallas_call | solution.py:339
  86.5 1.4 %place.1.place_ref = s32[320,128]{1,0:T(8,128)S(1)} custom-call(s32[1]{0:T(128)} %bitcast.core_ref, s32[1]{0:T(128)} %bitcast.1.part_ref, s32[64]{0:T(128)S(1)} %get-tuple-element.19.seen_ref, s32[64]{0:T(128)S(1)} %reshape.50.live_ref, f32[8,56,128]{2,1,0:T(8,128)S(1)} %all-to-all-done.pack_ref), custom_call_target="tpu_custom_call" | custom-call | flops 1000000 | bytes 400000 | tf_op jit(solution)/shard_map/place/pallas_call | solution.py:324
  87.9 0.0 collective-permute-done.6
  87.9 1.8 %select.17 = (bf16[4,512,128]{2,1,0:T(8,128)(2,1)S(1)}, f32[96,128]{1,0:T(8,128)S(1)}) custom-call(s32[64]{0:T(128)S(1)} %get-tuple-element.21.turn_ref, s32[64]{0:T(128)S(1)} %get-tuple-element.20.block_ref, s32[320,128]{1,0:T(8,128)S(1)} %place.1.place_ref, f32[128,128]{1,0:T(8,128)S(1)} %get-tuple-element.13.gram_ref, ...), custom_call_target="tpu_custom_call" | custom-call | flops 350000000 | bytes 2000000 | tf_op jit(solution)/shard_map/select/pallas_call | solution.py:355
  89.7 1.9 %collective-permute-start.7 = (bf16[4,512,128]{2,1,0:T(8,128)(2,1)S(1)}, bf16[4,512,128]{2,1,0:T(8,128)(2,1)S(1)}, u32[]{:S(2)}, u32[]{:S(2)}) collective-permute-start(bf16[4,512,128]{2,1,0:T(8,128)(2,1)S(1)} %get-tuple-element.15), channel_id=1, source_target_pairs={{0,4},{4,0},{1,5},{5,1},{2,6},{6,2},{3,7},{7,3},{8,12},{12,8},{9,1... | collective-permute-start | bytes 1572872 | tf_op jit(solution)/shard_map/select/ppermute | solution.py:363
  91.6 1.7 %select.16.own_ref = bf16[4,320,128]{2,1,0:T(8,128)(2,1)S(1)} custom-call(s32[64]{0:T(128)S(1)} %get-tuple-element.21.turn_ref, s32[64]{0:T(128)S(1)} %get-tuple-element.20.block_ref, s32[320,128]{1,0:T(8,128)S(1)} %place.1.place_ref, bf16[64,128,128]{2,1,0:T(8,128)(2,1)S(1)} %get-tuple-element.12.held_ref, bf16[12,128,128]{2,1,0:T(8,128)(2,1)S(1)} %bitcast.26), custom_call_target="tpu_custom_call" | custom-call | flops 350000000 | bytes 2000000 | tf_op jit(solution)/shard_map/select/pallas_call | solution.py:364
  93.3 0.2 collective-permute-done.7.other_ref
  93.5 0.9 exchange.1
  94.4 4.4 %all-to-all-start.1 = ((bf16[4,512,128]{2,1,0:T(8,128)(2,1)}), bf16[4,512,128]{2,1,0:T(8,128)(2,1)S(1)}, u32[]{:S(2)}, u32[]{:S(2)}) async-start(bf16[4,512,128]{2,1,0:T(8,128)(2,1)} %exchange.1), calls=%async_computation.1 | async-start | bytes 1048576 | tf_op jit(solution)/shard_map/exchange/all_to_all | solution.py:374
  98.8 0.0 copy-done
  98.8 0.1 reshape.59.live_ref
  98.9 1.4 %weights.1.weight_ref = bf16[1280,128]{1,0:T(8,128)(2,1)S(1)} custom-call(s32[1]{0:T(128)} %bitcast.core_ref, s32[32]{0:T(128)S(1)} %reshape.59.live_ref, f32[8,56,128]{2,1,0:T(8,128)S(1)} %all-to-all-done.pack_ref), custom_call_target="tpu_custom_call" | custom-call | flops 1000000 | bytes 400000 | tf_op jit(solution)/shard_map/weights/pallas_call | solution.py:331
  100.3 8.5 %all-to-all-done.1.recv_ref = bf16[4,512,128]{2,1,0:T(8,128)(2,1)S(1)} async-done(((bf16[4,512,128]{2,1,0:T(8,128)(2,1)}), bf16[4,512,128]{2,1,0:T(8,128)(2,1)S(1)}, u32[]{:S(2)}, u32[]{:S(2)}) %all-to-all-start.1) | async-done | bytes 524320 | tf_op jit(solution)/shard_map/exchange/all_to_all | solution.py:374
  108.7 3.2 %solve.1 = bf16[128,128]{1,0:T(8,128)(2,1)S(1)} custom-call(bf16[4,512,128]{2,1,0:T(8,128)(2,1)S(1)} %all-to-all-done.1.recv_ref, bf16[1280,128]{1,0:T(8,128)(2,1)S(1)} %weights.1.weight_ref, f32[128,128]{1,0:T(8,128)S(1)} %constant_dynamic-slice_fusion.start_ref), custom_call_target="tpu_custom_call" | custom-call | flops 800000000 | bytes 1200000 | tf_op jit(solution)/shard_map/solve/pallas_call | solution.py:377
  111.9 8.4 %all_to_all.15 = bf16[4,128,128]{2,1,0:T(8,128)(2,1)S(1)} all-to-all(bf16[4,128,128]{2,1,0:T(8,128)(2,1)S(1)} %broadcast_in_dim.4), channel_id=1, replica_groups=mesh['z'=12,'y'=8,'core'=2,'x'=4] {'x'}, dimensions={0} | all-to-all | bytes 262144 | tf_op jit(solution)/shard_map/gather_x/all_to_all | solution.py:245
  120.3 0.7 bitcast_convert_fusion
  (7 shorter events, 0.1 us)
Async XLA Ops:
  0.0 98.8 %copy-start = (f32[512,128]{1,0:T(8,128)S(1)}, f32[512,128]{1,0:T(8,128)}, u32[]{:S(2)}) copy-start(f32[512,128]{1,0:T(8,128)} %param.13) | copy-start | bytes 786436
  35.2 10.7 %collective-permute-start = (bf16[1536,128]{1,0:T(8,128)(2,1)S(1)}, bf16[1536,128]{1,0:T(8,128)(2,1)S(1)}, u32[]{:S(2)}, u32[]{:S(2)}) collective-permute-start(bf16[1536,128]{1,0:T(8,128)(2,1)S(1)} %bitcast.20), channel_id=1, source_target_pairs={{0,8},{8,16},{16,24},{24,32},{32,40},{40,48},{48,56},{56,0},{1,9},... | collective-permute-start | bytes 1179656 | tf_op jit(solution)/shard_map/gather_y/ppermute | solution.py:253
  39.9 13.5 %collective-permute-start.3 = (bf16[1536,128]{1,0:T(8,128)(2,1)S(1)}, bf16[1536,128]{1,0:T(8,128)(2,1)S(1)}, u32[]{:S(2)}, u32[]{:S(2)}) collective-permute-start(bf16[1536,128]{1,0:T(8,128)(2,1)S(1)} %bitcast.21), channel_id=1, source_target_pairs={{0,56},{8,0},{16,8},{24,16},{32,24},{40,32},{48,40},{56,48},{1,57}... | collective-permute-start | bytes 1179656 | tf_op jit(solution)/shard_map/gather_y/ppermute | solution.py:249
  46.0 12.1 %collective-permute-start.1 = (bf16[1536,128]{1,0:T(8,128)(2,1)S(1)}, bf16[1536,128]{1,0:T(8,128)(2,1)S(1)}, u32[]{:S(2)}, u32[]{:S(2)}) collective-permute-start(bf16[1536,128]{1,0:T(8,128)(2,1)S(1)} %collective-permute-done), channel_id=1, source_target_pairs={{0,8},{8,16},{16,24},{24,32},{32,40},{40,48},{48,56},{56,0},{1,9},... | collective-permute-start | bytes 1179656 | tf_op jit(solution)/shard_map/gather_y/ppermute | solution.py:253
  52.8 0.7 copy-start.1
  53.5 0.8 copy-start.2
  54.2 13.8 %collective-permute-start.4 = (bf16[1536,128]{1,0:T(8,128)(2,1)}, bf16[1536,128]{1,0:T(8,128)(2,1)S(1)}, u32[]{:S(2)}, u32[]{:S(2)}) collective-permute-start(bf16[1536,128]{1,0:T(8,128)(2,1)} %gather_y.1), channel_id=1, source_target_pairs={{0,56},{8,0},{16,8},{24,16},{32,24},{40,32},{48,40},{56,48},{1,57}... | collective-permute-start | bytes 1179656 | tf_op jit(solution)/shard_map/gather_y/ppermute | solution.py:249
  58.1 11.8 %collective-permute-start.2 = (bf16[1536,128]{1,0:T(8,128)(2,1)S(1)}, bf16[1536,128]{1,0:T(8,128)(2,1)S(1)}, u32[]{:S(2)}, u32[]{:S(2)}) collective-permute-start(bf16[1536,128]{1,0:T(8,128)(2,1)S(1)} %collective-permute-done.1), channel_id=1, source_target_pairs={{0,8},{8,16},{16,24},{24,32},{32,40},{40,48},{48,56},{56,0},{1,9},... | collective-permute-start | bytes 1179656 | tf_op jit(solution)/shard_map/gather_y/ppermute | solution.py:253
  63.7 11.4 %all-to-all-start = ((f32[8,56,128]{2,1,0:T(8,128)}), f32[8,56,128]{2,1,0:T(8,128)S(1)}, u32[]{:S(2)}, u32[]{:S(2)}) async-start(f32[8,56,128]{2,1,0:T(8,128)} %copy-done.1), calls=%async_computation | async-start | bytes 458752 | tf_op jit(solution)/shard_map/small_exchange/all_to_all | solution.py:305
  68.0 14.6 %collective-permute-start.5 = (bf16[1536,128]{1,0:T(8,128)(2,1)S(1)}, bf16[1536,128]{1,0:T(8,128)(2,1)S(1)}, u32[]{:S(2)}, u32[]{:S(2)}) collective-permute-start(bf16[1536,128]{1,0:T(8,128)(2,1)S(1)} %collective-permute-done.4), channel_id=1, source_target_pairs={{0,56},{8,0},{16,8},{24,16},{32,24},{40,32},{48,40},{56,48},{1,57}... | collective-permute-start | bytes 1179656 | tf_op jit(solution)/shard_map/gather_y/ppermute | solution.py:249
  69.9 17.9 %collective-permute-start.6 = (bf16[1536,128]{1,0:T(8,128)(2,1)S(1)}, bf16[1536,128]{1,0:T(8,128)(2,1)S(1)}, u32[]{:S(2)}, u32[]{:S(2)}) collective-permute-start(bf16[1536,128]{1,0:T(8,128)(2,1)S(1)} %collective-permute-done.2.after_ref), channel_id=1, source_target_pairs={{0,8},{8,16},{16,24},{24,32},{32,40},{40,48},{48,56},{56,0},{1,9},... | collective-permute-start | bytes 1179656 | tf_op jit(solution)/shard_map/gather_y/ppermute | solution.py:253
  82.6 1.0 copy-start.3
  89.7 3.8 %collective-permute-start.7 = (bf16[4,512,128]{2,1,0:T(8,128)(2,1)S(1)}, bf16[4,512,128]{2,1,0:T(8,128)(2,1)S(1)}, u32[]{:S(2)}, u32[]{:S(2)}) collective-permute-start(bf16[4,512,128]{2,1,0:T(8,128)(2,1)S(1)} %get-tuple-element.15), channel_id=1, source_target_pairs={{0,4},{4,0},{1,5},{5,1},{2,6},{6,2},{3,7},{7,3},{8,12},{12,8},{9,1... | collective-permute-start | bytes 1572872 | tf_op jit(solution)/shard_map/select/ppermute | solution.py:363
  94.4 14.4 %all-to-all-start.1 = ((bf16[4,512,128]{2,1,0:T(8,128)(2,1)}), bf16[4,512,128]{2,1,0:T(8,128)(2,1)S(1)}, u32[]{:S(2)}, u32[]{:S(2)}) async-start(bf16[4,512,128]{2,1,0:T(8,128)(2,1)} %exchange.1), calls=%async_computation.1 | async-start | bytes 1048576 | tf_op jit(solution)/shard_map/exchange/all_to_all | solution.py:374

commit v11 on v10

--- a/solution.py
+++ b/solution.py
@@ -116,7 +116,7 @@
     out_ref[...] = merged
 
 
-def collect_kernel(turn_ref, block_ref, *refs):
+def collect_kernel(turn_ref, block_ref, after_ref, *refs):
     piece_refs, (out_ref, gram_ref, held, sems) = refs[:-4], refs[-4:]
     fetch([(piece_ref, held.at[i]) for i, piece_ref in enumerate(piece_refs)], sems)
     for q in range(C * GROUPS * PAIRS):
@@ -342,13 +342,13 @@
                 jax.ShapeDtypeStruct((C * GROUPS * PAIRS, BLK, E), bf16),
                 jax.ShapeDtypeStruct((E, E), f32),
             ),
-            [smem()] * 2 + [hbm()] * len(pieces),
+            [smem()] * 2 + [hbm()] * (1 + len(pieces)),
             [
                 pltpu.VMEM((Y - 1, Z, BLK, E), bf16),
                 pltpu.SemaphoreType.DMA((Y - 1,)),
             ],
             nbytes=4_000_000,
-        )(turns, spots, *pieces)
+        )(turns, spots, place, *pieces)
     with jax.named_scope("select"):
         shape = jax.ShapeDtypeStruct((GROUPS, LIVE + 2 * GRAM, E), bf16)
         scratch = [pltpu.VMEM((Z, BLK, E), bf16), pltpu.SemaphoreType.DMA((1,))]

time: 122 us -> 120 us (0.984)
  waiting for transfers between devices: 22 us -> 20.6 us
    ppermute x3, waiting for transfers between devices: 7.29 us -> 5.88 us  [from_next(): return lax.ppermute(value, 'y', [(i, (i - 1) % Y) for i in range(Y)])]
where the time goes in v11:
time: 120 us
  blocking collectives  42.7 us (36%)
  starting transfers between devices  37.1 us (31%)
  waiting for transfers between devices  20.6 us (17%)
  Pallas kernels  13.1 us (11%)
  other arithmetic  3.12 us (3%)
  local copies, waits for them, and re-layouts  2.71 us (2%)
    all_gather x1, blocking collectives, local(): column = lax.all_gather(own_block, 'z', axis=0, tiled=True)  34.4 us
    ppermute x4, starting transfers between devices, from_last(): return lax.ppermute(value, 'y', [(i, (i + 1) % Y) for i in range(Y)])  20.7 us
    all_to_all x1, waiting for transfers between devices, local(): received = lax.all_to_all(merged, 'x', 0, 0, tiled=True)  8.48 us
    all_to_all x1, blocking collectives, spread(): lax.all_to_all(jnp.broadcast_to(value[None], (size,) + value.shape), axis...  8.36 us
    ppermute x4, waiting for transfers between devices, from_last(): return lax.ppermute(value, 'y', [(i, (i + 1) % Y) for i in range(Y)])  6.05 us
    ppermute x3, waiting for transfers between devices, from_next(): return lax.ppermute(value, 'y', [(i, (i - 1) % Y) for i in range(Y)])  5.88 us
    ppermute x3, starting transfers between devices, from_next(): return lax.ppermute(value, 'y', [(i, (i - 1) % Y) for i in range(Y)])  5.75 us
    all_to_all x1, starting transfers between devices, local(): received = lax.all_to_all(merged, 'x', 0, 0, tiled=True)  4.44 us
  transfers between devices with their start and end apart: 10, of which 5 were waited for; matrix products, arithmetic and copies ran while one was open for 1% of the time, Pallas kernels for 6%

profile of v11, /device:TPU:24, one launch (start us, length us, event | category | flops | bytes accessed | tf_op | source)
XLA Modules:
  0.0 119.6 jit_solution(1490373864921972629)
XLA Ops:
  0.0 0.0 copy-start
  0.0 0.9 convert_element_type.20
  0.9 34.4 %all-gather = bf16[1,1536,128]{2,1,0:T(8,128)(2,1)S(1)} all-gather(bf16[1,128,128]{2,1,0:T(8,128)(2,1)S(1)} %convert_element_type.20), channel_id=2, replica_groups=mesh['z'=12,'y'=8,'core'=2,'x'=4] {'z'}, dimensions={1}, use_global_device_ids=true | all-gather | bytes 425984 | tf_op jit(solution)/shard_map/gather_z/all_gather | solution.py:287
  35.2 4.7 %collective-permute-start = (bf16[1536,128]{1,0:T(8,128)(2,1)S(1)}, bf16[1536,128]{1,0:T(8,128)(2,1)S(1)}, u32[]{:S(2)}, u32[]{:S(2)}) collective-permute-start(bf16[1536,128]{1,0:T(8,128)(2,1)S(1)} %bitcast.23), channel_id=1, source_target_pairs={{0,8},{8,16},{16,24},{24,32},{32,40},{40,48},{48,56},{56,0},{1,9},... | collective-permute-start | bytes 1179656 | tf_op jit(solution)/shard_map/gather_y/ppermute | solution.py:253
  39.9 1.9 %collective-permute-start.3 = (bf16[1536,128]{1,0:T(8,128)(2,1)S(1)}, bf16[1536,128]{1,0:T(8,128)(2,1)S(1)}, u32[]{:S(2)}, u32[]{:S(2)}) collective-permute-start(bf16[1536,128]{1,0:T(8,128)(2,1)S(1)} %bitcast.24), channel_id=1, source_target_pairs={{0,56},{8,0},{16,8},{24,16},{32,24},{40,32},{48,40},{56,48},{1,57}... | collective-permute-start | bytes 1179656 | tf_op jit(solution)/shard_map/gather_y/ppermute | solution.py:249
  41.9 4.1 %collective-permute-done = bf16[1536,128]{1,0:T(8,128)(2,1)S(1)} collective-permute-done((bf16[1536,128]{1,0:T(8,128)(2,1)S(1)}, bf16[1536,128]{1,0:T(8,128)(2,1)S(1)}, u32[]{:S(2)}, u32[]{:S(2)}) %collective-permute-start) | collective-permute-done | bytes 393248 | tf_op jit(solution)/shard_map/gather_y/ppermute | solution.py:253
  46.0 5.3 %collective-permute-start.1 = (bf16[1536,128]{1,0:T(8,128)(2,1)S(1)}, bf16[1536,128]{1,0:T(8,128)(2,1)S(1)}, u32[]{:S(2)}, u32[]{:S(2)}) collective-permute-start(bf16[1536,128]{1,0:T(8,128)(2,1)S(1)} %collective-permute-done), channel_id=1, source_target_pairs={{0,8},{8,16},{16,24},{24,32},{32,40},{40,48},{48,56},{56,0},{1,9},... | collective-permute-start | bytes 1179656 | tf_op jit(solution)/shard_map/gather_y/ppermute | solution.py:253
  51.3 0.7 add_convert_fusion.1.blocks_ref
  52.0 0.8 add_convert_fusion.slots_ref
  52.8 0.0 copy-start.1
  52.8 0.7 copy-done.1
  53.5 0.0 collective-permute-done.3.value_ref
  53.5 0.0 copy-start.2
  53.5 0.8 copy-done.2
  54.2 1.9 %collective-permute-start.4 = (bf16[1536,128]{1,0:T(8,128)(2,1)}, bf16[1536,128]{1,0:T(8,128)(2,1)S(1)}, u32[]{:S(2)}, u32[]{:S(2)}) collective-permute-start(bf16[1536,128]{1,0:T(8,128)(2,1)} %gather_y.1), channel_id=1, source_target_pairs={{0,56},{8,0},{16,8},{24,16},{32,24},{40,32},{48,40},{56,48},{1,57}... | collective-permute-start | bytes 1179656 | tf_op jit(solution)/shard_map/gather_y/ppermute | solution.py:249
  56.1 1.9 %collective-permute-done.1 = bf16[1536,128]{1,0:T(8,128)(2,1)S(1)} collective-permute-done((bf16[1536,128]{1,0:T(8,128)(2,1)S(1)}, bf16[1536,128]{1,0:T(8,128)(2,1)S(1)}, u32[]{:S(2)}, u32[]{:S(2)}) %collective-permute-start.1) | collective-permute-done | bytes 393248 | tf_op jit(solution)/shard_map/gather_y/ppermute | solution.py:253
  58.1 5.6 %collective-permute-start.2 = (bf16[1536,128]{1,0:T(8,128)(2,1)S(1)}, bf16[1536,128]{1,0:T(8,128)(2,1)S(1)}, u32[]{:S(2)}, u32[]{:S(2)}) collective-permute-start(bf16[1536,128]{1,0:T(8,128)(2,1)S(1)} %collective-permute-done.1), channel_id=1, source_target_pairs={{0,8},{8,16},{16,24},{24,32},{32,40},{40,48},{48,56},{56,0},{1,9},... | collective-permute-start | bytes 1179656 | tf_op jit(solution)/shard_map/gather_y/ppermute | solution.py:253
  63.7 4.3 %all-to-all-start = ((f32[8,56,128]{2,1,0:T(8,128)}), f32[8,56,128]{2,1,0:T(8,128)S(1)}, u32[]{:S(2)}, u32[]{:S(2)}) async-start(f32[8,56,128]{2,1,0:T(8,128)} %copy-done.1), calls=%async_computation | async-start | bytes 458752 | tf_op jit(solution)/shard_map/small_exchange/all_to_all | solution.py:305
  68.0 0.0 collective-permute-done.4
  68.0 1.9 %collective-permute-start.5 = (bf16[1536,128]{1,0:T(8,128)(2,1)S(1)}, bf16[1536,128]{1,0:T(8,128)(2,1)S(1)}, u32[]{:S(2)}, u32[]{:S(2)}) collective-permute-start(bf16[1536,128]{1,0:T(8,128)(2,1)S(1)} %collective-permute-done.4), channel_id=1, source_target_pairs={{0,56},{8,0},{16,8},{24,16},{32,24},{40,32},{48,40},{56,48},{1,57}... | collective-permute-start | bytes 1179656 | tf_op jit(solution)/shard_map/gather_y/ppermute | solution.py:249
  69.9 0.0 collective-permute-done.2.after_ref
  69.9 5.1 %collective-permute-start.6 = (bf16[1536,128]{1,0:T(8,128)(2,1)S(1)}, bf16[1536,128]{1,0:T(8,128)(2,1)S(1)}, u32[]{:S(2)}, u32[]{:S(2)}) collective-permute-start(bf16[1536,128]{1,0:T(8,128)(2,1)S(1)} %collective-permute-done.2.after_ref), channel_id=1, source_target_pairs={{0,8},{8,16},{16,24},{24,32},{32,40},{40,48},{48,56},{56,0},{1,9},... | collective-permute-start | bytes 1179656 | tf_op jit(solution)/shard_map/gather_y/ppermute | solution.py:253
  75.1 0.0 all-to-all-done.pack_ref
  75.1 0.1 reshape.50.live_ref
  75.2 0.1 reshape.49
  75.3 1.4 %place.1.after_ref.place_ref = s32[320,128]{1,0:T(8,128)S(1)} custom-call(s32[1]{0:T(128)} %bitcast.core_ref, s32[1]{0:T(128)} %bitcast.1.part_ref, s32[64]{0:T(128)S(1)} %get-tuple-element.19.seen_ref, s32[64]{0:T(128)S(1)} %reshape.50.live_ref, f32[8,56,128]{2,1,0:T(8,128)S(1)} %all-to-all-done.pack_ref), custom_call_target="tpu_custom_call" | custom-call | flops 1000000 | bytes 400000 | tf_op jit(solution)/shard_map/place/pallas_call | solution.py:324
  76.7 5.9 %collective-permute-done.5 = bf16[1536,128]{1,0:T(8,128)(2,1)S(1)} collective-permute-done((bf16[1536,128]{1,0:T(8,128)(2,1)S(1)}, bf16[1536,128]{1,0:T(8,128)(2,1)S(1)}, u32[]{:S(2)}, u32[]{:S(2)}) %collective-permute-start.5) | collective-permute-done | bytes 393248 | tf_op jit(solution)/shard_map/gather_y/ppermute | solution.py:249
  82.6 0.0 copy-start.3
  82.6 1.0 copy-done.3
  83.6 2.9 %collect.1 = (bf16[64,128,128]{2,1,0:T(8,128)(2,1)S(1)}, f32[128,128]{1,0:T(8,128)S(1)}) custom-call(s32[64]{0:T(128)S(1)} %get-tuple-element.21.turn_ref, s32[64]{0:T(128)S(1)} %get-tuple-element.20.block_ref, s32[320,128]{1,0:T(8,128)S(1)} %place.1.after_ref.place_ref, bf16[12,128,128]{2,1,0:T(8,128)(2,1)S(1)} %bitcast.25, ...), custom_call_target="tpu_custom_call" | custom-call | flops 1000000 | bytes 4000000 | tf_op jit(solution)/shard_map/collect/pallas_call | solution.py:339
  86.5 0.0 collective-permute-done.6
  86.5 1.8 %select.17 = (bf16[4,512,128]{2,1,0:T(8,128)(2,1)S(1)}, f32[96,128]{1,0:T(8,128)S(1)}) custom-call(s32[64]{0:T(128)S(1)} %get-tuple-element.21.turn_ref, s32[64]{0:T(128)S(1)} %get-tuple-element.20.block_ref, s32[320,128]{1,0:T(8,128)S(1)} %place.1.after_ref.place_ref, f32[128,128]{1,0:T(8,128)S(1)} %get-tuple-element.13.gram_ref, ...), custom_call_target="tpu_custom_call" | custom-call | flops 350000000 | bytes 2000000 | tf_op jit(solution)/shard_map/select/pallas_call | solution.py:355
  88.3 1.9 %collective-permute-start.7 = (bf16[4,512,128]{2,1,0:T(8,128)(2,1)S(1)}, bf16[4,512,128]{2,1,0:T(8,128)(2,1)S(1)}, u32[]{:S(2)}, u32[]{:S(2)}) collective-permute-start(bf16[4,512,128]{2,1,0:T(8,128)(2,1)S(1)} %get-tuple-element.15), channel_id=1, source_target_pairs={{0,4},{4,0},{1,5},{5,1},{2,6},{6,2},{3,7},{7,3},{8,12},{12,8},{9,1... | collective-permute-start | bytes 1572872 | tf_op jit(solution)/shard_map/select/ppermute | solution.py:363
  90.2 1.7 %select.16.own_ref = bf16[4,320,128]{2,1,0:T(8,128)(2,1)S(1)} custom-call(s32[64]{0:T(128)S(1)} %get-tuple-element.21.turn_ref, s32[64]{0:T(128)S(1)} %get-tuple-element.20.block_ref, s32[320,128]{1,0:T(8,128)S(1)} %place.1.after_ref.place_ref, bf16[64,128,128]{2,1,0:T(8,128)(2,1)S(1)} %get-tuple-element.12.held_ref, bf16[12,128,128]{2,1,0:T(8,128)(2,1)S(1)} %bitcast.21), custom_call_target="tpu_custom_call" | custom-call | flops 350000000 | bytes 2000000 | tf_op jit(solution)/shard_map/select/pallas_call | solution.py:364
  91.9 0.2 collective-permute-done.7.other_ref
  92.1 0.9 exchange.1
  93.0 4.4 %all-to-all-start.1 = ((bf16[4,512,128]{2,1,0:T(8,128)(2,1)}), bf16[4,512,128]{2,1,0:T(8,128)(2,1)S(1)}, u32[]{:S(2)}, u32[]{:S(2)}) async-start(bf16[4,512,128]{2,1,0:T(8,128)(2,1)} %exchange.1), calls=%async_computation.1 | async-start | bytes 1048576 | tf_op jit(solution)/shard_map/exchange/all_to_all | solution.py:374
  97.4 0.0 copy-done
  97.4 0.1 reshape.59.live_ref
  97.5 1.4 %weights.1.weight_ref = bf16[1280,128]{1,0:T(8,128)(2,1)S(1)} custom-call(s32[1]{0:T(128)} %bitcast.core_ref, s32[32]{0:T(128)S(1)} %reshape.59.live_ref, f32[8,56,128]{2,1,0:T(8,128)S(1)} %all-to-all-done.pack_ref), custom_call_target="tpu_custom_call" | custom-call | flops 1000000 | bytes 400000 | tf_op jit(solution)/shard_map/weights/pallas_call | solution.py:331
  98.9 8.5 %all-to-all-done.1.recv_ref = bf16[4,512,128]{2,1,0:T(8,128)(2,1)S(1)} async-done(((bf16[4,512,128]{2,1,0:T(8,128)(2,1)}), bf16[4,512,128]{2,1,0:T(8,128)(2,1)S(1)}, u32[]{:S(2)}, u32[]{:S(2)}) %all-to-all-start.1) | async-done | bytes 524320 | tf_op jit(solution)/shard_map/exchange/all_to_all | solution.py:374
  107.3 3.2 %solve.1 = bf16[128,128]{1,0:T(8,128)(2,1)S(1)} custom-call(bf16[4,512,128]{2,1,0:T(8,128)(2,1)S(1)} %all-to-all-done.1.recv_ref, bf16[1280,128]{1,0:T(8,128)(2,1)S(1)} %weights.1.weight_ref, f32[128,128]{1,0:T(8,128)S(1)} %constant_dynamic-slice_fusion.start_ref), custom_call_target="tpu_custom_call" | custom-call | flops 800000000 | bytes 1200000 | tf_op jit(solution)/shard_map/solve/pallas_call | solution.py:377
  110.5 8.4 %all_to_all.15 = bf16[4,128,128]{2,1,0:T(8,128)(2,1)S(1)} all-to-all(bf16[4,128,128]{2,1,0:T(8,128)(2,1)S(1)} %broadcast_in_dim.4), channel_id=1, replica_groups=mesh['z'=12,'y'=8,'core'=2,'x'=4] {'x'}, dimensions={0} | all-to-all | bytes 262144 | tf_op jit(solution)/shard_map/gather_x/all_to_all | solution.py:245
  118.9 0.7 bitcast_convert_fusion
  (7 shorter events, 0.1 us)
Async XLA Ops:
  0.0 97.4 %copy-start = (f32[512,128]{1,0:T(8,128)S(1)}, f32[512,128]{1,0:T(8,128)}, u32[]{:S(2)}) copy-start(f32[512,128]{1,0:T(8,128)} %param.13) | copy-start | bytes 786436
  35.2 10.7 %collective-permute-start = (bf16[1536,128]{1,0:T(8,128)(2,1)S(1)}, bf16[1536,128]{1,0:T(8,128)(2,1)S(1)}, u32[]{:S(2)}, u32[]{:S(2)}) collective-permute-start(bf16[1536,128]{1,0:T(8,128)(2,1)S(1)} %bitcast.23), channel_id=1, source_target_pairs={{0,8},{8,16},{16,24},{24,32},{32,40},{40,48},{48,56},{56,0},{1,9},... | collective-permute-start | bytes 1179656 | tf_op jit(solution)/shard_map/gather_y/ppermute | solution.py:253
  39.9 13.5 %collective-permute-start.3 = (bf16[1536,128]{1,0:T(8,128)(2,1)S(1)}, bf16[1536,128]{1,0:T(8,128)(2,1)S(1)}, u32[]{:S(2)}, u32[]{:S(2)}) collective-permute-start(bf16[1536,128]{1,0:T(8,128)(2,1)S(1)} %bitcast.24), channel_id=1, source_target_pairs={{0,56},{8,0},{16,8},{24,16},{32,24},{40,32},{48,40},{56,48},{1,57}... | collective-permute-start | bytes 1179656 | tf_op jit(solution)/shard_map/gather_y/ppermute | solution.py:249
  46.0 12.1 %collective-permute-start.1 = (bf16[1536,128]{1,0:T(8,128)(2,1)S(1)}, bf16[1536,128]{1,0:T(8,128)(2,1)S(1)}, u32[]{:S(2)}, u32[]{:S(2)}) collective-permute-start(bf16[1536,128]{1,0:T(8,128)(2,1)S(1)} %collective-permute-done), channel_id=1, source_target_pairs={{0,8},{8,16},{16,24},{24,32},{32,40},{40,48},{48,56},{56,0},{1,9},... | collective-permute-start | bytes 1179656 | tf_op jit(solution)/shard_map/gather_y/ppermute | solution.py:253
  52.8 0.7 copy-start.1
  53.5 0.8 copy-start.2
  54.2 13.8 %collective-permute-start.4 = (bf16[1536,128]{1,0:T(8,128)(2,1)}, bf16[1536,128]{1,0:T(8,128)(2,1)S(1)}, u32[]{:S(2)}, u32[]{:S(2)}) collective-permute-start(bf16[1536,128]{1,0:T(8,128)(2,1)} %gather_y.1), channel_id=1, source_target_pairs={{0,56},{8,0},{16,8},{24,16},{32,24},{40,32},{48,40},{56,48},{1,57}... | collective-permute-start | bytes 1179656 | tf_op jit(solution)/shard_map/gather_y/ppermute | solution.py:249
  58.1 11.8 %collective-permute-start.2 = (bf16[1536,128]{1,0:T(8,128)(2,1)S(1)}, bf16[1536,128]{1,0:T(8,128)(2,1)S(1)}, u32[]{:S(2)}, u32[]{:S(2)}) collective-permute-start(bf16[1536,128]{1,0:T(8,128)(2,1)S(1)} %collective-permute-done.1), channel_id=1, source_target_pairs={{0,8},{8,16},{16,24},{24,32},{32,40},{40,48},{48,56},{56,0},{1,9},... | collective-permute-start | bytes 1179656 | tf_op jit(solution)/shard_map/gather_y/ppermute | solution.py:253
  63.7 11.4 %all-to-all-start = ((f32[8,56,128]{2,1,0:T(8,128)}), f32[8,56,128]{2,1,0:T(8,128)S(1)}, u32[]{:S(2)}, u32[]{:S(2)}) async-start(f32[8,56,128]{2,1,0:T(8,128)} %copy-done.1), calls=%async_computation | async-start | bytes 458752 | tf_op jit(solution)/shard_map/small_exchange/all_to_all | solution.py:305
  68.0 14.6 %collective-permute-start.5 = (bf16[1536,128]{1,0:T(8,128)(2,1)S(1)}, bf16[1536,128]{1,0:T(8,128)(2,1)S(1)}, u32[]{:S(2)}, u32[]{:S(2)}) collective-permute-start(bf16[1536,128]{1,0:T(8,128)(2,1)S(1)} %collective-permute-done.4), channel_id=1, source_target_pairs={{0,56},{8,0},{16,8},{24,16},{32,24},{40,32},{48,40},{56,48},{1,57}... | collective-permute-start | bytes 1179656 | tf_op jit(solution)/shard_map/gather_y/ppermute | solution.py:249
  69.9 16.5 %collective-permute-start.6 = (bf16[1536,128]{1,0:T(8,128)(2,1)S(1)}, bf16[1536,128]{1,0:T(8,128)(2,1)S(1)}, u32[]{:S(2)}, u32[]{:S(2)}) collective-permute-start(bf16[1536,128]{1,0:T(8,128)(2,1)S(1)} %collective-permute-done.2.after_ref), channel_id=1, source_target_pairs={{0,8},{8,16},{16,24},{24,32},{32,40},{40,48},{48,56},{56,0},{1,9},... | collective-permute-start | bytes 1179656 | tf_op jit(solution)/shard_map/gather_y/ppermute | solution.py:253
  82.6 1.0 copy-start.3
  88.3 3.8 %collective-permute-start.7 = (bf16[4,512,128]{2,1,0:T(8,128)(2,1)S(1)}, bf16[4,512,128]{2,1,0:T(8,128)(2,1)S(1)}, u32[]{:S(2)}, u32[]{:S(2)}) collective-permute-start(bf16[4,512,128]{2,1,0:T(8,128)(2,1)S(1)} %get-tuple-element.15), channel_id=1, source_target_pairs={{0,4},{4,0},{1,5},{5,1},{2,6},{6,2},{3,7},{7,3},{8,12},{12,8},{9,1... | collective-permute-start | bytes 1572872 | tf_op jit(solution)/shard_map/select/ppermute | solution.py:363
  93.0 14.4 %all-to-all-start.1 = ((bf16[4,512,128]{2,1,0:T(8,128)(2,1)}), bf16[4,512,128]{2,1,0:T(8,128)(2,1)S(1)}, u32[]{:S(2)}, u32[]{:S(2)}) async-start(bf16[4,512,128]{2,1,0:T(8,128)(2,1)} %exchange.1), calls=%async_computation.1 | async-start | bytes 1048576 | tf_op jit(solution)/shard_map/exchange/all_to_all | solution.py:374
